TPU v7x, 256 devices: a whole 4x4x8 slice. The times are simulated.
256 devices in a mesh: oi: 4 (over x), oj: 8 (over z_hi, core), vert: 8 (over z_lo, y).
Axes of the slice: x: 4, y: 4, z: 8 (z_hi: 4, z_lo: 2; z = z_hi * 2 + z_lo), core: 2. Of those that a mesh axis runs over, the one named last changes fastest.
Arguments:
- amplitudes: bfloat16 [32, 32, 8, 128, 128], P('oi', 'oj'), may hold values from -6 to 6
- chol: bfloat16 [64, 256, 4, 128], P(('oj', 'vert')), may hold values from -0.078125 to 0.078125
- occ_irrep: int32 [32], replicated, may hold values from 0 to 7
Outputs:
- residual: float32 [32, 32, 8, 4, 4], P('oi', 'oj', 'vert')
Inputs may be any that keep to these rules, and one draw needn't show every extreme that they name: `occ_irrep`: D2h irrep labels, multiplied by bitwise exclusive or.
All inputs are finite; a program needn't handle non-finite values.
Results may differ from a plain program's by a relative error of at most 0.0028.
Values may be sent and summed in bfloat16 or wider, within the bound.
No kernel may reach another device: no remote copies, remote signals or barrier semaphores. Data moves between devices by JAX's collectives and lax.ppermute only.
A program may use at most 192 MiB of HBM per device.

v0:
```python
import jax
import jax.numpy as jnp
from jax import lax
from jax.sharding import PartitionSpec as P

IRREPS = 8
WB = 4


def ladder_terms(totals, piece, start, amplitudes, pair_irrep, own_irreps, vert_first, local_count):
    groups = piece.reshape(
        piece.shape[0] // IRREPS, IRREPS, piece.shape[1], piece.shape[2], piece.shape[3]
    )
    first_aux = start // IRREPS
    partner_irreps = jnp.bitwise_xor(own_irreps[None, None, :], pair_irrep[:, :, None])
    selector = (
        partner_irreps[:, :, :, None] == jnp.arange(IRREPS, dtype=jnp.int32)[None, None, None, :]
    )
    for offset in range(groups.shape[0]):
        aux_irrep = first_aux + offset
        blocks = groups[offset]
        own_blocks = lax.dynamic_slice_in_dim(blocks, vert_first, local_count, 0)
        amp_blocks = jnp.take(amplitudes, jnp.bitwise_xor(own_irreps, aux_irrep), axis=2)
        half_step = jnp.einsum(
            "lpac,ijlcd->ijlpad", own_blocks, amp_blocks, preferred_element_type=jnp.float32
        ).astype(jnp.bfloat16)
        every_block = jnp.einsum(
            "ijlpad,gpbd->ijlgab", half_step, blocks, preferred_element_type=jnp.float32
        )
        picked = jnp.where(selector[:, :, :, :, None, None], every_block, jnp.float32(0.0))
        totals = totals + jnp.sum(picked, axis=3)
    return totals


def local(amplitudes, chol, occ_irrep):
    occ_rows = amplitudes.shape[0]
    occ_cols = amplitudes.shape[1]
    local_count = IRREPS // lax.axis_size("vert")
    vert_first = lax.axis_index("vert") * local_count
    own_irreps = vert_first + jnp.arange(local_count, dtype=jnp.int32)
    irrep_rows = lax.dynamic_slice_in_dim(occ_irrep, lax.axis_index("oi") * occ_rows, occ_rows)
    irrep_cols = lax.dynamic_slice_in_dim(occ_irrep, lax.axis_index("oj") * occ_cols, occ_cols)
    pair_irrep = jnp.bitwise_xor(irrep_rows[:, None], irrep_cols[None, :])
    zeros_start = jnp.zeros((occ_rows, occ_cols, local_count, WB, WB), jnp.float32)
    window = lax.all_gather(chol, ("oj", "vert"), axis=0, tiled=True)
    ladder = ladder_terms(
        zeros_start, window, 0, amplitudes, pair_irrep, own_irreps, vert_first, local_count
    )
    all_irreps = lax.all_gather(ladder, "vert", axis=2, tiled=True)
    stacked = lax.all_gather(all_irreps, "oi", axis=0, tiled=True)
    traded = lax.all_to_all(stacked, "oj", split_axis=0, concat_axis=1, tiled=True)
    mirrored = lax.dynamic_slice_in_dim(traded, lax.axis_index("oi") * occ_rows, occ_rows, 1)
    turned = jnp.transpose(mirrored, (1, 0, 2, 4, 3))
    picks = jnp.bitwise_xor(own_irreps[None, None, :], pair_irrep[:, :, None])
    partner = jnp.take_along_axis(turned, picks[:, :, :, None, None], axis=2)
    return ladder + partner


def solution(mesh):
    return jax.shard_map(
        local,
        mesh=mesh,
        in_specs=(P("oi", "oj", None, None, None), P(("oj", "vert"), None, None, None), P()),
        out_specs=P("oi", "oj", "vert", None, None),
        check_vma=False,
    )
```

profile of v0, /device:TPU:4, one launch (start us, length us, event | category | flops | bytes accessed | tf_op | source)
XLA Modules:
  0.0 575.5 jit_solution(17051624750905093428)
XLA Ops:
  6.5 1.7 copy.129
  8.3 7.6 %constant_dynamic-slice_fusion.6 = (bf16[8,4,1,128,128]{4,3,2,1,0:T(8,128)(2,1)S(1)}, bf16[8,4,1,128,128]{4,3,2,1,0:T(8,128)(2,1)}, bf16[8,4,1,128,128]{4,3,2,1,...) fusion(bf16[8,4,8,128,128]{4,3,2,1,0:T(8,128)(2,1)} %param.5, ...), kind=kLoop, calls=%fused_computation.110 | loop fusion | bytes 16777248 | tf_op jit(solution)/shard_map/jit(_take) | solution.py:23
  15.9 2.3 copy.245
  18.4 2.3 copy.243
  20.7 2.3 copy.241
  22.9 2.3 copy.239
  25.2 2.3 copy.237
  31.7 184.9 %all-gather.3.cloned.1.call-done = bf16[64,256,4,128]{3,1,2,0:T(8,128)(2,1)} async-done(((bf16[1,256,4,128]{3,1,2,0:T(8,128)(2,1)}), bf16[64,256,4,128]{3,1,2,0:T(8,128)(2,1)}) %all-gather.3.cloned.1.call-update) | async-done | bytes 16777232 | tf_op jit(solution)/shard_map/all_gather | solution.py:45
  216.5 11.4 %fusion.198 = (bf16[8,256,4,128]{3,1,2,0:T(8,128)(2,1)S(1)}, bf16[8,256,4,128]{3,1,2,0:T(8,128)(2,1)}, bf16[8,256,4,128]{3,1,2,0:T(8,128)(2,1)}, bf16[8,256,4,12...) fusion(bf16[64,256,4,128]{3,1,2,0:T(8,128)(2,1)} %all-gather.3., ...), kind=kLoop, calls=%fused_computation.139 | loop fusion | bytes 33554432 | tf_op jit(solution)/shard_map/slice | solution.py:21
  228.0 4.5 copy.246
  232.5 4.5 copy.244
  237.0 4.3 constant_dynamic-slice_fusion.9
  241.2 1.9 copy.159
  243.1 1.4 copy.155
  244.5 3.8 convert_bitcast_fusion
  248.3 22.5 %fusion.139 = f32[8,4,4,4]{0,3,2,1:T(4,128)S(1)} fusion(bf16[8,256,4,128]{1,0,3,2:T(8,128)(2,1)S(1)} %copy-done.5, bf16[8,4,256,4,128,1]{2,4,3,1,0,5:T(8,128)(2,1)S(1)} %convert_bitcast_fusion, pred[8,4,8]{0,2,1:T(8,128)(4,1)S(1)} %iota_compare_fusion), kind=kOutput, calls=%fused_computation.56 | convolution fusion | flops 268443136 | bytes 10488064 | tf_op jit(solution)/shard_map/ijlpad,gpbd->ijlgab/dot_general | solution.py:27
  270.8 2.4 convert_bitcast_fusion.1
  273.2 22.7 %fusion.134 = f32[8,4,4,4]{0,3,2,1:T(4,128)S(1)} fusion(bf16[8,256,4,128]{1,0,3,2:T(8,128)(2,1)S(1)} %copy-done.2, bf16[8,4,256,4,128,1]{2,4,3,1,0,5:T(8,128)(2,1)S(1)} %convert_bitcast_fusion.1, pred[8,4,8]{0,2,1:T(8,128)(4,1)S(1)} %iota_compare_fusion), kind=kOutput, calls=%fused_computation.55 | convolution fusion | flops 268443136 | bytes 10488064 | tf_op jit(solution)/shard_map/ijlpad,gpbd->ijlgab/dot_general | solution.py:27
  295.9 4.5 copy.242
  300.4 4.5 copy.240
  304.9 4.3 constant_dynamic-slice_fusion.11
  309.2 1.4 copy.151
  310.6 3.7 convert_bitcast_fusion.2
  314.4 22.5 %fusion.129 = f32[8,4,4,4]{0,3,2,1:T(4,128)S(1)} fusion(bf16[8,256,4,128]{1,0,3,2:T(8,128)(2,1)S(1)} %copy-done.7, bf16[8,4,256,4,128,1]{2,4,3,1,0,5:T(8,128)(2,1)S(1)} %convert_bitcast_fusion.2, pred[8,4,8]{0,2,1:T(8,128)(4,1)S(1)} %iota_compare_fusion), kind=kOutput, calls=%fused_computation.54 | convolution fusion | flops 268443136 | bytes 10488064 | tf_op jit(solution)/shard_map/ijlpad,gpbd->ijlgab/dot_general | solution.py:27
  338.1 3.7 convert_bitcast_fusion.3
  341.9 22.7 %fusion.124 = f32[8,4,4,4]{0,3,2,1:T(4,128)S(1)} fusion(bf16[8,256,4,128]{1,0,3,2:T(8,128)(2,1)S(1)} %copy-done.3, bf16[8,4,256,4,128,1]{2,4,3,1,0,5:T(8,128)(2,1)S(1)} %convert_bitcast_fusion.3, pred[8,4,8]{0,2,1:T(8,128)(4,1)S(1)} %iota_compare_fusion), kind=kOutput, calls=%fused_computation.53 | convolution fusion | flops 268443136 | bytes 10488064 | tf_op jit(solution)/shard_map/ijlpad,gpbd->ijlgab/dot_general | solution.py:27
  364.5 4.5 copy.238
  369.0 4.5 copy.236
  373.5 4.3 constant_dynamic-slice_fusion.13
  377.8 1.4 copy.143
  379.2 3.7 convert_bitcast_fusion.4
  383.0 23.1 %fusion.119 = f32[8,4,4,4]{0,3,2,1:T(4,128)} fusion(bf16[8,256,4,128]{1,0,3,2:T(8,128)(2,1)S(1)} %copy-done.8, bf16[8,4,256,4,128,1]{2,4,3,1,0,5:T(8,128)(2,1)S(1)} %convert_bitcast_fusion.4, pred[8,4,8]{0,2,1:T(8,128)(4,1)S(1)} %iota_compare_fusion), kind=kOutput, calls=%fused_computation.52 | convolution fusion | flops 268443136 | bytes 10488064 | tf_op jit(solution)/shard_map/ijlpad,gpbd->ijlgab/dot_general | solution.py:27
  407.4 3.7 convert_bitcast_fusion.5
  411.1 23.3 %fusion.114 = f32[8,4,4,4]{0,3,2,1:T(4,128)} fusion(bf16[8,256,4,128]{1,0,3,2:T(8,128)(2,1)S(1)} %copy-done.4, bf16[8,4,256,4,128,1]{2,4,3,1,0,5:T(8,128)(2,1)S(1)} %convert_bitcast_fusion.5, pred[8,4,8]{0,2,1:T(8,128)(4,1)S(1)} %iota_compare_fusion), kind=kOutput, calls=%fused_computation.51 | convolution fusion | flops 268443136 | bytes 10488064 | tf_op jit(solution)/shard_map/ijlpad,gpbd->ijlgab/dot_general | solution.py:27
  434.4 4.5 copy.232
  438.9 2.9 copy.234
  441.8 4.4 constant_dynamic-slice_fusion.15
  446.2 1.4 copy.131
  447.7 3.6 convert_bitcast_fusion.7
  451.3 23.3 %fusion.104 = f32[8,4,4,4]{0,3,2,1:T(4,128)} fusion(bf16[8,256,4,128]{1,0,3,2:T(8,128)(2,1)S(1)} %copy-done.6, bf16[8,4,256,4,128,1]{2,4,3,1,0,5:T(8,128)(2,1)S(1)} %convert_bitcast_fusion.7, pred[8,4,8]{0,2,1:T(8,128)(4,1)S(1)} %iota_compare_fusion), kind=kOutput, calls=%fused_computation.49 | convolution fusion | flops 268443136 | bytes 10488064 | tf_op jit(solution)/shard_map/ijlpad,gpbd->ijlgab/dot_general | solution.py:27
  474.6 1.4 copy.135
  476.0 2.3 convert_bitcast_fusion.6
  478.4 22.5 %fusion.109 = f32[8,4,4,4]{0,3,2,1:T(4,128)S(1)} fusion(bf16[8,256,4,128]{1,0,3,2:T(8,128)(2,1)S(1)} %copy-done.1, bf16[8,4,256,4,128,1]{2,4,3,1,0,5:T(8,128)(2,1)S(1)} %convert_bitcast_fusion.6, pred[8,4,8]{0,2,1:T(8,128)(4,1)S(1)} %iota_compare_fusion), kind=kOutput, calls=%fused_computation.50 | convolution fusion | flops 268443136 | bytes 10488064 | tf_op jit(solution)/shard_map/ijlpad,gpbd->ijlgab/dot_general | solution.py:27
  500.9 28.4 %all-gather = f32[8,4,32,4]{0,3,1,2:T(4,128)S(1)} all-gather(f32[8,4,4,4]{0,3,1,2:T(4,128)S(1)} %copy.161), channel_id=2, replica_groups=mesh['oi'=4,'oj'=8,'vert'=8] {'vert'}, dimensions={2}, use_global_device_ids=true | all-gather | bytes 18432 | tf_op jit(solution)/shard_map/all_gather | solution.py:49
  529.7 12.6 %all_gather.11 = f32[32,4,8,4,4]{2,4,3,1,0:T(4,128)S(1)} all-gather(f32[8,4,8,4,4]{2,4,3,1,0:T(4,128)S(1)} %copy.163), channel_id=1, replica_groups=mesh['oi'=4,'oj'=8,'vert'=8] {'oi'}, dimensions={0}, use_global_device_ids=true | all-gather | bytes 81920 | tf_op jit(solution)/shard_map/all_gather | solution.py:50
  542.3 1.8 reshape.659
  544.1 9.9 %all-to-all-start = ((f32[8,1,2048]{2,1,0:T(1,128)}), f32[8,1,2048]{2,1,0:T(1,128)S(1)}, u32[]{:S(2)}, u32[]{:S(2)}) async-start(f32[8,1,2048]{2,1,0:T(1,128)} %reshape.659), calls=%async_computation | async-start | bytes 131072 | tf_op jit(solution)/shard_map/all_to_all | solution.py:51
  554.1 8.1 %all-to-all-done = f32[8,1,2048]{2,1,0:T(1,128)S(1)} async-done(((f32[8,1,2048]{2,1,0:T(1,128)}), f32[8,1,2048]{2,1,0:T(1,128)S(1)}, u32[]{:S(2)}, u32[]{:S(2)}) %all-to-all-start) | async-done | bytes 65568 | tf_op jit(solution)/shard_map/all_to_all | solution.py:51
  (68 shorter events, 13.6 us)
Async XLA Ops:
  6.5 210.0 %all-gather.3.cloned.1.call-start = ((), (), s32[]{:S(2)}) async-start(), calls=%async_computation.1 | async-start | bytes 17039360 | tf_op jit(solution)/shard_map/all_gather | solution.py:45
  8.3 9.9 %copy-start.17 = (s32[32]{0:T(128)S(1)}, s32[32]{0:T(128)}, u32[]{:S(2)}) copy-start(s32[32]{0:T(128)} %param.7) | copy-start | bytes 388
  18.3 209.6 %copy-start.13 = (s32[4]{0:T(128)}, s32[4]{0:T(128)S(1)}, u32[]{:S(2)}) copy-start(s32[4]{0:T(128)S(1)} %dynamic_slice.34) | copy-start | bytes 52
  18.4 209.6 %copy-start.15 = (s32[8]{0:T(128)}, s32[8]{0:T(128)S(1)}, u32[]{:S(2)}) copy-start(s32[8]{0:T(128)S(1)} %dynamic_slice.33) | copy-start | bytes 100
  244.5 3.8 copy-start.5
  248.3 22.5 %copy-start = (bf16[8,4,1,128,128]{3,4,1,0,2:T(8,128)(2,1)S(1)}, bf16[8,4,1,128,128]{3,4,1,0,2:T(8,128)(2,1)}, u32[]{:S(2)}) copy-start(bf16[8,4,1,128,128]{3,4,1,0,2:T(8,128)(2,1)} %copy.243) | copy-start | bytes 3145732
  270.8 2.4 copy-start.2
  310.6 3.7 copy-start.7
  338.1 3.7 copy-start.3
  379.2 3.7 copy-start.8
  407.4 3.7 copy-start.4
  441.8 9.5 %copy-start.6 = (bf16[8,256,4,128]{1,0,3,2:T(8,128)(2,1)S(1)}, bf16[8,256,4,128]{1,0,3,2:T(8,128)(2,1)}, u32[]{:S(2)}) copy-start(bf16[8,256,4,128]{1,0,3,2:T(8,128)(2,1)} %copy.232) | copy-start | bytes 6291460
  474.6 3.8 copy-start.1
  478.3 22.5 %copy-start.10 = (f32[8,4,4,4]{0,3,2,1:T(4,128)S(1)}, f32[8,4,4,4]{0,3,2,1:T(4,128)}, u32[]{:S(2)}) copy-start(f32[8,4,4,4]{0,3,2,1:T(4,128)} %fusion.119) | copy-start | bytes 6148
  478.3 22.5 %copy-start.11 = (f32[8,4,4,4]{0,3,2,1:T(4,128)S(1)}, f32[8,4,4,4]{0,3,2,1:T(4,128)}, u32[]{:S(2)}) copy-start(f32[8,4,4,4]{0,3,2,1:T(4,128)} %fusion.114) | copy-start | bytes 6148
  478.3 22.5 %copy-start.12 = (f32[8,4,4,4]{0,3,2,1:T(4,128)S(1)}, f32[8,4,4,4]{0,3,2,1:T(4,128)}, u32[]{:S(2)}) copy-start(f32[8,4,4,4]{0,3,2,1:T(4,128)} %fusion.104) | copy-start | bytes 6148
  478.4 75.6 %copy-start.14 = (s32[4]{0:T(128)S(1)}, s32[4]{0:T(128)}, u32[]{:S(2)}) copy-start(s32[4]{0:T(128)} %copy-done.13) | copy-start | bytes 52
  478.4 75.6 %copy-start.16 = (s32[8]{0:T(128)S(1)}, s32[8]{0:T(128)}, u32[]{:S(2)}) copy-start(s32[8]{0:T(128)} %copy-done.15) | copy-start | bytes 100
  500.8 66.1 %copy-start.9 = (s32[32]{0:T(128)S(1)}, s32[32]{0:T(128)}, u32[]{:S(2)}) copy-start(s32[32]{0:T(128)} %reshape.603) | copy-start | bytes 388
  544.1 18.1 %all-to-all-start = ((f32[8,1,2048]{2,1,0:T(1,128)}), f32[8,1,2048]{2,1,0:T(1,128)S(1)}, u32[]{:S(2)}, u32[]{:S(2)}) async-start(f32[8,1,2048]{2,1,0:T(1,128)} %reshape.659), calls=%async_computation | async-start | bytes 131072 | tf_op jit(solution)/shard_map/all_to_all | solution.py:51
Sparse Core Ops, SparseCore 0:
  9.2 207.3 all-gather.2
where the time goes:
time: 584 us; the launch traced here: 575 us
  matrix products  209 us (36%)
  waiting for transfers between devices  193 us (33%)
  local copies, waits for them, and re-layouts  106 us (18%)
  blocking collectives  41 us (7%)
  between operations  14.1 us (2%)
  starting transfers between devices  9.91 us (2%)
    all_gather x1, waiting for transfers between devices, local(): window = lax.all_gather(chol, ('oj', 'vert'), axis=0, tiled=True)  185 us
    dot_general x8, matrix products, ladder_terms(): jnp.einsum('ijlpad,gpbd->ijlgab', half_step, blocks, preferred_element_ty...  182 us
    unnamed x58, local copies, waits for them, and re-layouts  54.7 us
    dynamic_slice x12, local copies, waits for them, and re-layouts, ladder_terms(): own_blocks = lax.dynamic_slice_in_dim(blocks, vert_first, local_count, 0)  28.7 us
    all_gather x1, blocking collectives, local(): all_irreps = lax.all_gather(ladder, 'vert', axis=2, tiled=True)  28.4 us
    dot_general x8, matrix products, ladder_terms(): jnp.einsum('lpac,ijlcd->ijlpad', own_blocks, amp_blocks, preferred_elemen...  26.9 us
    all_gather x1, blocking collectives, local(): stacked = lax.all_gather(all_irreps, 'oi', axis=0, tiled=True)  12.6 us
  transfers between devices with their start and end apart: 2, of which 2 were waited for; matrix products, arithmetic and copies ran while one was open for 4% of the time, Pallas kernels for 0%

commit v1 on v0

v1 whole, which is shorter than its diff:
```python
import jax
import jax.numpy as jnp
from jax import lax
from jax.experimental import pallas as pl
from jax.experimental.pallas import tpu as pltpu
from jax.sharding import PartitionSpec as P

IRREPS = 8
VB = 128
PB = 256
WB = 4
LO = 8
HI = VB // LO
PAIRS = 32
COLS = PAIRS * LO
AXES = ("oi", "oj", "vert")
CHIPS = [
    (x, zh, core, zl, y)
    for x in range(4)
    for zh in range(4)
    for core in range(2)
    for zl in range(2)
    for y in range(4)
]
NT = (((1,), (1,)), ((), ()))


def flat_index(x, zh, core, zl, y):
    return x * 64 + (zh * 2 + core) * 8 + zl * 4 + y


def fetch_pairs(rz, ry):
    pairs = []
    for x, zh, core, zl, y in CHIPS:
        source = (x, (zh + y + 2 * zl) % 4, zl, core ^ rz, y ^ ry)
        pairs.append((flat_index(*source), flat_index(x, zh, core, zl, y)))
    return pairs


def across_pairs():
    pairs = []
    for x, zh, core, zl, y in CHIPS:
        step = 1 if core else -1
        pairs.append((flat_index(x, zh, core, zl, y), flat_index((x + step) % 4, zh, core, zl, y)))
    return pairs


def swap_pairs():
    return [(flat_index(*d), flat_index(d[0], d[1], 1 - d[2], d[3], d[4])) for d in CHIPS]


def mirror_pairs(k):
    pairs = []
    for x in range(4):
        for col in range(8):
            target = (col // 2) * 8 + 2 * x + (k ^ (col % 2))
            pairs.append((x * 8 + col, target))
    return pairs


def spread_kernel(amp_ref, out_ref):
    wide = amp_ref[:, 0].astype(jnp.float32).reshape(PAIRS, HI, LO, VB)
    for hi in range(HI):
        out_ref[0, :, hi * VB : (hi + 1) * VB] = (
            wide[:, hi].reshape(COLS, VB).astype(jnp.bfloat16)
        )


def spread(amplitudes):
    return pl.pallas_call(
        spread_kernel,
        out_shape=jax.ShapeDtypeStruct((IRREPS, COLS, HI * VB), jnp.bfloat16),
        grid=(IRREPS,),
        in_specs=[pl.BlockSpec((PAIRS, 1, VB, VB), lambda g: (0, g, 0, 0))],
        out_specs=pl.BlockSpec((1, COLS, HI * VB), lambda g: (g, 0, 0)),
        compiler_params=pltpu.CompilerParams(vmem_limit_bytes=24 * 2**20),
        cost_estimate=pl.CostEstimate(flops=0, bytes_accessed=2**24, transcendentals=0),
    )(amplitudes)


def ladder_kernel(
    flip_ref, place_ref, *refs
):
    pieces = refs[:8]
    amp_ref, sym_ref, own_sel_ref, mirror_sel_ref, own_ref, mirror_ref = refs[8:14]
    chol, window, turned, sem = refs[14:]
    step = pl.program_id(0)

    @pl.when(step == 0)
    def _():
        copies = []
        for at in range(8):
            for ry in range(4):
                copies.append(
                    pltpu.make_async_copy(
                        pieces[at].at[ry],
                        chol.at[place_ref[2 * at] * 4 + ry, place_ref[2 * at + 1]],
                        sem.at[at * 4 + ry],
                    )
                )
        for copy in copies:
            copy.start()
        for copy in copies:
            copy.wait()
        turned[...] = jnp.zeros_like(turned)

    left = chol[step].reshape(WB * VB, PB)
    for gb in range(IRREPS):
        for half in range(2):
            right = chol[gb, 2 * half : 2 * half + 2].reshape(2 * VB, PB)
            block = lax.dot_general(left, right, NT, preferred_element_type=jnp.float32)
            for a in range(WB):
                base = ((gb * WB + a) * WB + 2 * half) * LO
                for hi in range(HI):
                    row = a * VB + hi * LO
                    window[base : base + 2 * LO, hi * VB : (hi + 1) * VB] = jnp.concatenate(
                        [block[row : row + LO, :VB], block[row : row + LO, VB:]], 0
                    ).astype(jnp.bfloat16)

    full = lax.dot_general(window[...], amp_ref[0], NT, preferred_element_type=jnp.float32)
    full = full.reshape(IRREPS * WB * WB, LO, COLS)
    lo_row = lax.broadcasted_iota(jnp.int32, (LO, COLS), 0)
    lo_col = lax.broadcasted_iota(jnp.int32, (LO, COLS), 1)
    full = jnp.where((lo_col % LO == lo_row)[None], full, 0.0)
    sums = jnp.sum(full, axis=1).reshape(IRREPS, WB * WB, COLS)
    irrep = lax.broadcasted_iota(jnp.int32, (IRREPS, 1, COLS), 0)
    wanted = jnp.bitwise_xor(sym_ref[...], step)[None]
    sums = jnp.where(irrep == wanted, sums, 0.0)
    turned[...] += sums

    row = lax.broadcasted_iota(jnp.int32, (WB * WB, VB), 0)
    group = lax.broadcasted_iota(jnp.int32, (WB * WB, VB), 1) // PAIRS
    own = jnp.dot(
        jnp.sum(sums, axis=0),
        own_sel_ref[...],
        preferred_element_type=jnp.float32,
        precision=lax.Precision.HIGHEST,
    )
    own = jnp.where(group == row % WB, own, 0.0)
    own_ref[0] = jnp.sum(own.reshape(WB, WB, VB), axis=1)

    @pl.when(step == IRREPS - 1)
    def _():
        every = turned[...].reshape(IRREPS * WB * WB, COLS)
        for k in range(2):
            other = jnp.dot(
                every,
                mirror_sel_ref[k],
                preferred_element_type=jnp.float32,
                precision=lax.Precision.HIGHEST,
            ).reshape(IRREPS, WB * WB, VB)
            other = jnp.where((group == row // WB)[None], other, 0.0)
            mirror_ref[k] = jnp.sum(other.reshape(IRREPS, WB, WB, VB), axis=1)


def ladder(flip, place, pieces, amp, sym, own_sel, mirror_sel):
    anywhere = pl.BlockSpec(memory_space=pl.ANY)
    return pl.pallas_call(
        ladder_kernel,
        out_shape=[
            jax.ShapeDtypeStruct((IRREPS, WB, VB), jnp.float32),
            jax.ShapeDtypeStruct((2, IRREPS, WB, VB), jnp.float32),
        ],
        grid_spec=pltpu.PrefetchScalarGridSpec(
            num_scalar_prefetch=2,
            grid=(IRREPS,),
            in_specs=[anywhere] * 8
            + [
                pl.BlockSpec((1, COLS, HI * VB), lambda g, flip, place: (g ^ flip[0], 0, 0)),
                pl.BlockSpec((1, COLS), lambda g, flip, place: (0, 0)),
                pl.BlockSpec((COLS, VB), lambda g, flip, place: (0, 0)),
                pl.BlockSpec((2, COLS, VB), lambda g, flip, place: (0, 0, 0)),
            ],
            out_specs=[
                pl.BlockSpec((1, WB, VB), lambda g, flip, place: (g, 0, 0)),
                pl.BlockSpec((2, IRREPS, WB, VB), lambda g, flip, place: (0, 0, 0, 0)),
            ],
            scratch_shapes=[
                pltpu.VMEM((IRREPS, WB, VB, PB), jnp.bfloat16),
                pltpu.VMEM((IRREPS * WB * WB * LO, HI * VB), jnp.bfloat16),
                pltpu.VMEM((IRREPS, WB * WB, COLS), jnp.float32),
                pltpu.SemaphoreType.DMA((32,)),
            ],
        ),
        compiler_params=pltpu.CompilerParams(vmem_limit_bytes=40 * 2**20),
        cost_estimate=pl.CostEstimate(flops=2 * 8 * 10**9, bytes_accessed=12 * 10**6, transcendentals=0),
    )(flip, place, *pieces, amp, sym, own_sel, mirror_sel)


def local(amplitudes, chol, occ_irrep):
    x = lax.axis_index("oi")
    oj = lax.axis_index("oj")
    vert = lax.axis_index("vert")
    zh, core, zl, y = oj // 2, oj % 2, vert // 4, vert % 4
    even = x % 2

    def permute(value, pairs):
        return lax.ppermute(value, AXES, pairs)

    own = jnp.transpose(chol[0], (1, 2, 0))
    quarters = [lax.dynamic_index_in_dim(own, 2 * even + (zl ^ rz), 0, False) for rz in range(2)]
    pieces, place = [], []
    for rz in range(2):
        near = jnp.stack([permute(quarters[rz], fetch_pairs(rz, ry)) for ry in range(4)])
        far = permute(near, across_pairs())
        pieces += [near, far, permute(near, swap_pairs()), permute(far, swap_pairs())]
        first = core ^ rz ^ zl
        place += [first, 2 * even + core, first, 2 * (1 - even) + core]
        place += [1 - first, 2 * even + 1 - core, 1 - first, 2 * (1 - even) + 1 - core]
    place = jnp.stack(place).astype(jnp.int32)

    block = ((zh + y + 2 * zl) % 4) * 2 + zl
    flip = (block ^ vert).astype(jnp.int32)[None]
    occ_rows, occ_cols = amplitudes.shape[0], amplitudes.shape[1]
    irrep_rows = lax.dynamic_slice_in_dim(occ_irrep, x * occ_rows, occ_rows)
    irrep_cols = lax.dynamic_slice_in_dim(occ_irrep, oj * occ_cols, occ_cols)
    sym = jnp.bitwise_xor(irrep_rows[:, None], irrep_cols[None, :])
    sym = jnp.broadcast_to(sym.reshape(1, PAIRS, 1), (1, PAIRS, LO)).reshape(1, COLS)

    pair = jnp.arange(COLS, dtype=jnp.int32)[:, None] // LO
    lane = jnp.arange(VB, dtype=jnp.int32)[None, :] % PAIRS
    own_sel = (pair == lane).astype(jnp.float32)
    row, col = pair // occ_cols, pair % occ_cols
    spot = core * 16 + col * 4 + row % 4
    mirror_sel = jnp.stack(
        [((lane == spot) & (row // 4 == (core ^ k))).astype(jnp.float32) for k in range(2)]
    )

    amp = spread(amplitudes.reshape(PAIRS, IRREPS, VB, VB))
    mine, other = ladder(flip, place, pieces, amp, sym, own_sel, mirror_sel)
    total = mine
    for k in range(2):
        total = total + lax.ppermute(other[k], ("oi", "oj"), mirror_pairs(k))
    for bit in (4, 2, 1):
        pairs = [(v, v ^ bit) for v in range(IRREPS)]
        total = total[:bit] + lax.ppermute(total[bit:], "vert", pairs)
    total = total.reshape(WB, WB, occ_rows, occ_cols)
    return jnp.transpose(total, (2, 3, 0, 1))[:, :, None]


def solution(mesh):
    return jax.shard_map(
        local,
        mesh=mesh,
        in_specs=(P("oi", "oj", None, None, None), P(("oj", "vert"), None, None, None), P()),
        out_specs=P("oi", "oj", "vert", None, None),
        check_vma=False,
    )
```

time: 584 us -> 109 us (0.19); the launches traced: 575 us -> 108 us
  matrix products: 209 us -> 0 us
  waiting for transfers between devices: 193 us -> 17.4 us
  local copies, waits for them, and re-layouts: 106 us -> 14.3 us
  blocking collectives: 41 us -> 0 us
  starting transfers between devices: 9.91 us -> 46.7 us
  Pallas kernels: 0 us -> 29.3 us
  between operations: 14.1 us -> 0.21 us
    dot_general x16 -> x0, matrix products: 209 us -> none  [the longest x8 182 us: ladder_terms(): jnp.einsum('ijlpad,gpbd->ijlgab', half_step, blocks, preferred_element_ty...]
    all_gather x1 -> x0, waiting for transfers between devices: 185 us -> none  [local(): window = lax.all_gather(chol, ('oj', 'vert'), axis=0, tiled=True)]
    ppermute x0 -> x19, starting transfers between devices: none -> 46.7 us  [the longest x14 26.9 us: permute(): return lax.ppermute(value, AXES, pairs)]
    unnamed x58 -> x6, local copies, waits for them, and re-layouts: 54.7 us -> 10 us
    all_gather x2 -> x0, blocking collectives: 41 us -> none  [the longest x1 28.4 us: local(): all_irreps = lax.all_gather(ladder, 'vert', axis=2, tiled=True)]
    pallas_call x0 -> x2, Pallas kernels: none -> 29.3 us  [the longest x1 26.3 us: ladder(): pl.pallas_call(ladder_kernel, out_shape=[jax.ShapeDtypeStruct((IRREPS, WB...]
    dynamic_slice x15 -> x2, local copies, waits for them, and re-layouts: 28.9 us -> 1.46 us  [the longest x1 0.73 us: local(): irrep_cols = lax.dynamic_slice_in_dim(occ_irrep, oj * occ_cols, occ_cols)]
    ppermute x0 -> x19, waiting for transfers between devices: none -> 17.4 us  [the longest x3 6.8 us: local(): total = total[:bit] + lax.ppermute(total[bit:], 'vert', pairs)]
  transfers between devices with their start and end apart: 2 -> 19, of which waited for: 2 -> 7; matrix products, arithmetic and copies ran while one was open for 4% -> 2% of each run, Pallas kernels for 0% -> 3%
where the time goes in v1:
time: 109 us; the launch traced here: 108 us
  starting transfers between devices  46.7 us (43%)
  Pallas kernels  29.3 us (27%)
  waiting for transfers between devices  17.4 us (16%)
  local copies, waits for them, and re-layouts  14.3 us (13%)
    ppermute x14, starting transfers between devices, permute(): return lax.ppermute(value, AXES, pairs)  26.9 us
    pallas_call x1, Pallas kernels, ladder(): pl.pallas_call(ladder_kernel, out_shape=[jax.ShapeDtypeStruct((IRREPS, WB...  26.3 us
    ppermute x3, starting transfers between devices, local(): total = total[:bit] + lax.ppermute(total[bit:], 'vert', pairs)  10.2 us
    unnamed x6, local copies, waits for them, and re-layouts  10 us
    ppermute x2, starting transfers between devices, local(): total = total + lax.ppermute(other[k], ('oi', 'oj'), mirror_pairs(k))  9.66 us
    ppermute x3, waiting for transfers between devices, local(): total = total[:bit] + lax.ppermute(total[bit:], 'vert', pairs)  6.8 us
    ppermute x2, waiting for transfers between devices, local(): total = total + lax.ppermute(other[k], ('oi', 'oj'), mirror_pairs(k))  5.42 us
    ppermute x14, waiting for transfers between devices, permute(): return lax.ppermute(value, AXES, pairs)  5.14 us
  transfers between devices with their start and end apart: 19, of which 7 were waited for; matrix products, arithmetic and copies ran while one was open for 2% of the time, Pallas kernels for 3%

profile of v1, /device:TPU:4, one launch (start us, length us, event | category | flops | bytes accessed | tf_op | source)
XLA Modules:
  0.0 108.3 jit_solution(231414019580723859)
XLA Ops:
  0.0 1.3 %constant_dynamic-slice_fusion = (bf16[1,256,1,128]{3,2,1,0:T(2,128)(2,1)S(1)}, bf16[1,256,1,128]{3,2,1,0:T(2,128)(2,1)S(1)}) fusion(bf16[1,256,4,128]{3,2,1,0:T(4,128)(2,1)} %param.4, s32[]{:T(128)S(6)} %select_n.138, s32[]{:T(128)S(6)} %select_n.137), kind=kLoop, calls=%fused_computation.36 | loop fusion | bytes 262152 | tf_op jit(solution)/shard_map/dynamic-slice.3
  1.3 0.1 copy.8
  1.5 5.2 %collective-permute-start.10 = (bf16[128,256]{1,0:T(8,128)(2,1)S(1)}, bf16[128,256]{1,0:T(8,128)(2,1)S(1)}, u32[]{:S(2)}, u32[]{:S(2)}) collective-permute-start(bf16[128,256]{1,0:T(8,128)(2,1)S(1)} %bitcast.46), channel_id=1, source_target_pairs={{7,0},{22,1},{37,2},{52,3},{47,4},{62,5},{13,6},{28,7},{3,8},{18,9... | collective-permute-start | bytes 196616 | tf_op jit(solution)/shard_map/ppermute | solution.py:198
  6.7 5.6 %collective-permute-start.9 = (bf16[128,256]{1,0:T(8,128)(2,1)S(1)}, bf16[128,256]{1,0:T(8,128)(2,1)S(1)}, u32[]{:S(2)}, u32[]{:S(2)}) collective-permute-start(bf16[128,256]{1,0:T(8,128)(2,1)S(1)} %bitcast.47), channel_id=1, source_target_pairs={{6,0},{23,1},{36,2},{53,3},{46,4},{63,5},{12,6},{29,7},{2,8},{19,9... | collective-permute-start | bytes 196616 | tf_op jit(solution)/shard_map/ppermute | solution.py:198
  12.3 0.0 collective-permute-start.8
  12.3 0.1 copy.7
  12.5 3.9 %collective-permute-start.3 = (bf16[128,256]{1,0:T(8,128)(2,1)S(1)}, bf16[128,256]{1,0:T(8,128)(2,1)S(1)}, u32[]{:S(2)}, u32[]{:S(2)}) collective-permute-start(bf16[128,256]{1,0:T(8,128)(2,1)S(1)} %bitcast.42), channel_id=1, source_target_pairs={{3,0},{18,1},{33,2},{48,3},{43,4},{58,5},{9,6},{24,7},{7,8},{22,9}... | collective-permute-start | bytes 196616 | tf_op jit(solution)/shard_map/ppermute | solution.py:198
  16.4 0.2 compare_and_fusion.1
  16.6 0.0 collective-permute-done.10
  16.6 6.3 %collective-permute-start.2 = (bf16[128,256]{1,0:T(8,128)(2,1)S(1)}, bf16[128,256]{1,0:T(8,128)(2,1)S(1)}, u32[]{:S(2)}, u32[]{:S(2)}) collective-permute-start(bf16[128,256]{1,0:T(8,128)(2,1)S(1)} %bitcast.43), channel_id=1, source_target_pairs={{2,0},{19,1},{32,2},{49,3},{42,4},{59,5},{8,6},{25,7},{6,8},{23,9}... | collective-permute-start | bytes 196616 | tf_op jit(solution)/shard_map/ppermute | solution.py:198
  22.9 0.0 collective-permute-done.9
  22.9 0.0 collective-permute-start.1
  22.9 0.7 collective-permute-start
  23.7 0.6 collective-permute-start.11
  24.3 3.8 %collective-permute-done.2 = bf16[128,256]{1,0:T(8,128)(2,1)S(1)} collective-permute-done((bf16[128,256]{1,0:T(8,128)(2,1)S(1)}, bf16[128,256]{1,0:T(8,128)(2,1)S(1)}, u32[]{:S(2)}, u32[]{:S(2)}) %collective-permute-start.2) | collective-permute-done | bytes 65568 | tf_op jit(solution)/shard_map/ppermute | solution.py:198
  28.1 0.0 collective-permute-done.1
  28.1 0.0 collective-permute-done
  28.1 0.6 collective-permute-start.4
  28.8 0.7 dynamic_slice.16
  29.5 0.7 dynamic_slice.15
  30.2 0.1 broadcast_xor_fusion
  30.3 2.5 %collective-permute-start.12 = (bf16[4,128,256]{2,1,0:T(8,128)(2,1)S(1)}, bf16[4,128,256]{2,1,0:T(8,128)(2,1)S(1)}, u32[]{:S(2)}, u32[]{:S(2)}) collective-permute-start(bf16[4,128,256]{2,1,0:T(8,128)(2,1)S(1)} %pad_maximum_fusion.1.refs_4_), channel_id=1, source_target_pairs={{0,8},{1,9},{2,10},{3,11},{4,12},{5,13},{6,14},{7,15},{8,0},{9,1},... | collective-permute-start | bytes 786440 | tf_op jit(solution)/shard_map/ppermute | solution.py:198
  32.8 0.1 collective-permute-start.5
  32.8 0.5 collective-permute-start.13
  33.3 1.3 %collective-permute-done.4.refs_1_ = bf16[4,128,256]{2,1,0:T(8,128)(2,1)S(1)} collective-permute-done((bf16[4,128,256]{2,1,0:T(8,128)(2,1)S(1)}, bf16[4,128,256]{2,1,0:T(8,128)(2,1)S(1)}, u32[]{:S(2)}, u32[]{:S(2)}) %collective-permute-start.4) | collective-permute-done | bytes 262176 | tf_op jit(solution)/shard_map/ppermute | solution.py:198
  34.6 0.9 collective-permute-start.6
  35.5 0.1 xor.44
  35.6 0.1 broadcast_in_dim.18
  35.7 0.1 broadcast_in_dim.19.refs_9_
  35.8 0.0 copy-start
  35.8 3.4 %copy-done = bf16[8,4,8,128,128]{4,3,2,1,0:T(8,128)(2,1)S(1)} copy-done((bf16[8,4,8,128,128]{4,3,2,1,0:T(8,128)(2,1)S(1)}, bf16[8,4,8,128,128]{4,3,2,1,0:T(8,128)(2,1)}, u32[]{:S(2)}) %copy-start) | copy-done | bytes 8388632
  39.1 2.9 %shard_map.37.refs_8_ = bf16[8,256,2048]{2,1,0:T(8,128)(2,1)S(1)} custom-call(bf16[32,8,128,128]{3,2,1,0:T(8,128)(2,1)S(1)} %bitcast.39), custom_call_target="tpu_custom_call" | custom-call | bytes 16777216 | tf_op jit(solution)/shard_map/pallas_call | solution.py:70
  42.1 3.3 %copy-done.1 = bf16[8,256,2048]{2,1,0:T(8,128)(2,1)} copy-done((bf16[8,256,2048]{2,1,0:T(8,128)(2,1)}, bf16[8,256,2048]{2,1,0:T(8,128)(2,1)S(1)}, u32[]{:S(2)}) %copy-start.1) | copy-done | bytes 8388632
  45.3 0.1 stack.80.place_ref
  45.4 0.1 compare_convert_fusion.refs_10_
  45.6 3.4 %copy-done.2 = bf16[8,256,2048]{2,1,0:T(8,128)(2,1)S(1)} copy-done((bf16[8,256,2048]{2,1,0:T(8,128)(2,1)S(1)}, bf16[8,256,2048]{2,1,0:T(8,128)(2,1)}, u32[]{:S(2)}) %copy-start.2) | copy-done | bytes 8388632
  49.0 26.3 %shard_map.38 = (f32[8,4,128]{2,1,0:T(4,128)S(1)}, f32[2,8,4,128]{3,2,1,0:T(4,128)S(1)}) custom-call(s32[1]{0:T(128)} %bitcast.flip_ref, s32[16]{0:T(128)S(1)} %stack.80.place_ref, bf16[4,128,256]{2,1,0:T(8,128)(2,1)S(1)} %pad_maximum_fusion.refs_0_, bf16[4,128,256]{2,1,0:T(8,128)(2,1)S(1)} %collective-permute-done.4.refs_1_, ...), custom_call_target="tpu_custom_call" | custom-call | flops 16000000000 | bytes 12000000 | tf_op jit(solution)/shard_map/pallas_call | solution.py:158
  75.3 5.3 %collective-permute-start.14 = (f32[8,4,128]{2,1,0:T(4,128)S(1)}, f32[8,4,128]{2,1,0:T(4,128)S(1)}, u32[]{:S(2)}, u32[]{:S(2)}) collective-permute-start(f32[8,4,128]{2,1,0:T(4,128)S(1)} %get-tuple-element.11), channel_id=1, source_target_pairs={{0,0},{8,8},{16,64},{24,72},{32,128},{40,136},{48,192},{56,200},{6... | collective-permute-start | bytes 49160 | tf_op jit(solution)/shard_map/ppermute | solution.py:233
  80.7 4.3 %collective-permute-start.15 = (f32[8,4,128]{2,1,0:T(4,128)S(1)}, f32[8,4,128]{2,1,0:T(4,128)S(1)}, u32[]{:S(2)}, u32[]{:S(2)}) collective-permute-start(f32[8,4,128]{2,1,0:T(4,128)S(1)} %get-tuple-element.12), channel_id=1, source_target_pairs={{0,8},{8,0},{16,72},{24,64},{32,136},{40,128},{48,200},{56,192},{6... | collective-permute-start | bytes 49160 | tf_op jit(solution)/shard_map/ppermute | solution.py:233
  85.0 2.3 %collective-permute-done.14 = f32[8,4,128]{2,1,0:T(4,128)S(1)} collective-permute-done((f32[8,4,128]{2,1,0:T(4,128)S(1)}, f32[8,4,128]{2,1,0:T(4,128)S(1)}, u32[]{:S(2)}, u32[]{:S(2)}) %collective-permute-start.14) | collective-permute-done | bytes 16416 | tf_op jit(solution)/shard_map/ppermute | solution.py:233
  87.3 3.2 %collective-permute-done.15 = f32[8,4,128]{2,1,0:T(4,128)S(1)} collective-permute-done((f32[8,4,128]{2,1,0:T(4,128)S(1)}, f32[8,4,128]{2,1,0:T(4,128)S(1)}, u32[]{:S(2)}, u32[]{:S(2)}) %collective-permute-start.15) | collective-permute-done | bytes 16416 | tf_op jit(solution)/shard_map/ppermute | solution.py:233
  90.4 4.4 %collective-permute-start.16 = (f32[4,4,128]{2,1,0:T(4,128)S(1)}, f32[4,4,128]{2,1,0:T(4,128)S(1)}, u32[]{:S(2)}, u32[]{:S(2)}) collective-permute-start(f32[4,4,128]{2,1,0:T(4,128)S(1)} %slice.33), channel_id=1, source_target_pairs={{0,4},{1,5},{2,6},{3,7},{4,0},{5,1},{6,2},{7,3},{8,12},{9,13},{10,... | collective-permute-start | bytes 24584 | tf_op jit(solution)/shard_map/ppermute | solution.py:236
  94.9 1.6 %collective-permute-done.16 = f32[4,4,128]{2,1,0:T(4,128)S(1)} collective-permute-done((f32[4,4,128]{2,1,0:T(4,128)S(1)}, f32[4,4,128]{2,1,0:T(4,128)S(1)}, u32[]{:S(2)}, u32[]{:S(2)}) %collective-permute-start.16) | collective-permute-done | bytes 8224 | tf_op jit(solution)/shard_map/ppermute | solution.py:236
  96.5 5.8 %collective-permute-start.17 = (f32[2,4,128]{2,1,0:T(4,128)S(1)}, f32[2,4,128]{2,1,0:T(4,128)S(1)}, u32[]{:S(2)}, u32[]{:S(2)}) collective-permute-start(f32[2,4,128]{2,1,0:T(4,128)S(1)} %slice.35), channel_id=1, source_target_pairs={{0,2},{1,3},{2,0},{3,1},{4,6},{5,7},{6,4},{7,5},{8,10},{9,11},{10,... | collective-permute-start | bytes 12296 | tf_op jit(solution)/shard_map/ppermute | solution.py:236
  102.3 1.6 %collective-permute-done.17 = f32[2,4,128]{2,1,0:T(4,128)S(1)} collective-permute-done((f32[2,4,128]{2,1,0:T(4,128)S(1)}, f32[2,4,128]{2,1,0:T(4,128)S(1)}, u32[]{:S(2)}, u32[]{:S(2)}) %collective-permute-start.17) | collective-permute-done | bytes 4128 | tf_op jit(solution)/shard_map/ppermute | solution.py:236
  103.9 3.6 %collective-permute-done.18 = f32[1,4,128]{2,1,0:T(4,128)S(1)} collective-permute-done((f32[1,4,128]{2,1,0:T(4,128)S(1)}, f32[1,4,128]{2,1,0:T(4,128)S(1)}, u32[]{:S(2)}, u32[]{:S(2)}) %collective-permute-start.18) | collective-permute-done | bytes 2080 | tf_op jit(solution)/shard_map/ppermute | solution.py:236
  107.4 0.1 reshape.336
  107.6 0.8 copy.9
  (27 shorter events, 0.2 us)
Async XLA Ops:
  1.5 15.1 %collective-permute-start.10 = (bf16[128,256]{1,0:T(8,128)(2,1)S(1)}, bf16[128,256]{1,0:T(8,128)(2,1)S(1)}, u32[]{:S(2)}, u32[]{:S(2)}) collective-permute-start(bf16[128,256]{1,0:T(8,128)(2,1)S(1)} %bitcast.46), channel_id=1, source_target_pairs={{7,0},{22,1},{37,2},{52,3},{47,4},{62,5},{13,6},{28,7},{3,8},{18,9... | collective-permute-start | bytes 196616 | tf_op jit(solution)/shard_map/ppermute | solution.py:198
  6.7 16.2 %collective-permute-start.9 = (bf16[128,256]{1,0:T(8,128)(2,1)S(1)}, bf16[128,256]{1,0:T(8,128)(2,1)S(1)}, u32[]{:S(2)}, u32[]{:S(2)}) collective-permute-start(bf16[128,256]{1,0:T(8,128)(2,1)S(1)} %bitcast.47), channel_id=1, source_target_pairs={{6,0},{23,1},{36,2},{53,3},{46,4},{63,5},{12,6},{29,7},{2,8},{19,9... | collective-permute-start | bytes 196616 | tf_op jit(solution)/shard_map/ppermute | solution.py:198
  12.3 10.6 %collective-permute-start.8 = (bf16[128,256]{1,0:T(8,128)(2,1)S(1)}, bf16[128,256]{1,0:T(8,128)(2,1)S(1)}, u32[]{:S(2)}, u32[]{:S(2)}) collective-permute-start(bf16[128,256]{1,0:T(8,128)(2,1)S(1)} %bitcast.48), channel_id=1, source_target_pairs={{5,0},{20,1},{39,2},{54,3},{45,4},{60,5},{15,6},{30,7},{1,8},{16,9... | collective-permute-start | bytes 196616 | tf_op jit(solution)/shard_map/ppermute | solution.py:198
  12.3 11.3 %collective-permute-start.7 = (bf16[128,256]{1,0:T(8,128)(2,1)S(1)}, bf16[128,256]{1,0:T(8,128)(2,1)S(1)}, u32[]{:S(2)}, u32[]{:S(2)}) collective-permute-start(bf16[128,256]{1,0:T(8,128)(2,1)S(1)} %bitcast.49), channel_id=1, source_target_pairs={{4,0},{21,1},{38,2},{55,3},{44,4},{61,5},{14,6},{31,7},{0,8},{17,9... | collective-permute-start | bytes 196616 | tf_op jit(solution)/shard_map/ppermute | solution.py:198
  12.5 11.8 %collective-permute-start.3 = (bf16[128,256]{1,0:T(8,128)(2,1)S(1)}, bf16[128,256]{1,0:T(8,128)(2,1)S(1)}, u32[]{:S(2)}, u32[]{:S(2)}) collective-permute-start(bf16[128,256]{1,0:T(8,128)(2,1)S(1)} %bitcast.42), channel_id=1, source_target_pairs={{3,0},{18,1},{33,2},{48,3},{43,4},{58,5},{9,6},{24,7},{7,8},{22,9}... | collective-permute-start | bytes 196616 | tf_op jit(solution)/shard_map/ppermute | solution.py:198
  16.6 11.5 %collective-permute-start.2 = (bf16[128,256]{1,0:T(8,128)(2,1)S(1)}, bf16[128,256]{1,0:T(8,128)(2,1)S(1)}, u32[]{:S(2)}, u32[]{:S(2)}) collective-permute-start(bf16[128,256]{1,0:T(8,128)(2,1)S(1)} %bitcast.43), channel_id=1, source_target_pairs={{2,0},{19,1},{32,2},{49,3},{42,4},{59,5},{8,6},{25,7},{6,8},{23,9}... | collective-permute-start | bytes 196616 | tf_op jit(solution)/shard_map/ppermute | solution.py:198
  22.9 5.2 %collective-permute-start.1 = (bf16[128,256]{1,0:T(8,128)(2,1)S(1)}, bf16[128,256]{1,0:T(8,128)(2,1)S(1)}, u32[]{:S(2)}, u32[]{:S(2)}) collective-permute-start(bf16[128,256]{1,0:T(8,128)(2,1)S(1)} %bitcast.44), channel_id=1, source_target_pairs={{1,0},{16,1},{35,2},{50,3},{41,4},{56,5},{11,6},{26,7},{5,8},{20,9... | collective-permute-start | bytes 196616 | tf_op jit(solution)/shard_map/ppermute | solution.py:198
  22.9 5.2 %collective-permute-start = (bf16[128,256]{1,0:T(8,128)(2,1)S(1)}, bf16[128,256]{1,0:T(8,128)(2,1)S(1)}, u32[]{:S(2)}, u32[]{:S(2)}) collective-permute-start(bf16[128,256]{1,0:T(8,128)(2,1)S(1)} %bitcast.45), channel_id=1, source_target_pairs={{0,0},{17,1},{34,2},{51,3},{40,4},{57,5},{10,6},{27,7},{4,8},{21,9... | collective-permute-start | bytes 196616 | tf_op jit(solution)/shard_map/ppermute | solution.py:198
  23.7 9.1 %collective-permute-start.11 = (bf16[4,128,256]{2,1,0:T(8,128)(2,1)S(1)}, bf16[4,128,256]{2,1,0:T(8,128)(2,1)S(1)}, u32[]{:S(2)}, u32[]{:S(2)}) collective-permute-start(bf16[4,128,256]{2,1,0:T(8,128)(2,1)S(1)} %pad_maximum_fusion.1.refs_4_), channel_id=1, source_target_pairs={{0,192},{1,193},{2,194},{3,195},{4,196},{5,197},{6,198},{7,199},{8... | collective-permute-start | bytes 786440 | tf_op jit(solution)/shard_map/ppermute | solution.py:198
  28.1 6.4 %collective-permute-start.4 = (bf16[4,128,256]{2,1,0:T(8,128)(2,1)S(1)}, bf16[4,128,256]{2,1,0:T(8,128)(2,1)S(1)}, u32[]{:S(2)}, u32[]{:S(2)}) collective-permute-start(bf16[4,128,256]{2,1,0:T(8,128)(2,1)S(1)} %pad_maximum_fusion.refs_0_), channel_id=1, source_target_pairs={{0,192},{1,193},{2,194},{3,195},{4,196},{5,197},{6,198},{7,199},{8... | collective-permute-start | bytes 786440 | tf_op jit(solution)/shard_map/ppermute | solution.py:198
  30.3 15.2 %collective-permute-start.12 = (bf16[4,128,256]{2,1,0:T(8,128)(2,1)S(1)}, bf16[4,128,256]{2,1,0:T(8,128)(2,1)S(1)}, u32[]{:S(2)}, u32[]{:S(2)}) collective-permute-start(bf16[4,128,256]{2,1,0:T(8,128)(2,1)S(1)} %pad_maximum_fusion.1.refs_4_), channel_id=1, source_target_pairs={{0,8},{1,9},{2,10},{3,11},{4,12},{5,13},{6,14},{7,15},{8,0},{9,1},... | collective-permute-start | bytes 786440 | tf_op jit(solution)/shard_map/ppermute | solution.py:198
  32.8 12.8 %collective-permute-start.5 = (bf16[4,128,256]{2,1,0:T(8,128)(2,1)S(1)}, bf16[4,128,256]{2,1,0:T(8,128)(2,1)S(1)}, u32[]{:S(2)}, u32[]{:S(2)}) collective-permute-start(bf16[4,128,256]{2,1,0:T(8,128)(2,1)S(1)} %pad_maximum_fusion.refs_0_), channel_id=1, source_target_pairs={{0,8},{1,9},{2,10},{3,11},{4,12},{5,13},{6,14},{7,15},{8,0},{9,1},... | collective-permute-start | bytes 786440 | tf_op jit(solution)/shard_map/ppermute | solution.py:198
  32.8 12.8 %collective-permute-start.13 = (bf16[4,128,256]{2,1,0:T(8,128)(2,1)S(1)}, bf16[4,128,256]{2,1,0:T(8,128)(2,1)S(1)}, u32[]{:S(2)}, u32[]{:S(2)}) collective-permute-start(bf16[4,128,256]{2,1,0:T(8,128)(2,1)S(1)} %collective-permute-done.11.refs_5_), channel_id=1, source_target_pairs={{0,8},{1,9},{2,10},{3,11},{4,12},{5,13},{6,14},{7,15},{8,0},{9,1},... | collective-permute-start | bytes 786440 | tf_op jit(solution)/shard_map/ppermute | solution.py:198
  34.6 11.0 %collective-permute-start.6 = (bf16[4,128,256]{2,1,0:T(8,128)(2,1)S(1)}, bf16[4,128,256]{2,1,0:T(8,128)(2,1)S(1)}, u32[]{:S(2)}, u32[]{:S(2)}) collective-permute-start(bf16[4,128,256]{2,1,0:T(8,128)(2,1)S(1)} %collective-permute-done.4.refs_1_), channel_id=1, source_target_pairs={{0,8},{1,9},{2,10},{3,11},{4,12},{5,13},{6,14},{7,15},{8,0},{9,1},... | collective-permute-start | bytes 786440 | tf_op jit(solution)/shard_map/ppermute | solution.py:198
  35.8 3.4 %copy-start = (bf16[8,4,8,128,128]{4,3,2,1,0:T(8,128)(2,1)S(1)}, bf16[8,4,8,128,128]{4,3,2,1,0:T(8,128)(2,1)}, u32[]{:S(2)}) copy-start(bf16[8,4,8,128,128]{4,3,2,1,0:T(8,128)(2,1)} %param.3) | copy-start | bytes 25165828
  42.1 3.3 %copy-start.1 = (bf16[8,256,2048]{2,1,0:T(8,128)(2,1)}, bf16[8,256,2048]{2,1,0:T(8,128)(2,1)S(1)}, u32[]{:S(2)}) copy-start(bf16[8,256,2048]{2,1,0:T(8,128)(2,1)S(1)} %shard_map.37.refs_8_) | copy-start | bytes 25165828
  45.6 3.4 %copy-start.2 = (bf16[8,256,2048]{2,1,0:T(8,128)(2,1)S(1)}, bf16[8,256,2048]{2,1,0:T(8,128)(2,1)}, u32[]{:S(2)}) copy-start(bf16[8,256,2048]{2,1,0:T(8,128)(2,1)} %copy-done.1) | copy-start | bytes 25165828
  75.3 11.9 %collective-permute-start.14 = (f32[8,4,128]{2,1,0:T(4,128)S(1)}, f32[8,4,128]{2,1,0:T(4,128)S(1)}, u32[]{:S(2)}, u32[]{:S(2)}) collective-permute-start(f32[8,4,128]{2,1,0:T(4,128)S(1)} %get-tuple-element.11), channel_id=1, source_target_pairs={{0,0},{8,8},{16,64},{24,72},{32,128},{40,136},{48,192},{56,200},{6... | collective-permute-start | bytes 49160 | tf_op jit(solution)/shard_map/ppermute | solution.py:233
  80.7 9.7 %collective-permute-start.15 = (f32[8,4,128]{2,1,0:T(4,128)S(1)}, f32[8,4,128]{2,1,0:T(4,128)S(1)}, u32[]{:S(2)}, u32[]{:S(2)}) collective-permute-start(f32[8,4,128]{2,1,0:T(4,128)S(1)} %get-tuple-element.12), channel_id=1, source_target_pairs={{0,8},{8,0},{16,72},{24,64},{32,136},{40,128},{48,200},{56,192},{6... | collective-permute-start | bytes 49160 | tf_op jit(solution)/shard_map/ppermute | solution.py:233
  90.4 6.0 %collective-permute-start.16 = (f32[4,4,128]{2,1,0:T(4,128)S(1)}, f32[4,4,128]{2,1,0:T(4,128)S(1)}, u32[]{:S(2)}, u32[]{:S(2)}) collective-permute-start(f32[4,4,128]{2,1,0:T(4,128)S(1)} %slice.33), channel_id=1, source_target_pairs={{0,4},{1,5},{2,6},{3,7},{4,0},{5,1},{6,2},{7,3},{8,12},{9,13},{10,... | collective-permute-start | bytes 24584 | tf_op jit(solution)/shard_map/ppermute | solution.py:236
  96.5 7.4 %collective-permute-start.17 = (f32[2,4,128]{2,1,0:T(4,128)S(1)}, f32[2,4,128]{2,1,0:T(4,128)S(1)}, u32[]{:S(2)}, u32[]{:S(2)}) collective-permute-start(f32[2,4,128]{2,1,0:T(4,128)S(1)} %slice.35), channel_id=1, source_target_pairs={{0,2},{1,3},{2,0},{3,1},{4,6},{5,7},{6,4},{7,5},{8,10},{9,11},{10,... | collective-permute-start | bytes 12296 | tf_op jit(solution)/shard_map/ppermute | solution.py:236
  103.9 3.6 %collective-permute-start.18 = (f32[1,4,128]{2,1,0:T(4,128)S(1)}, f32[1,4,128]{2,1,0:T(4,128)S(1)}, u32[]{:S(2)}, u32[]{:S(2)}) collective-permute-start(f32[1,4,128]{2,1,0:T(4,128)S(1)} %slice.37), channel_id=1, source_target_pairs={{0,1},{1,0},{2,3},{3,2},{4,5},{5,4},{6,7},{7,6},{8,9},{9,8},{10,11... | collective-permute-start | bytes 6152 | tf_op jit(solution)/shard_map/ppermute | solution.py:236

commit v2 on v1

--- a/solution.py
+++ b/solution.py
@@ -29,53 +29,40 @@
     return x * 64 + (zh * 2 + core) * 8 + zl * 4 + y
 
 
-def fetch_pairs(rz, ry):
+def fetch_pairs(far):
     pairs = []
     for x, zh, core, zl, y in CHIPS:
-        source = (x, (zh + y + 2 * zl) % 4, zl, core ^ rz, y ^ ry)
+        source = (x, (zh + y + 2 * zl) % 4, zl, core, y ^ (2 * far))
         pairs.append((flat_index(*source), flat_index(x, zh, core, zl, y)))
     return pairs
 
 
-def across_pairs():
-    pairs = []
-    for x, zh, core, zl, y in CHIPS:
-        step = 1 if core else -1
-        pairs.append((flat_index(x, zh, core, zl, y), flat_index((x + step) % 4, zh, core, zl, y)))
-    return pairs
-
-
-def swap_pairs():
-    return [(flat_index(*d), flat_index(d[0], d[1], 1 - d[2], d[3], d[4])) for d in CHIPS]
-
-
-def mirror_pairs(k):
-    pairs = []
-    for x in range(4):
-        for col in range(8):
-            target = (col // 2) * 8 + 2 * x + (k ^ (col % 2))
-            pairs.append((x * 8 + col, target))
-    return pairs
-
-
-def spread_kernel(amp_ref, out_ref):
-    wide = amp_ref[:, 0].astype(jnp.float32).reshape(PAIRS, HI, LO, VB)
-    for hi in range(HI):
-        out_ref[0, :, hi * VB : (hi + 1) * VB] = (
-            wide[:, hi].reshape(COLS, VB).astype(jnp.bfloat16)
-        )
-
-
-def spread(amplitudes):
-    return pl.pallas_call(
-        spread_kernel,
-        out_shape=jax.ShapeDtypeStruct((IRREPS, COLS, HI * VB), jnp.bfloat16),
-        grid=(IRREPS,),
-        in_specs=[pl.BlockSpec((PAIRS, 1, VB, VB), lambda g: (0, g, 0, 0))],
-        out_specs=pl.BlockSpec((1, COLS, HI * VB), lambda g: (g, 0, 0)),
-        compiler_params=pltpu.CompilerParams(vmem_limit_bytes=24 * 2**20),
-        cost_estimate=pl.CostEstimate(flops=0, bytes_accessed=2**24, transcendentals=0),
-    )(amplitudes)
+def moved_pairs(move):
+    return [(flat_index(*d), flat_index(*move(*d))) for d in CHIPS]
+
+
+def next_row(x, zh, core, zl, y):
+    return (x, zh, core, zl, y ^ 1)
+
+
+def lower(x, zh, core, zl, y):
+    return ((x + 3) % 4, zh, core, zl, y)
+
+
+def upper(x, zh, core, zl, y):
+    return ((x + 1) % 4, zh, core, zl, y)
+
+
+def apart(x, zh, core, zl, y):
+    return ((x + (1 if core else 3)) % 4, zh, core, zl, y)
+
+
+def other_core(x, zh, core, zl, y):
+    return (x, zh, 1 - core, zl, y)
+
+
+def mirrored(x, zh, core, zl, y):
+    return (zh, x, core, zl, y)
 
 
 def ladder_kernel(
@@ -83,7 +70,7 @@
 ):
     pieces = refs[:8]
     amp_ref, sym_ref, own_sel_ref, mirror_sel_ref, own_ref, mirror_ref = refs[8:14]
-    chol, window, turned, sem = refs[14:]
+    chol, window, spread, turned, sem = refs[14:]
     step = pl.program_id(0)
 
     @pl.when(step == 0)
@@ -104,6 +91,10 @@
             copy.wait()
         turned[...] = jnp.zeros_like(turned)
 
+    wide = amp_ref[:, 0].astype(jnp.float32).reshape(PAIRS, HI, LO, VB)
+    for hi in range(HI):
+        spread[:, hi * VB : (hi + 1) * VB] = wide[:, hi].reshape(COLS, VB).astype(jnp.bfloat16)
+
     left = chol[step].reshape(WB * VB, PB)
     for gb in range(IRREPS):
         for half in range(2):
@@ -117,7 +108,7 @@
                         [block[row : row + LO, :VB], block[row : row + LO, VB:]], 0
                     ).astype(jnp.bfloat16)
 
-    full = lax.dot_general(window[...], amp_ref[0], NT, preferred_element_type=jnp.float32)
+    full = lax.dot_general(window[...], spread[...], NT, preferred_element_type=jnp.float32)
     full = full.reshape(IRREPS * WB * WB, LO, COLS)
     lo_row = lax.broadcasted_iota(jnp.int32, (LO, COLS), 0)
     lo_col = lax.broadcasted_iota(jnp.int32, (LO, COLS), 1)
@@ -166,7 +157,7 @@
             grid=(IRREPS,),
             in_specs=[anywhere] * 8
             + [
-                pl.BlockSpec((1, COLS, HI * VB), lambda g, flip, place: (g ^ flip[0], 0, 0)),
+                pl.BlockSpec((PAIRS, 1, VB, VB), lambda g, flip, place: (0, g ^ flip[0], 0, 0)),
                 pl.BlockSpec((1, COLS), lambda g, flip, place: (0, 0)),
                 pl.BlockSpec((COLS, VB), lambda g, flip, place: (0, 0)),
                 pl.BlockSpec((2, COLS, VB), lambda g, flip, place: (0, 0, 0)),
@@ -178,11 +169,12 @@
             scratch_shapes=[
                 pltpu.VMEM((IRREPS, WB, VB, PB), jnp.bfloat16),
                 pltpu.VMEM((IRREPS * WB * WB * LO, HI * VB), jnp.bfloat16),
+                pltpu.VMEM((COLS, HI * VB), jnp.bfloat16),
                 pltpu.VMEM((IRREPS, WB * WB, COLS), jnp.float32),
                 pltpu.SemaphoreType.DMA((32,)),
             ],
         ),
-        compiler_params=pltpu.CompilerParams(vmem_limit_bytes=40 * 2**20),
+        compiler_params=pltpu.CompilerParams(vmem_limit_bytes=52 * 2**20),
         cost_estimate=pl.CostEstimate(flops=2 * 8 * 10**9, bytes_accessed=12 * 10**6, transcendentals=0),
     )(flip, place, *pieces, amp, sym, own_sel, mirror_sel)
 
@@ -192,21 +184,20 @@
     oj = lax.axis_index("oj")
     vert = lax.axis_index("vert")
     zh, core, zl, y = oj // 2, oj % 2, vert // 4, vert % 4
-    even = x % 2
 
     def permute(value, pairs):
         return lax.ppermute(value, AXES, pairs)
 
-    own = jnp.transpose(chol[0], (1, 2, 0))
-    quarters = [lax.dynamic_index_in_dim(own, 2 * even + (zl ^ rz), 0, False) for rz in range(2)]
+    mine = lax.dynamic_index_in_dim(chol[0], x, 1, False).T
+    pair = jnp.stack([mine, permute(mine, moved_pairs(next_row))])
+    near = jnp.concatenate([permute(pair, fetch_pairs(far)) for far in range(2)])
+    above, below = permute(near, moved_pairs(lower)), permute(near, moved_pairs(upper))
+    opposite = permute(jnp.where(core == 0, above, below), moved_pairs(apart))
     pieces, place = [], []
-    for rz in range(2):
-        near = jnp.stack([permute(quarters[rz], fetch_pairs(rz, ry)) for ry in range(4)])
-        far = permute(near, across_pairs())
-        pieces += [near, far, permute(near, swap_pairs()), permute(far, swap_pairs())]
-        first = core ^ rz ^ zl
-        place += [first, 2 * even + core, first, 2 * (1 - even) + core]
-        place += [1 - first, 2 * even + 1 - core, 1 - first, 2 * (1 - even) + 1 - core]
+    for hop, piece in ((0, near), (1, above), (3, below), (2, opposite)):
+        first, a = core ^ zl, (x + hop) % 4
+        pieces += [piece, permute(piece, moved_pairs(other_core))]
+        place += [first, a, 1 - first, a]
     place = jnp.stack(place).astype(jnp.int32)
 
     block = ((zh + y + 2 * zl) % 4) * 2 + zl
@@ -226,11 +217,10 @@
         [((lane == spot) & (row // 4 == (core ^ k))).astype(jnp.float32) for k in range(2)]
     )
 
-    amp = spread(amplitudes.reshape(PAIRS, IRREPS, VB, VB))
+    amp = amplitudes.reshape(PAIRS, IRREPS, VB, VB)
     mine, other = ladder(flip, place, pieces, amp, sym, own_sel, mirror_sel)
-    total = mine
-    for k in range(2):
-        total = total + lax.ppermute(other[k], ("oi", "oj"), mirror_pairs(k))
+    other = other[0] + permute(other[1], moved_pairs(other_core))
+    total = mine + permute(other, moved_pairs(mirrored))
     for bit in (4, 2, 1):
         pairs = [(v, v ^ bit) for v in range(IRREPS)]
         total = total[:bit] + lax.ppermute(total[bit:], "vert", pairs)

time: 109 us -> 99.8 us (0.916)
  starting transfers between devices: 46.7 us -> 31.9 us
  waiting for transfers between devices: 17.4 us -> 32 us
  local copies, waits for them, and re-layouts: 14.3 us -> 4.62 us
    ppermute x14 -> x12, waiting for transfers between devices: 5.14 us -> 24.8 us  [permute(): return lax.ppermute(value, AXES, pairs)]
    ppermute x2 -> x0, starting transfers between devices: 9.66 us -> none  [local(): total = total + lax.ppermute(other[k], ('oi', 'oj'), mirror_pairs(k))]
    unnamed x6 -> x5, local copies, waits for them, and re-layouts: 10 us -> 1.65 us
    ppermute x2 -> x0, waiting for transfers between devices: 5.42 us -> none  [local(): total = total + lax.ppermute(other[k], ('oi', 'oj'), mirror_pairs(k))]
    pallas_call x1, Pallas kernels: 26.3 us -> 29.3 us  [ladder(): pl.pallas_call(ladder_kernel, out_shape=[jax.ShapeDtypeStruct((IRREPS, WB...]
    pallas_call x1 -> x0, Pallas kernels: 2.92 us -> none  [spread(): pl.pallas_call(spread_kernel, out_shape=jax.ShapeDtypeStruct((IRREPS, COL...]
    ppermute x14 -> x12, starting transfers between devices: 26.9 us -> 24.1 us  [permute(): return lax.ppermute(value, AXES, pairs)]
    ppermute x3, starting transfers between devices: 10.2 us -> 7.78 us  [local(): total = total[:bit] + lax.ppermute(total[bit:], 'vert', pairs)]
  transfers between devices with their start and end apart: 19 -> 15, of which waited for: 7 -> 11; matrix products, arithmetic and copies ran while one was open for 2% -> 3% of each run, Pallas kernels for 3% -> 0%
where the time goes in v2:
time: 99.8 us; the launch traced here: 99.2 us
  waiting for transfers between devices  32 us (32%)
  starting transfers between devices  31.9 us (32%)
  Pallas kernels  29.3 us (29%)
  local copies, waits for them, and re-layouts  4.62 us (5%)
  other arithmetic  1.19 us (1%)
    pallas_call x1, Pallas kernels, ladder(): pl.pallas_call(ladder_kernel, out_shape=[jax.ShapeDtypeStruct((IRREPS, WB...  29.3 us
    ppermute x12, waiting for transfers between devices, permute(): return lax.ppermute(value, AXES, pairs)  24.8 us
    ppermute x12, starting transfers between devices, permute(): return lax.ppermute(value, AXES, pairs)  24.1 us
    ppermute x3, starting transfers between devices, local(): total = total[:bit] + lax.ppermute(total[bit:], 'vert', pairs)  7.78 us
    ppermute x3, waiting for transfers between devices, local(): total = total[:bit] + lax.ppermute(total[bit:], 'vert', pairs)  7.22 us
  transfers between devices with their start and end apart: 15, of which 11 were waited for; matrix products, arithmetic and copies ran while one was open for 3% of the time, Pallas kernels for 0%

profile of v2, /device:TPU:4, one launch (start us, length us, event | category | flops | bytes accessed | tf_op | source)
XLA Modules:
  0.0 99.2 jit_solution(15568798361880186220)
XLA Ops:
  0.0 0.0 copy-start
  0.0 0.9 copy-done
  1.0 0.1 constant_dynamic-slice_fusion
  1.1 0.1 copy.6
  1.2 1.7 %collective-permute-start = (bf16[128,256]{1,0:T(8,128)(2,1)S(1)}, bf16[128,256]{1,0:T(8,128)(2,1)S(1)}, u32[]{:S(2)}, u32[]{:S(2)}) collective-permute-start(bf16[128,256]{1,0:T(8,128)(2,1)S(1)} %bitcast.21), channel_id=1, source_target_pairs={{0,1},{1,0},{2,3},{3,2},{4,5},{5,4},{6,7},{7,6},{8,9},{9,8},{10,11... | collective-permute-start | bytes 196616 | tf_op jit(solution)/shard_map/ppermute | solution.py:189
  2.9 2.7 %collective-permute-done = bf16[128,256]{1,0:T(8,128)(2,1)S(1)} collective-permute-done((bf16[128,256]{1,0:T(8,128)(2,1)S(1)}, bf16[128,256]{1,0:T(8,128)(2,1)S(1)}, u32[]{:S(2)}, u32[]{:S(2)}) %collective-permute-start) | collective-permute-done | bytes 65568 | tf_op jit(solution)/shard_map/ppermute | solution.py:189
  5.6 0.7 collective-permute-start.1
  6.3 11.1 %collective-permute-start.2 = (bf16[2,128,256]{2,1,0:T(8,128)(2,1)S(1)}, bf16[2,128,256]{2,1,0:T(8,128)(2,1)S(1)}, u32[]{:S(2)}, u32[]{:S(2)}) collective-permute-start(bf16[2,128,256]{2,1,0:T(8,128)(2,1)S(1)} %pad_maximum_fusion), channel_id=1, source_target_pairs={{2,0},{19,1},{32,2},{49,3},{42,4},{59,5},{8,6},{25,7},{6,8},{23,9}... | collective-permute-start | bytes 393224 | tf_op jit(solution)/shard_map/ppermute | solution.py:189
  17.4 0.0 collective-permute-done.1
  17.5 4.1 %collective-permute-done.2 = bf16[2,128,256]{2,1,0:T(8,128)(2,1)S(1)} collective-permute-done((bf16[2,128,256]{2,1,0:T(8,128)(2,1)S(1)}, bf16[2,128,256]{2,1,0:T(8,128)(2,1)S(1)}, u32[]{:S(2)}, u32[]{:S(2)}) %collective-permute-start.2) | collective-permute-done | bytes 131104 | tf_op jit(solution)/shard_map/ppermute | solution.py:189
  21.6 1.3 %collective-permute-start.6 = (bf16[4,128,256]{2,1,0:T(8,128)(2,1)S(1)}, bf16[4,128,256]{2,1,0:T(8,128)(2,1)S(1)}, u32[]{:S(2)}, u32[]{:S(2)}) collective-permute-start(bf16[4,128,256]{2,1,0:T(8,128)(2,1)S(1)} %constant_dynamic-update-slice_fusion.refs_0_), channel_id=1, source_target_pairs={{0,64},{1,65},{2,66},{3,67},{4,68},{5,69},{6,70},{7,71},{8,72},{9,... | collective-permute-start | bytes 786440 | tf_op jit(solution)/shard_map/ppermute | solution.py:189
  22.9 0.8 collective-permute-start.4
  23.7 0.2 compare_and_fusion.1
  23.9 6.7 %collective-permute-done.6.refs_4_ = bf16[4,128,256]{2,1,0:T(8,128)(2,1)S(1)} collective-permute-done((bf16[4,128,256]{2,1,0:T(8,128)(2,1)S(1)}, bf16[4,128,256]{2,1,0:T(8,128)(2,1)S(1)}, u32[]{:S(2)}, u32[]{:S(2)}) %collective-permute-start.6) | collective-permute-done | bytes 262176 | tf_op jit(solution)/shard_map/ppermute | solution.py:189
  30.5 1.5 %collective-permute-done.4.refs_2_ = bf16[4,128,256]{2,1,0:T(8,128)(2,1)S(1)} collective-permute-done((bf16[4,128,256]{2,1,0:T(8,128)(2,1)S(1)}, bf16[4,128,256]{2,1,0:T(8,128)(2,1)S(1)}, u32[]{:S(2)}, u32[]{:S(2)}) %collective-permute-start.4) | collective-permute-done | bytes 262176 | tf_op jit(solution)/shard_map/ppermute | solution.py:189
  32.1 0.9 collective-permute-start.8
  33.0 0.7 add_convert_fusion.refs_11_
  33.7 0.7 dynamic_slice.12
  34.4 0.7 dynamic_slice.11
  35.1 0.1 broadcast_xor_fusion
  35.2 0.7 collective-permute-start.3
  35.9 0.1 collective-permute-start.7
  36.0 0.5 collective-permute-start.5
  36.4 2.1 %collective-permute-done.8.refs_6_ = bf16[4,128,256]{2,1,0:T(8,128)(2,1)S(1)} collective-permute-done((bf16[4,128,256]{2,1,0:T(8,128)(2,1)S(1)}, bf16[4,128,256]{2,1,0:T(8,128)(2,1)S(1)}, u32[]{:S(2)}, u32[]{:S(2)}) %collective-permute-start.8) | collective-permute-done | bytes 262176 | tf_op jit(solution)/shard_map/ppermute | solution.py:189
  38.5 0.0 collective-permute-start.9
  38.5 0.1 xor.37
  38.6 0.1 broadcast_in_dim.18
  38.7 0.1 broadcast_in_dim.19.refs_9_
  38.8 0.1 stack.53.place_ref
  38.9 0.1 compare_convert_fusion.refs_10_
  39.0 0.0 collective-permute-done.3.refs_1_
  39.0 0.0 collective-permute-done.7.refs_5_
  39.0 0.0 collective-permute-done.5.refs_3_
  39.0 1.0 %collective-permute-done.9.refs_7_ = bf16[4,128,256]{2,1,0:T(8,128)(2,1)S(1)} collective-permute-done((bf16[4,128,256]{2,1,0:T(8,128)(2,1)S(1)}, bf16[4,128,256]{2,1,0:T(8,128)(2,1)S(1)}, u32[]{:S(2)}, u32[]{:S(2)}) %collective-permute-start.9) | collective-permute-done | bytes 262176 | tf_op jit(solution)/shard_map/ppermute | solution.py:189
  40.0 0.7 copy-done.1
  40.7 29.3 %shard_map.37 = (f32[8,4,128]{2,1,0:T(4,128)S(1)}, f32[2,8,4,128]{3,2,1,0:T(4,128)S(1)}) custom-call(s32[1]{0:T(128)} %bitcast.flip_ref, s32[16]{0:T(128)S(1)} %stack.53.place_ref, bf16[4,128,256]{2,1,0:T(8,128)(2,1)S(1)} %constant_dynamic-update-slice_fusion.refs_0_, bf16[4,128,256]{2,1,0:T(8,128)(2,1)S(1)} %collective-permute-done.3.refs_1_, ...), custom_call_target="tpu_custom_call" | custom-call | flops 16000000000 | bytes 12000000 | tf_op jit(solution)/shard_map/pallas_call | solution.py:149
  70.0 0.2 collective-permute-start.10
  70.3 1.0 %collective-permute-done.10 = f32[8,4,128]{2,1,0:T(4,128)S(1)} collective-permute-done((f32[8,4,128]{2,1,0:T(4,128)S(1)}, f32[8,4,128]{2,1,0:T(4,128)S(1)}, u32[]{:S(2)}, u32[]{:S(2)}) %collective-permute-start.10) | collective-permute-done | bytes 16416 | tf_op jit(solution)/shard_map/ppermute | solution.py:189
  71.3 6.2 %collective-permute-start.11 = (f32[8,4,128]{2,1,0:T(4,128)S(1)}, f32[8,4,128]{2,1,0:T(4,128)S(1)}, u32[]{:S(2)}, u32[]{:S(2)}) collective-permute-start(f32[8,4,128]{2,1,0:T(4,128)S(1)} %bitcast_add_fusion), channel_id=1, source_target_pairs={{0,0},{1,1},{2,2},{3,3},{4,4},{5,5},{6,6},{7,7},{8,8},{9,9},{10,10... | collective-permute-start | bytes 49160 | tf_op jit(solution)/shard_map/ppermute | solution.py:189
  77.5 5.8 %collective-permute-done.11 = f32[8,4,128]{2,1,0:T(4,128)S(1)} collective-permute-done((f32[8,4,128]{2,1,0:T(4,128)S(1)}, f32[8,4,128]{2,1,0:T(4,128)S(1)}, u32[]{:S(2)}, u32[]{:S(2)}) %collective-permute-start.11) | collective-permute-done | bytes 16416 | tf_op jit(solution)/shard_map/ppermute | solution.py:189
  83.3 1.7 %collective-permute-start.12 = (f32[4,4,128]{2,1,0:T(4,128)S(1)}, f32[4,4,128]{2,1,0:T(4,128)S(1)}, u32[]{:S(2)}, u32[]{:S(2)}) collective-permute-start(f32[4,4,128]{2,1,0:T(4,128)S(1)} %slice.33), channel_id=1, source_target_pairs={{0,4},{1,5},{2,6},{3,7},{4,0},{5,1},{6,2},{7,3},{8,12},{9,13},{10,... | collective-permute-start | bytes 24584 | tf_op jit(solution)/shard_map/ppermute | solution.py:226
  84.9 2.1 %collective-permute-done.12 = f32[4,4,128]{2,1,0:T(4,128)S(1)} collective-permute-done((f32[4,4,128]{2,1,0:T(4,128)S(1)}, f32[4,4,128]{2,1,0:T(4,128)S(1)}, u32[]{:S(2)}, u32[]{:S(2)}) %collective-permute-start.12) | collective-permute-done | bytes 8224 | tf_op jit(solution)/shard_map/ppermute | solution.py:226
  87.0 6.1 %collective-permute-start.13 = (f32[2,4,128]{2,1,0:T(4,128)S(1)}, f32[2,4,128]{2,1,0:T(4,128)S(1)}, u32[]{:S(2)}, u32[]{:S(2)}) collective-permute-start(f32[2,4,128]{2,1,0:T(4,128)S(1)} %slice.35), channel_id=1, source_target_pairs={{0,2},{1,3},{2,0},{3,1},{4,6},{5,7},{6,4},{7,5},{8,10},{9,11},{10,... | collective-permute-start | bytes 12296 | tf_op jit(solution)/shard_map/ppermute | solution.py:226
  93.1 1.6 %collective-permute-done.13 = f32[2,4,128]{2,1,0:T(4,128)S(1)} collective-permute-done((f32[2,4,128]{2,1,0:T(4,128)S(1)}, f32[2,4,128]{2,1,0:T(4,128)S(1)}, u32[]{:S(2)}, u32[]{:S(2)}) %collective-permute-start.13) | collective-permute-done | bytes 4128 | tf_op jit(solution)/shard_map/ppermute | solution.py:226
  94.7 0.0 collective-permute-start.14
  94.7 3.6 %collective-permute-done.14 = f32[1,4,128]{2,1,0:T(4,128)S(1)} collective-permute-done((f32[1,4,128]{2,1,0:T(4,128)S(1)}, f32[1,4,128]{2,1,0:T(4,128)S(1)}, u32[]{:S(2)}, u32[]{:S(2)}) %collective-permute-start.14) | collective-permute-done | bytes 2080 | tf_op jit(solution)/shard_map/ppermute | solution.py:226
  98.3 0.1 reshape.330
  98.4 0.8 copy.7
  (19 shorter events, 0.2 us)
Async XLA Ops:
  0.0 1.0 copy-start
  1.2 4.4 %collective-permute-start = (bf16[128,256]{1,0:T(8,128)(2,1)S(1)}, bf16[128,256]{1,0:T(8,128)(2,1)S(1)}, u32[]{:S(2)}, u32[]{:S(2)}) collective-permute-start(bf16[128,256]{1,0:T(8,128)(2,1)S(1)} %bitcast.21), channel_id=1, source_target_pairs={{0,1},{1,0},{2,3},{3,2},{4,5},{5,4},{6,7},{7,6},{8,9},{9,8},{10,11... | collective-permute-start | bytes 196616 | tf_op jit(solution)/shard_map/ppermute | solution.py:189
  5.6 11.9 %collective-permute-start.1 = (bf16[2,128,256]{2,1,0:T(8,128)(2,1)S(1)}, bf16[2,128,256]{2,1,0:T(8,128)(2,1)S(1)}, u32[]{:S(2)}, u32[]{:S(2)}) collective-permute-start(bf16[2,128,256]{2,1,0:T(8,128)(2,1)S(1)} %pad_maximum_fusion), channel_id=1, source_target_pairs={{0,0},{17,1},{34,2},{51,3},{40,4},{57,5},{10,6},{27,7},{4,8},{21,9... | collective-permute-start | bytes 393224 | tf_op jit(solution)/shard_map/ppermute | solution.py:189
  6.3 15.3 %collective-permute-start.2 = (bf16[2,128,256]{2,1,0:T(8,128)(2,1)S(1)}, bf16[2,128,256]{2,1,0:T(8,128)(2,1)S(1)}, u32[]{:S(2)}, u32[]{:S(2)}) collective-permute-start(bf16[2,128,256]{2,1,0:T(8,128)(2,1)S(1)} %pad_maximum_fusion), channel_id=1, source_target_pairs={{2,0},{19,1},{32,2},{49,3},{42,4},{59,5},{8,6},{25,7},{6,8},{23,9}... | collective-permute-start | bytes 393224 | tf_op jit(solution)/shard_map/ppermute | solution.py:189
  21.6 9.0 %collective-permute-start.6 = (bf16[4,128,256]{2,1,0:T(8,128)(2,1)S(1)}, bf16[4,128,256]{2,1,0:T(8,128)(2,1)S(1)}, u32[]{:S(2)}, u32[]{:S(2)}) collective-permute-start(bf16[4,128,256]{2,1,0:T(8,128)(2,1)S(1)} %constant_dynamic-update-slice_fusion.refs_0_), channel_id=1, source_target_pairs={{0,64},{1,65},{2,66},{3,67},{4,68},{5,69},{6,70},{7,71},{8,72},{9,... | collective-permute-start | bytes 786440 | tf_op jit(solution)/shard_map/ppermute | solution.py:189
  22.9 9.2 %collective-permute-start.4 = (bf16[4,128,256]{2,1,0:T(8,128)(2,1)S(1)}, bf16[4,128,256]{2,1,0:T(8,128)(2,1)S(1)}, u32[]{:S(2)}, u32[]{:S(2)}) collective-permute-start(bf16[4,128,256]{2,1,0:T(8,128)(2,1)S(1)} %constant_dynamic-update-slice_fusion.refs_0_), channel_id=1, source_target_pairs={{0,192},{1,193},{2,194},{3,195},{4,196},{5,197},{6,198},{7,199},{8... | collective-permute-start | bytes 786440 | tf_op jit(solution)/shard_map/ppermute | solution.py:189
  32.1 6.4 %collective-permute-start.8 = (bf16[4,128,256]{2,1,0:T(8,128)(2,1)S(1)}, bf16[4,128,256]{2,1,0:T(8,128)(2,1)S(1)}, u32[]{:S(2)}, u32[]{:S(2)}) collective-permute-start(bf16[4,128,256]{2,1,0:T(8,128)(2,1)S(1)} %broadcast_select_fusion), channel_id=1, source_target_pairs={{0,192},{1,193},{2,194},{3,195},{4,196},{5,197},{6,198},{7,199},{8... | collective-permute-start | bytes 786440 | tf_op jit(solution)/shard_map/ppermute | solution.py:189
  35.2 3.8 %collective-permute-start.3 = (bf16[4,128,256]{2,1,0:T(8,128)(2,1)S(1)}, bf16[4,128,256]{2,1,0:T(8,128)(2,1)S(1)}, u32[]{:S(2)}, u32[]{:S(2)}) collective-permute-start(bf16[4,128,256]{2,1,0:T(8,128)(2,1)S(1)} %constant_dynamic-update-slice_fusion.refs_0_), channel_id=1, source_target_pairs={{0,8},{1,9},{2,10},{3,11},{4,12},{5,13},{6,14},{7,15},{8,0},{9,1},... | collective-permute-start | bytes 786440 | tf_op jit(solution)/shard_map/ppermute | solution.py:189
  35.9 3.1 %collective-permute-start.7 = (bf16[4,128,256]{2,1,0:T(8,128)(2,1)S(1)}, bf16[4,128,256]{2,1,0:T(8,128)(2,1)S(1)}, u32[]{:S(2)}, u32[]{:S(2)}) collective-permute-start(bf16[4,128,256]{2,1,0:T(8,128)(2,1)S(1)} %collective-permute-done.6.refs_4_), channel_id=1, source_target_pairs={{0,8},{1,9},{2,10},{3,11},{4,12},{5,13},{6,14},{7,15},{8,0},{9,1},... | collective-permute-start | bytes 786440 | tf_op jit(solution)/shard_map/ppermute | solution.py:189
  36.0 3.1 %collective-permute-start.5 = (bf16[4,128,256]{2,1,0:T(8,128)(2,1)S(1)}, bf16[4,128,256]{2,1,0:T(8,128)(2,1)S(1)}, u32[]{:S(2)}, u32[]{:S(2)}) collective-permute-start(bf16[4,128,256]{2,1,0:T(8,128)(2,1)S(1)} %collective-permute-done.4.refs_2_), channel_id=1, source_target_pairs={{0,8},{1,9},{2,10},{3,11},{4,12},{5,13},{6,14},{7,15},{8,0},{9,1},... | collective-permute-start | bytes 786440 | tf_op jit(solution)/shard_map/ppermute | solution.py:189
  38.5 1.5 %collective-permute-start.9 = (bf16[4,128,256]{2,1,0:T(8,128)(2,1)S(1)}, bf16[4,128,256]{2,1,0:T(8,128)(2,1)S(1)}, u32[]{:S(2)}, u32[]{:S(2)}) collective-permute-start(bf16[4,128,256]{2,1,0:T(8,128)(2,1)S(1)} %collective-permute-done.8.refs_6_), channel_id=1, source_target_pairs={{0,8},{1,9},{2,10},{3,11},{4,12},{5,13},{6,14},{7,15},{8,0},{9,1},... | collective-permute-start | bytes 786440 | tf_op jit(solution)/shard_map/ppermute | solution.py:189
  40.0 0.7 copy-start.1
  70.0 1.3 %collective-permute-start.10 = (f32[8,4,128]{2,1,0:T(4,128)S(1)}, f32[8,4,128]{2,1,0:T(4,128)S(1)}, u32[]{:S(2)}, u32[]{:S(2)}) collective-permute-start(f32[8,4,128]{2,1,0:T(4,128)S(1)} %slice_bitcast_fusion), channel_id=1, source_target_pairs={{0,8},{1,9},{2,10},{3,11},{4,12},{5,13},{6,14},{7,15},{8,0},{9,1},... | collective-permute-start | bytes 49160 | tf_op jit(solution)/shard_map/ppermute | solution.py:189
  71.3 11.9 %collective-permute-start.11 = (f32[8,4,128]{2,1,0:T(4,128)S(1)}, f32[8,4,128]{2,1,0:T(4,128)S(1)}, u32[]{:S(2)}, u32[]{:S(2)}) collective-permute-start(f32[8,4,128]{2,1,0:T(4,128)S(1)} %bitcast_add_fusion), channel_id=1, source_target_pairs={{0,0},{1,1},{2,2},{3,3},{4,4},{5,5},{6,6},{7,7},{8,8},{9,9},{10,10... | collective-permute-start | bytes 49160 | tf_op jit(solution)/shard_map/ppermute | solution.py:189
  83.3 3.7 %collective-permute-start.12 = (f32[4,4,128]{2,1,0:T(4,128)S(1)}, f32[4,4,128]{2,1,0:T(4,128)S(1)}, u32[]{:S(2)}, u32[]{:S(2)}) collective-permute-start(f32[4,4,128]{2,1,0:T(4,128)S(1)} %slice.33), channel_id=1, source_target_pairs={{0,4},{1,5},{2,6},{3,7},{4,0},{5,1},{6,2},{7,3},{8,12},{9,13},{10,... | collective-permute-start | bytes 24584 | tf_op jit(solution)/shard_map/ppermute | solution.py:226
  87.0 7.7 %collective-permute-start.13 = (f32[2,4,128]{2,1,0:T(4,128)S(1)}, f32[2,4,128]{2,1,0:T(4,128)S(1)}, u32[]{:S(2)}, u32[]{:S(2)}) collective-permute-start(f32[2,4,128]{2,1,0:T(4,128)S(1)} %slice.35), channel_id=1, source_target_pairs={{0,2},{1,3},{2,0},{3,1},{4,6},{5,7},{6,4},{7,5},{8,10},{9,11},{10,... | collective-permute-start | bytes 12296 | tf_op jit(solution)/shard_map/ppermute | solution.py:226
  94.7 3.6 %collective-permute-start.14 = (f32[1,4,128]{2,1,0:T(4,128)S(1)}, f32[1,4,128]{2,1,0:T(4,128)S(1)}, u32[]{:S(2)}, u32[]{:S(2)}) collective-permute-start(f32[1,4,128]{2,1,0:T(4,128)S(1)} %slice.37), channel_id=1, source_target_pairs={{0,1},{1,0},{2,3},{3,2},{4,5},{5,4},{6,7},{7,6},{8,9},{9,8},{10,11... | collective-permute-start | bytes 6152 | tf_op jit(solution)/shard_map/ppermute | solution.py:226

commit v3 on v0

v3 whole, which is shorter than its diff:
```python
import jax
import jax.numpy as jnp
from jax import lax
from jax.experimental import pallas as pl
from jax.experimental.pallas import tpu as pltpu
from jax.sharding import PartitionSpec as P

IRREPS = 8
VB = 128
PB = 256
WB = 4
LO = 8
HI = VB // LO
PAIRS = 32
HOPS = (0, 1, 3, 2)
COLS = PAIRS * LO
AXES = ("oi", "oj", "vert")
CHIPS = [
    (x, zh, core, zl, y)
    for x in range(4)
    for zh in range(4)
    for core in range(2)
    for zl in range(2)
    for y in range(4)
]
NT = (((1,), (1,)), ((), ()))


def flat_index(x, zh, core, zl, y):
    return x * 64 + (zh * 2 + core) * 8 + zl * 4 + y


def fetch_pairs(row):
    pairs = []
    for x, zh, core, zl, y in CHIPS:
        source = (x, (zh + y + 2 * zl) % 4, zl, core, y ^ row)
        pairs.append((flat_index(*source), flat_index(x, zh, core, zl, y)))
    return pairs


def moved_pairs(move):
    return [(flat_index(*d), flat_index(*move(*d))) for d in CHIPS]


def lower(x, zh, core, zl, y):
    return ((x + 3) % 4, zh, core, zl, y)


def upper(x, zh, core, zl, y):
    return ((x + 1) % 4, zh, core, zl, y)


def apart(x, zh, core, zl, y):
    return ((x + (1 if core else 3)) % 4, zh, core, zl, y)


def other_core(x, zh, core, zl, y):
    return (x, zh, 1 - core, zl, y)


def mirrored(x, zh, core, zl, y):
    return (zh, x, core, zl, y)


def exact_pick(values, chosen):
    top = values.astype(jnp.bfloat16)
    rest = values - top.astype(jnp.float32)
    middle = rest.astype(jnp.bfloat16)
    low = (rest - middle.astype(jnp.float32)).astype(jnp.bfloat16)
    rows = values.shape[0]
    parts = jnp.dot(
        jnp.concatenate([top, middle, low], 0), chosen, preferred_element_type=jnp.float32
    )
    return parts[:rows] + (parts[rows : 2 * rows] + parts[2 * rows :])


def place_of():
    x, oj, vert = lax.axis_index("oi"), lax.axis_index("oj"), lax.axis_index("vert")
    zh, core, zl, y = oj // 2, lax.rem(oj, 2), vert // 4, lax.rem(vert, 4)
    block = lax.rem(zh + y + 2 * zl, 4) * 2 + zl
    return x, oj, vert, core, jnp.bitwise_xor(block, vert), jnp.bitwise_xor(core, zl)


def load_pieces(pieces, chol, sems, first):
    copies = []
    for at, piece in enumerate(pieces):
        half = first if at % 2 == 0 else 1 - first
        target = chol.at[pl.ds(half * 4, 4), at // 2]
        copies.append(pltpu.make_async_copy(piece, target, sems.at[at]))
    return copies


def pair_labels(occ, x, oj):
    pair = lax.broadcasted_iota(jnp.int32, (1, COLS), 1) // LO
    sym = jnp.zeros((1, COLS), jnp.int32)
    for row in range(8):
        for col in range(4):
            label = jnp.bitwise_xor(occ[x * 8 + row], occ[oj * 4 + col])
            sym = jnp.where(pair == row * 4 + col, label, sym)
    lo_row = lax.broadcasted_iota(jnp.int32, (LO, COLS), 0)
    lo_col = lax.broadcasted_iota(jnp.int32, (LO, COLS), 1) % LO
    return jnp.where(lo_row == lo_col, sym, -1)


def store_block(window, base, block, row):
    for hi in range(HI):
        at = row + hi * LO
        window[base : base + 2 * LO, hi * VB : (hi + 1) * VB] = jnp.concatenate(
            [block[at : at + LO, :VB], block[at : at + LO, VB:]], 0
        ).astype(jnp.bfloat16)


def spread_out(amp, spread):
    wide = amp.astype(jnp.float32).reshape(PAIRS, HI, LO, VB)
    for hi in range(HI):
        spread[:, hi * VB : (hi + 1) * VB] = wide[:, hi].reshape(COLS, VB).astype(jnp.bfloat16)


def collect(full, sym, ga, where, straight, turned):
    totals = {}
    for at, (gb, a, b) in enumerate(where):
        wanted = sym == jnp.bitwise_xor(ga, gb)
        slot = WB * a + b
        totals[slot] = jnp.where(wanted, full[at], totals.get(slot, 0.0))
        turned[gb, slot] = jnp.where(wanted, full[at], turned[gb, slot])
    for slot, total in totals.items():
        straight[ga, slot] = total


def finish(slots, straight, turned, own_ref, mirror_ref, x, core, vert):
    count = len(slots)
    actual = [lax.rem(x + hop, WB) for hop in HOPS]
    source = lax.broadcasted_iota(jnp.int32, (COLS, VB), 0) // LO
    lane = lax.broadcasted_iota(jnp.int32, (COLS, VB), 1) % PAIRS
    group = lax.broadcasted_iota(jnp.int32, (IRREPS, VB), 1) // PAIRS

    def summed(values):
        rows = [jnp.sum(values[:, WB * a + b], axis=1) for a, b in slots]
        return jnp.concatenate(rows, 0)

    def split(values, chosen, by_first):
        picked = exact_pick(values, chosen)
        lines = {}
        for at, (a, b) in enumerate(slots):
            line, wide = (a, b) if by_first else (b, a)
            part = jnp.where(group == actual[wide], picked[at * IRREPS : (at + 1) * IRREPS], 0.0)
            lines[line] = lines.get(line, 0.0) + part
        return lines

    own = split(summed(straight), (source == lane).astype(jnp.bfloat16), True)
    for line, value in own.items():
        for ga in range(IRREPS):
            there = (jnp.bitwise_xor(vert, ga), pl.ds(actual[line], 1))
            own_ref[there] = own_ref[there] + value[ga : ga + 1]
    every = summed(turned)
    target = core * 16 + (source % 4) * 4 + (source // 4) % 4
    for k in range(2):
        here = (source // 16) == jnp.bitwise_xor(core, k)
        other = split(every, ((lane == target) & here).astype(jnp.bfloat16), False)
        for line, value in other.items():
            for ga in range(IRREPS):
                there = (k, jnp.bitwise_xor(vert, ga), pl.ds(actual[line], 1))
                mirror_ref[there] = mirror_ref[there] + value[ga : ga + 1]


def amp_copy(amp_ref, amp, sems, flip, ga):
    return pltpu.make_async_copy(
        amp_ref.at[:, jnp.bitwise_xor(ga, flip)], amp.at[ga], sems.at[ga]
    )


def begin(occ_ref, amp_ref, pieces, chol, amp, occ, sems, flip, first):
    chol_sem, amp_sem, occ_sem = sems
    occ_copy = pltpu.make_async_copy(occ_ref, occ, occ_sem)
    occ_copy.start()
    amp_copy(amp_ref, amp, amp_sem, flip, 0).start()
    copies = load_pieces(pieces, chol, chol_sem, first)
    for copy in copies:
        copy.start()
    occ_copy.wait()
    for copy in copies:
        copy.wait()
    for ga in range(1, IRREPS):
        amp_copy(amp_ref, amp, amp_sem, flip, ga).start()


def early_kernel(occ_ref, amp_ref, *refs):
    pieces, (own_ref, mirror_ref) = refs[:6], refs[6:8]
    chol, amp, window, spread, straight, turned, occ, *sems = refs[8:]
    x, oj, vert, core, flip, first = place_of()
    begin(occ_ref, amp_ref, pieces, chol, amp, occ, sems, flip, first)
    sym = pair_labels(occ, x, oj)
    where = []
    for tile in range(12):
        for a in range(3):
            for at in (2 * tile, 2 * tile + 1):
                where.append((at // 3, a, at % 3))
    slots = [(a, b) for a in range(3) for b in range(3)]
    for a, b in slots:
        turned[:, WB * a + b] = jnp.zeros((IRREPS, LO, COLS), jnp.float32)
    own_ref[...] = jnp.zeros_like(own_ref)
    mirror_ref[...] = jnp.zeros_like(mirror_ref)

    def one_irrep(ga, carry):
        amp_copy(amp_ref, amp, sems[1], flip, ga).wait()
        spread_out(amp[ga], spread)
        left = chol[ga].reshape(3 * VB, PB)
        for tile in range(12):
            two = [chol[at // 3, at % 3] for at in (2 * tile, 2 * tile + 1)]
            block = lax.dot_general(
                left, jnp.concatenate(two, 0), NT, preferred_element_type=jnp.float32
            )
            for a in range(3):
                store_block(window, (tile * 3 + a) * 2 * LO, block, a * VB)
        full = []
        for start, stop in ((0, 32), (32, 72)):
            rows = window[start * LO : stop * LO]
            part = lax.dot_general(rows, spread[...], NT, preferred_element_type=jnp.float32)
            full.append(part.reshape(stop - start, LO, COLS))
        collect(jnp.concatenate(full, 0), sym, ga, where, straight, turned)
        return carry

    lax.fori_loop(0, IRREPS, one_irrep, 0)
    finish(slots, straight, turned, own_ref, mirror_ref, x, core, vert)


def late_kernel(occ_ref, amp_ref, own_in, mirror_in, *refs):
    pieces, (own_ref, mirror_ref) = refs[:8], refs[8:10]
    chol, amp, window, spread, straight, turned, occ, *sems = refs[10:]
    x, oj, vert, core, flip, first = place_of()
    begin(occ_ref, amp_ref, pieces, chol, amp, occ, sems, flip, first)
    sym = pair_labels(occ, x, oj)
    where = []
    for tile in range(4):
        for a in range(4):
            where += [(2 * tile, a, 3), (2 * tile + 1, a, 3)]
    for at in range(24):
        where.append((at // 3, 3, at % 3))
    slots = [(a, 3) for a in range(4)] + [(3, b) for b in range(3)]
    for a, b in slots:
        turned[:, WB * a + b] = jnp.zeros((IRREPS, LO, COLS), jnp.float32)
    own_ref[...] = own_in[...]
    mirror_ref[...] = mirror_in[...]

    def one_irrep(ga, carry):
        amp_copy(amp_ref, amp, sems[1], flip, ga).wait()
        spread_out(amp[ga], spread)
        left = chol[ga].reshape(WB * VB, PB)
        for tile in range(4):
            two = [chol[2 * tile, 3], chol[2 * tile + 1, 3]]
            block = lax.dot_general(
                left, jnp.concatenate(two, 0), NT, preferred_element_type=jnp.float32
            )
            for a in range(WB):
                store_block(window, (tile * WB + a) * 2 * LO, block, a * VB)
        for tile in range(12):
            two = [chol[at // 3, at % 3] for at in (2 * tile, 2 * tile + 1)]
            block = lax.dot_general(
                chol[ga, 3], jnp.concatenate(two, 0), NT, preferred_element_type=jnp.float32
            )
            store_block(window, (16 + tile) * 2 * LO, block, 0)
        for start, stop in ((0, 32), (32, 56)):
            rows = window[start * LO : stop * LO]
            part = lax.dot_general(rows, spread[...], NT, preferred_element_type=jnp.float32)
            part = part.reshape(stop - start, LO, COLS)
            collect(part, sym, ga, where[start:stop], straight, turned)
        return carry

    lax.fori_loop(0, IRREPS, one_irrep, 0)
    finish(slots, straight, turned, own_ref, mirror_ref, x, core, vert)


def ladder(kernel, slots, window, before, pieces):
    anywhere = pl.BlockSpec(memory_space=pl.ANY)
    whole = pl.BlockSpec(memory_space=pltpu.VMEM)
    occ, amp, *earlier = before
    return pl.pallas_call(
        kernel,
        out_shape=[
            jax.ShapeDtypeStruct((IRREPS, WB, VB), jnp.float32),
            jax.ShapeDtypeStruct((2, IRREPS, WB, VB), jnp.float32),
        ],
        in_specs=[anywhere] * 2 + [whole] * len(earlier) + [anywhere] * len(pieces),
        out_specs=[whole] * 2,
        scratch_shapes=[
            pltpu.VMEM((IRREPS, slots, VB, PB), jnp.bfloat16),
            pltpu.VMEM((IRREPS, PAIRS, VB, VB), jnp.bfloat16),
            pltpu.VMEM(window + (HI * VB,), jnp.bfloat16),
            pltpu.VMEM((COLS, HI * VB), jnp.bfloat16),
            pltpu.VMEM((IRREPS, WB * WB, LO, COLS), jnp.float32),
            pltpu.VMEM((IRREPS, WB * WB, LO, COLS), jnp.float32),
            pltpu.SMEM((PAIRS,), jnp.int32),
            pltpu.SemaphoreType.DMA((8,)),
            pltpu.SemaphoreType.DMA((8,)),
            pltpu.SemaphoreType.DMA,
        ],
        compiler_params=pltpu.CompilerParams(vmem_limit_bytes=50 * 2**20),
        cost_estimate=pl.CostEstimate(
            flops=8 * 10**9, bytes_accessed=12 * 10**6, transcendentals=0
        ),
    )(*before, *pieces)


def local(amplitudes, chol, occ_irrep):
    x = lax.axis_index("oi")
    core = lax.rem(lax.axis_index("oj"), 2)

    def permute(value, pairs):
        return lax.ppermute(value, AXES, pairs)

    mine = lax.dynamic_index_in_dim(chol[0], x, 1, False).T
    near = jnp.stack([permute(mine, fetch_pairs(row)) for row in range(4)])
    above, below = permute(near, moved_pairs(lower)), permute(near, moved_pairs(upper))
    pieces = []
    for piece in (near, above, below):
        pieces += [piece, permute(piece, moved_pairs(other_core))]
    beyond = jnp.where(core == 0, jnp.stack(pieces[2:4]), jnp.stack(pieces[4:6]))
    beyond = permute(beyond, moved_pairs(apart))
    occ_rows, occ_cols = amplitudes.shape[0], amplitudes.shape[1]
    amp = amplitudes.reshape(PAIRS, IRREPS, VB, VB)
    before = (occ_irrep, amp)
    mine, other = ladder(early_kernel, 3, (72 * LO,), before, pieces)
    before += (mine, other)
    pieces += [beyond[0], beyond[1]]
    mine, other = ladder(late_kernel, 4, (56 * LO,), before, pieces)
    other = other[0] + permute(other[1], moved_pairs(other_core))
    total = mine + permute(other, moved_pairs(mirrored))
    total = jnp.sum(lax.all_to_all(total, "vert", 0, 0), axis=0)
    total = total.reshape(WB, WB, occ_rows, occ_cols)
    return jnp.transpose(total, (2, 3, 0, 1))[:, :, None]


def solution(mesh):
    return jax.shard_map(
        local,
        mesh=mesh,
        in_specs=(P("oi", "oj", None, None, None), P(("oj", "vert"), None, None, None), P()),
        out_specs=P("oi", "oj", "vert", None, None),
        check_vma=False,
    )
```

time: 584 us -> 89.4 us (0.15); the launches traced: 575 us -> 89.2 us
  matrix products: 209 us -> 0 us
  waiting for transfers between devices: 193 us -> 19 us
  local copies, waits for them, and re-layouts: 106 us -> 2.79 us
  Pallas kernels: 0 us -> 28.1 us
  blocking collectives: 41 us -> 13.1 us
  starting transfers between devices: 9.91 us -> 25.9 us
  between operations: 14.1 us -> 0.1 us
    dot_general x16 -> x0, matrix products: 209 us -> none  [the longest x8 182 us: ladder_terms(): jnp.einsum('ijlpad,gpbd->ijlgab', half_step, blocks, preferred_element_ty...]
    all_gather x1 -> x0, waiting for transfers between devices: 185 us -> none  [local(): window = lax.all_gather(chol, ('oj', 'vert'), axis=0, tiled=True)]
    unnamed x58 -> x4, local copies, waits for them, and re-layouts: 54.7 us -> 1.61 us
    all_gather x2 -> x0, blocking collectives: 41 us -> none  [the longest x1 28.4 us: local(): all_irreps = lax.all_gather(ladder, 'vert', axis=2, tiled=True)]
    dynamic_slice x15 -> x2, local copies, waits for them, and re-layouts: 28.9 us -> 0.25 us  [local(): mine = lax.dynamic_index_in_dim(chol[0], x, 1, False).T]
    pallas_call x0 -> x2, Pallas kernels: none -> 28.1 us  [ladder(): pl.pallas_call(kernel, out_shape=[jax.ShapeDtypeStruct((IRREPS, WB, VB),...]
    ppermute x0 -> x12, starting transfers between devices: none -> 25.9 us  [permute(): return lax.ppermute(value, AXES, pairs)]
    ppermute x0 -> x12, waiting for transfers between devices: none -> 19 us  [permute(): return lax.ppermute(value, AXES, pairs)]
  transfers between devices with their start and end apart: 2 -> 12, of which waited for: 2 -> 8; matrix products, arithmetic and copies ran while one was open for 4% -> 0% of each run, Pallas kernels for 0% -> 15%
where the time goes in v3:
time: 89.4 us; the launch traced here: 89.2 us
  Pallas kernels  28.1 us (31%)
  starting transfers between devices  25.9 us (29%)
  waiting for transfers between devices  19 us (21%)
  blocking collectives  13.1 us (15%)
  local copies, waits for them, and re-layouts  2.79 us (3%)
    pallas_call x2, Pallas kernels, ladder(): pl.pallas_call(kernel, out_shape=[jax.ShapeDtypeStruct((IRREPS, WB, VB),...  28.1 us
    ppermute x12, starting transfers between devices, permute(): return lax.ppermute(value, AXES, pairs)  25.9 us
    ppermute x12, waiting for transfers between devices, permute(): return lax.ppermute(value, AXES, pairs)  19 us
    all_to_all x1, blocking collectives, local(): total = jnp.sum(lax.all_to_all(total, 'vert', 0, 0), axis=0)  13.1 us
  transfers between devices with their start and end apart: 12, of which 8 were waited for; matrix products, arithmetic and copies ran while one was open for 0% of the time, Pallas kernels for 15%

profile of v3, /device:TPU:4, one launch (start us, length us, event | category | flops | bytes accessed | tf_op | source)
XLA Modules:
  0.0 89.2 jit_solution(1636709818747765503)
XLA Ops:
  0.0 0.0 copy-start
  0.0 0.9 %copy-done = bf16[1,256,4,128]{3,2,1,0:T(4,128)(2,1)S(1)} copy-done((bf16[1,256,4,128]{3,2,1,0:T(4,128)(2,1)S(1)}, bf16[1,256,4,128]{3,2,1,0:T(4,128)(2,1)}, u32[]{:S(2)}) %copy-start) | copy-done | bytes 262168
  1.0 0.1 constant_dynamic-slice_fusion
  1.1 0.1 copy.5
  1.2 0.7 collective-permute-start
  1.9 10.1 %collective-permute-start.1 = (bf16[128,256]{1,0:T(8,128)(2,1)S(1)}, bf16[128,256]{1,0:T(8,128)(2,1)S(1)}, u32[]{:S(2)}, u32[]{:S(2)}) collective-permute-start(bf16[128,256]{1,0:T(8,128)(2,1)S(1)} %bitcast.29), channel_id=1, source_target_pairs={{1,0},{16,1},{35,2},{50,3},{41,4},{56,5},{11,6},{26,7},{5,8},{20,9... | collective-permute-start | bytes 196616 | tf_op jit(solution)/shard_map/ppermute | solution.py:309
  12.0 3.3 %collective-permute-start.2 = (bf16[128,256]{1,0:T(8,128)(2,1)S(1)}, bf16[128,256]{1,0:T(8,128)(2,1)S(1)}, u32[]{:S(2)}, u32[]{:S(2)}) collective-permute-start(bf16[128,256]{1,0:T(8,128)(2,1)S(1)} %bitcast.30), channel_id=1, source_target_pairs={{2,0},{19,1},{32,2},{49,3},{42,4},{59,5},{8,6},{25,7},{6,8},{23,9}... | collective-permute-start | bytes 196616 | tf_op jit(solution)/shard_map/ppermute | solution.py:309
  15.2 0.4 collective-permute-start.3
  15.6 0.0 collective-permute-done
  15.6 0.0 collective-permute-done.1
  15.7 3.5 %collective-permute-done.2 = bf16[128,256]{1,0:T(8,128)(2,1)S(1)} collective-permute-done((bf16[128,256]{1,0:T(8,128)(2,1)S(1)}, bf16[128,256]{1,0:T(8,128)(2,1)S(1)}, u32[]{:S(2)}, u32[]{:S(2)}) %collective-permute-start.2) | collective-permute-done | bytes 65568 | tf_op jit(solution)/shard_map/ppermute | solution.py:309
  19.2 2.2 %collective-permute-done.3 = bf16[128,256]{1,0:T(8,128)(2,1)S(1)} collective-permute-done((bf16[128,256]{1,0:T(8,128)(2,1)S(1)}, bf16[128,256]{1,0:T(8,128)(2,1)S(1)}, u32[]{:S(2)}, u32[]{:S(2)}) %collective-permute-start.3) | collective-permute-done | bytes 65568 | tf_op jit(solution)/shard_map/ppermute | solution.py:309
  21.4 1.3 %collective-permute-start.7 = (bf16[4,128,256]{2,1,0:T(8,128)(2,1)S(1)}, bf16[4,128,256]{2,1,0:T(8,128)(2,1)S(1)}, u32[]{:S(2)}, u32[]{:S(2)}) collective-permute-start(bf16[4,128,256]{2,1,0:T(8,128)(2,1)S(1)} %pad_maximum_fusion.refs_0_), channel_id=1, source_target_pairs={{0,64},{1,65},{2,66},{3,67},{4,68},{5,69},{6,70},{7,71},{8,72},{9,... | collective-permute-start | bytes 786440 | tf_op jit(solution)/shard_map/ppermute | solution.py:309
  22.6 0.8 collective-permute-start.5
  23.5 5.8 %collective-permute-done.7.refs_4_ = bf16[4,128,256]{2,1,0:T(8,128)(2,1)S(1)} collective-permute-done((bf16[4,128,256]{2,1,0:T(8,128)(2,1)S(1)}, bf16[4,128,256]{2,1,0:T(8,128)(2,1)S(1)}, u32[]{:S(2)}, u32[]{:S(2)}) %collective-permute-start.7) | collective-permute-done | bytes 262176 | tf_op jit(solution)/shard_map/ppermute | solution.py:309
  29.3 0.0 collective-permute-start.8
  29.3 0.9 %collective-permute-done.5.refs_2_ = bf16[4,128,256]{2,1,0:T(8,128)(2,1)S(1)} collective-permute-done((bf16[4,128,256]{2,1,0:T(8,128)(2,1)S(1)}, bf16[4,128,256]{2,1,0:T(8,128)(2,1)S(1)}, u32[]{:S(2)}, u32[]{:S(2)}) %collective-permute-start.5) | collective-permute-done | bytes 262176 | tf_op jit(solution)/shard_map/ppermute | solution.py:309
  30.2 0.0 collective-permute-start.6
  30.2 0.5 collective-permute-start.4
  30.7 0.1 collective-permute-done.8.refs_5_
  30.8 0.9 %collective-permute-done.6.refs_3_ = bf16[4,128,256]{2,1,0:T(8,128)(2,1)S(1)} collective-permute-done((bf16[4,128,256]{2,1,0:T(8,128)(2,1)S(1)}, bf16[4,128,256]{2,1,0:T(8,128)(2,1)S(1)}, u32[]{:S(2)}, u32[]{:S(2)}) %collective-permute-start.6) | collective-permute-done | bytes 262176 | tf_op jit(solution)/shard_map/ppermute | solution.py:309
  31.7 0.1 maximum_select_fusion
  31.8 0.9 %collective-permute-start.9 = (bf16[2,4,128,256]{3,2,1,0:T(8,128)(2,1)S(1)}, bf16[2,4,128,256]{3,2,1,0:T(8,128)(2,1)S(1)}, u32[]{:S(2)}, u32[]{:S(2)}) collective-permute-start(bf16[2,4,128,256]{3,2,1,0:T(8,128)(2,1)S(1)} %maximum_select_fusion), channel_id=1, source_target_pairs={{0,192},{1,193},{2,194},{3,195},{4,196},{5,197},{6,198},{7,199},{8... | collective-permute-start | bytes 1572872 | tf_op jit(solution)/shard_map/ppermute | solution.py:309
  32.7 0.0 collective-permute-done.4.refs_1_
  32.7 0.0 copy-start.1
  32.7 0.7 copy-done.1
  33.4 13.6 %shard_map.37 = (f32[8,4,128]{2,1,0:T(4,128)S(1)}, f32[2,8,4,128]{3,2,1,0:T(4,128)S(1)}) custom-call(s32[32]{0:T(128)S(1)} %copy-done.1, bf16[32,8,128,128]{3,2,1,0:T(8,128)(2,1)} %bitcast.36, bf16[4,128,256]{2,1,0:T(8,128)(2,1)S(1)} %pad_maximum_fusion.refs_0_, bf16[4,128,256]{2,1,0:T(8,128)(2,1)S(1)} %collective-permute-done.4.refs_1_, ...), custom_call_target="tpu_custom_call" | custom-call | flops 8000000000 | bytes 12000000 | tf_op jit(solution)/shard_map/pallas_call | solution.py:277
  47.0 0.0 collective-permute-done.9
  47.0 14.5 %shard_map.38 = (f32[8,4,128]{2,1,0:T(4,128)S(1)}, f32[2,8,4,128]{3,2,1,0:T(4,128)S(1)}) custom-call(s32[32]{0:T(128)S(1)} %copy-done.1, bf16[32,8,128,128]{3,2,1,0:T(8,128)(2,1)} %bitcast.37, f32[8,4,128]{2,1,0:T(4,128)S(1)} %get-tuple-element.9.own_in, f32[2,8,4,128]{3,2,1,0:T(4,128)S(1)} %get-tuple-element.10.mirror_in, ...), custom_call_target="tpu_custom_call" | custom-call | flops 8000000000 | bytes 12000000 | tf_op jit(solution)/shard_map/pallas_call | solution.py:277
  61.5 0.8 collective-permute-start.10
  62.4 0.8 collective-permute-done.10
  63.2 7.1 %collective-permute-start.11 = (f32[8,4,128]{2,1,0:T(4,128)S(1)}, f32[8,4,128]{2,1,0:T(4,128)S(1)}, u32[]{:S(2)}, u32[]{:S(2)}) collective-permute-start(f32[8,4,128]{2,1,0:T(4,128)S(1)} %bitcast_add_fusion), channel_id=1, source_target_pairs={{0,0},{1,1},{2,2},{3,3},{4,4},{5,5},{6,6},{7,7},{8,8},{9,9},{10,10... | collective-permute-start | bytes 49160 | tf_op jit(solution)/shard_map/ppermute | solution.py:309
  70.3 4.8 %collective-permute-done.11 = f32[8,4,128]{2,1,0:T(4,128)S(1)} collective-permute-done((f32[8,4,128]{2,1,0:T(4,128)S(1)}, f32[8,4,128]{2,1,0:T(4,128)S(1)}, u32[]{:S(2)}, u32[]{:S(2)}) %collective-permute-start.11) | collective-permute-done | bytes 16416 | tf_op jit(solution)/shard_map/ppermute | solution.py:309
  75.1 13.1 %all_to_all.5 = f32[8,4,128]{2,1,0:T(4,128)S(1)} all-to-all(f32[8,4,128]{2,1,0:T(4,128)S(1)} %add.12), channel_id=1, replica_groups=mesh['oi'=4,'oj'=8,'vert'=8] {'vert'}, dimensions={0} | all-to-all | bytes 32768 | tf_op jit(solution)/shard_map/all_to_all | solution.py:328
  88.3 0.1 reshape.9
  88.4 0.8 copy.6
  (6 shorter events, 0.1 us)
Async XLA Ops:
  0.0 1.0 %copy-start = (bf16[1,256,4,128]{3,2,1,0:T(4,128)(2,1)S(1)}, bf16[1,256,4,128]{3,2,1,0:T(4,128)(2,1)}, u32[]{:S(2)}) copy-start(bf16[1,256,4,128]{3,2,1,0:T(4,128)(2,1)} %param.4) | copy-start | bytes 786436
  1.2 14.4 %collective-permute-start = (bf16[128,256]{1,0:T(8,128)(2,1)S(1)}, bf16[128,256]{1,0:T(8,128)(2,1)S(1)}, u32[]{:S(2)}, u32[]{:S(2)}) collective-permute-start(bf16[128,256]{1,0:T(8,128)(2,1)S(1)} %bitcast.28), channel_id=1, source_target_pairs={{0,0},{17,1},{34,2},{51,3},{40,4},{57,5},{10,6},{27,7},{4,8},{21,9... | collective-permute-start | bytes 196616 | tf_op jit(solution)/shard_map/ppermute | solution.py:309
  1.9 13.8 %collective-permute-start.1 = (bf16[128,256]{1,0:T(8,128)(2,1)S(1)}, bf16[128,256]{1,0:T(8,128)(2,1)S(1)}, u32[]{:S(2)}, u32[]{:S(2)}) collective-permute-start(bf16[128,256]{1,0:T(8,128)(2,1)S(1)} %bitcast.29), channel_id=1, source_target_pairs={{1,0},{16,1},{35,2},{50,3},{41,4},{56,5},{11,6},{26,7},{5,8},{20,9... | collective-permute-start | bytes 196616 | tf_op jit(solution)/shard_map/ppermute | solution.py:309
  12.0 7.2 %collective-permute-start.2 = (bf16[128,256]{1,0:T(8,128)(2,1)S(1)}, bf16[128,256]{1,0:T(8,128)(2,1)S(1)}, u32[]{:S(2)}, u32[]{:S(2)}) collective-permute-start(bf16[128,256]{1,0:T(8,128)(2,1)S(1)} %bitcast.30), channel_id=1, source_target_pairs={{2,0},{19,1},{32,2},{49,3},{42,4},{59,5},{8,6},{25,7},{6,8},{23,9}... | collective-permute-start | bytes 196616 | tf_op jit(solution)/shard_map/ppermute | solution.py:309
  15.2 6.1 %collective-permute-start.3 = (bf16[128,256]{1,0:T(8,128)(2,1)S(1)}, bf16[128,256]{1,0:T(8,128)(2,1)S(1)}, u32[]{:S(2)}, u32[]{:S(2)}) collective-permute-start(bf16[128,256]{1,0:T(8,128)(2,1)S(1)} %bitcast.31), channel_id=1, source_target_pairs={{3,0},{18,1},{33,2},{48,3},{43,4},{58,5},{9,6},{24,7},{7,8},{22,9}... | collective-permute-start | bytes 196616 | tf_op jit(solution)/shard_map/ppermute | solution.py:309
  21.4 7.9 %collective-permute-start.7 = (bf16[4,128,256]{2,1,0:T(8,128)(2,1)S(1)}, bf16[4,128,256]{2,1,0:T(8,128)(2,1)S(1)}, u32[]{:S(2)}, u32[]{:S(2)}) collective-permute-start(bf16[4,128,256]{2,1,0:T(8,128)(2,1)S(1)} %pad_maximum_fusion.refs_0_), channel_id=1, source_target_pairs={{0,64},{1,65},{2,66},{3,67},{4,68},{5,69},{6,70},{7,71},{8,72},{9,... | collective-permute-start | bytes 786440 | tf_op jit(solution)/shard_map/ppermute | solution.py:309
  22.6 7.5 %collective-permute-start.5 = (bf16[4,128,256]{2,1,0:T(8,128)(2,1)S(1)}, bf16[4,128,256]{2,1,0:T(8,128)(2,1)S(1)}, u32[]{:S(2)}, u32[]{:S(2)}) collective-permute-start(bf16[4,128,256]{2,1,0:T(8,128)(2,1)S(1)} %pad_maximum_fusion.refs_0_), channel_id=1, source_target_pairs={{0,192},{1,193},{2,194},{3,195},{4,196},{5,197},{6,198},{7,199},{8... | collective-permute-start | bytes 786440 | tf_op jit(solution)/shard_map/ppermute | solution.py:309
  29.3 1.5 %collective-permute-start.8 = (bf16[4,128,256]{2,1,0:T(8,128)(2,1)S(1)}, bf16[4,128,256]{2,1,0:T(8,128)(2,1)S(1)}, u32[]{:S(2)}, u32[]{:S(2)}) collective-permute-start(bf16[4,128,256]{2,1,0:T(8,128)(2,1)S(1)} %collective-permute-done.7.refs_4_), channel_id=1, source_target_pairs={{0,8},{1,9},{2,10},{3,11},{4,12},{5,13},{6,14},{7,15},{8,0},{9,1},... | collective-permute-start | bytes 786440 | tf_op jit(solution)/shard_map/ppermute | solution.py:309
  30.2 1.5 %collective-permute-start.6 = (bf16[4,128,256]{2,1,0:T(8,128)(2,1)S(1)}, bf16[4,128,256]{2,1,0:T(8,128)(2,1)S(1)}, u32[]{:S(2)}, u32[]{:S(2)}) collective-permute-start(bf16[4,128,256]{2,1,0:T(8,128)(2,1)S(1)} %collective-permute-done.5.refs_2_), channel_id=1, source_target_pairs={{0,8},{1,9},{2,10},{3,11},{4,12},{5,13},{6,14},{7,15},{8,0},{9,1},... | collective-permute-start | bytes 786440 | tf_op jit(solution)/shard_map/ppermute | solution.py:309
  30.2 2.5 %collective-permute-start.4 = (bf16[4,128,256]{2,1,0:T(8,128)(2,1)S(1)}, bf16[4,128,256]{2,1,0:T(8,128)(2,1)S(1)}, u32[]{:S(2)}, u32[]{:S(2)}) collective-permute-start(bf16[4,128,256]{2,1,0:T(8,128)(2,1)S(1)} %pad_maximum_fusion.refs_0_), channel_id=1, source_target_pairs={{0,8},{1,9},{2,10},{3,11},{4,12},{5,13},{6,14},{7,15},{8,0},{9,1},... | collective-permute-start | bytes 786440 | tf_op jit(solution)/shard_map/ppermute | solution.py:309
  31.8 15.2 %collective-permute-start.9 = (bf16[2,4,128,256]{3,2,1,0:T(8,128)(2,1)S(1)}, bf16[2,4,128,256]{3,2,1,0:T(8,128)(2,1)S(1)}, u32[]{:S(2)}, u32[]{:S(2)}) collective-permute-start(bf16[2,4,128,256]{3,2,1,0:T(8,128)(2,1)S(1)} %maximum_select_fusion), channel_id=1, source_target_pairs={{0,192},{1,193},{2,194},{3,195},{4,196},{5,197},{6,198},{7,199},{8... | collective-permute-start | bytes 1572872 | tf_op jit(solution)/shard_map/ppermute | solution.py:309
  32.7 0.7 copy-start.1
  61.5 1.6 %collective-permute-start.10 = (f32[8,4,128]{2,1,0:T(4,128)S(1)}, f32[8,4,128]{2,1,0:T(4,128)S(1)}, u32[]{:S(2)}, u32[]{:S(2)}) collective-permute-start(f32[8,4,128]{2,1,0:T(4,128)S(1)} %slice_bitcast_fusion.2), channel_id=1, source_target_pairs={{0,8},{1,9},{2,10},{3,11},{4,12},{5,13},{6,14},{7,15},{8,0},{9,1},... | collective-permute-start | bytes 49160 | tf_op jit(solution)/shard_map/ppermute | solution.py:309
  63.2 11.9 %collective-permute-start.11 = (f32[8,4,128]{2,1,0:T(4,128)S(1)}, f32[8,4,128]{2,1,0:T(4,128)S(1)}, u32[]{:S(2)}, u32[]{:S(2)}) collective-permute-start(f32[8,4,128]{2,1,0:T(4,128)S(1)} %bitcast_add_fusion), channel_id=1, source_target_pairs={{0,0},{1,1},{2,2},{3,3},{4,4},{5,5},{6,6},{7,7},{8,8},{9,9},{10,10... | collective-permute-start | bytes 49160 | tf_op jit(solution)/shard_map/ppermute | solution.py:309

commit v4 on v3

--- a/solution.py
+++ b/solution.py
@@ -82,10 +82,11 @@
 
 
 def load_pieces(pieces, chol, sems, first):
+    pieces = list(pieces[:12]) + [beyond.at[at] for beyond in pieces[12:] for at in range(4)]
     copies = []
     for at, piece in enumerate(pieces):
-        half = first if at % 2 == 0 else 1 - first
-        target = chol.at[pl.ds(half * 4, 4), at // 2]
+        half = first if at // 2 % 2 == 0 else 1 - first
+        target = chol.at[pl.ds(half * 4 + 2 * (at % 2), 2), at // 4]
         copies.append(pltpu.make_async_copy(piece, target, sems.at[at]))
     return copies
 
@@ -185,8 +186,8 @@
 
 
 def early_kernel(occ_ref, amp_ref, *refs):
-    pieces, (own_ref, mirror_ref) = refs[:6], refs[6:8]
-    chol, amp, window, spread, straight, turned, occ, *sems = refs[8:]
+    pieces, (own_ref, mirror_ref) = refs[:12], refs[12:14]
+    chol, amp, window, spread, straight, turned, occ, *sems = refs[14:]
     x, oj, vert, core, flip, first = place_of()
     begin(occ_ref, amp_ref, pieces, chol, amp, occ, sems, flip, first)
     sym = pair_labels(occ, x, oj)
@@ -225,8 +226,8 @@
 
 
 def late_kernel(occ_ref, amp_ref, own_in, mirror_in, *refs):
-    pieces, (own_ref, mirror_ref) = refs[:8], refs[8:10]
-    chol, amp, window, spread, straight, turned, occ, *sems = refs[10:]
+    pieces, (own_ref, mirror_ref) = refs[:13], refs[13:15]
+    chol, amp, window, spread, straight, turned, occ, *sems = refs[15:]
     x, oj, vert, core, flip, first = place_of()
     begin(occ_ref, amp_ref, pieces, chol, amp, occ, sems, flip, first)
     sym = pair_labels(occ, x, oj)
@@ -290,7 +291,7 @@
             pltpu.VMEM((IRREPS, WB * WB, LO, COLS), jnp.float32),
             pltpu.VMEM((IRREPS, WB * WB, LO, COLS), jnp.float32),
             pltpu.SMEM((PAIRS,), jnp.int32),
-            pltpu.SemaphoreType.DMA((8,)),
+            pltpu.SemaphoreType.DMA((16,)),
             pltpu.SemaphoreType.DMA((8,)),
             pltpu.SemaphoreType.DMA,
         ],
@@ -309,19 +310,22 @@
         return lax.ppermute(value, AXES, pairs)
 
     mine = lax.dynamic_index_in_dim(chol[0], x, 1, False).T
-    near = jnp.stack([permute(mine, fetch_pairs(row)) for row in range(4)])
-    above, below = permute(near, moved_pairs(lower)), permute(near, moved_pairs(upper))
+    rows = [permute(mine, fetch_pairs(row)) for row in range(4)]
+    near = [jnp.stack(rows[:2]), jnp.stack(rows[2:])]
+    near[1], labels = lax.optimization_barrier((near[1], jnp.bitwise_and(occ_irrep, IRREPS - 1)))
+    above = [permute(half, moved_pairs(lower)) for half in near]
+    below = [permute(half, moved_pairs(upper)) for half in near]
     pieces = []
     for piece in (near, above, below):
-        pieces += [piece, permute(piece, moved_pairs(other_core))]
-    beyond = jnp.where(core == 0, jnp.stack(pieces[2:4]), jnp.stack(pieces[4:6]))
+        pieces += piece + [permute(half, moved_pairs(other_core)) for half in piece]
+    beyond = jnp.where(core == 0, jnp.stack(pieces[4:8]), jnp.stack(pieces[8:12]))
     beyond = permute(beyond, moved_pairs(apart))
     occ_rows, occ_cols = amplitudes.shape[0], amplitudes.shape[1]
     amp = amplitudes.reshape(PAIRS, IRREPS, VB, VB)
-    before = (occ_irrep, amp)
+    before = (labels, amp)
     mine, other = ladder(early_kernel, 3, (72 * LO,), before, pieces)
     before += (mine, other)
-    pieces += [beyond[0], beyond[1]]
+    pieces += [beyond]
     mine, other = ladder(late_kernel, 4, (56 * LO,), before, pieces)
     other = other[0] + permute(other[1], moved_pairs(other_core))
     total = mine + permute(other, moved_pairs(mirrored))

time: 89.4 us -> 87.8 us (0.982)
  waiting for transfers between devices: 19 us -> 9.51 us
  starting transfers between devices: 25.9 us -> 30.7 us
  blocking collectives: 13.1 us -> 15.8 us
    ppermute x12 -> x17, waiting for transfers between devices: 19 us -> 9.51 us  [permute(): return lax.ppermute(value, AXES, pairs)]
    ppermute x12 -> x17, starting transfers between devices: 25.9 us -> 30.7 us  [permute(): return lax.ppermute(value, AXES, pairs)]
    all_to_all x1, blocking collectives: 13.1 us -> 15.8 us  [local(): total = jnp.sum(lax.all_to_all(total, 'vert', 0, 0), axis=0)]
  transfers between devices with their start and end apart: 12 -> 17, of which waited for: 8 -> 9; matrix products, arithmetic and copies ran while one was open for 0% -> 1% of each run, Pallas kernels for 15% -> 16%
where the time goes in v4:
time: 87.8 us; the launch traced here: 87.6 us
  starting transfers between devices  30.7 us (35%)
  Pallas kernels  28.6 us (33%)
  blocking collectives  15.8 us (18%)
  waiting for transfers between devices  9.51 us (11%)
  local copies, waits for them, and re-layouts  2.1 us (2%)
    ppermute x17, starting transfers between devices, permute(): return lax.ppermute(value, AXES, pairs)  30.7 us
    pallas_call x2, Pallas kernels, ladder(): pl.pallas_call(kernel, out_shape=[jax.ShapeDtypeStruct((IRREPS, WB, VB),...  28.6 us
    all_to_all x1, blocking collectives, local(): total = jnp.sum(lax.all_to_all(total, 'vert', 0, 0), axis=0)  15.8 us
    ppermute x17, waiting for transfers between devices, permute(): return lax.ppermute(value, AXES, pairs)  9.51 us
  transfers between devices with their start and end apart: 17, of which 9 were waited for; matrix products, arithmetic and copies ran while one was open for 1% of the time, Pallas kernels for 16%

profile of v4, /device:TPU:4, one launch (start us, length us, event | category | flops | bytes accessed | tf_op | source)
XLA Modules:
  0.0 87.6 jit_solution(17275620885694095578)
XLA Ops:
  0.0 0.0 copy-start
  0.0 0.9 %copy-done = bf16[1,256,4,128]{3,2,1,0:T(4,128)(2,1)S(1)} copy-done((bf16[1,256,4,128]{3,2,1,0:T(4,128)(2,1)S(1)}, bf16[1,256,4,128]{3,2,1,0:T(4,128)(2,1)}, u32[]{:S(2)}) %copy-start) | copy-done | bytes 262168
  1.0 0.1 constant_dynamic-slice_fusion
  1.1 0.1 copy.5
  1.2 9.9 %collective-permute-start = (bf16[128,256]{1,0:T(8,128)(2,1)S(1)}, bf16[128,256]{1,0:T(8,128)(2,1)S(1)}, u32[]{:S(2)}, u32[]{:S(2)}) collective-permute-start(bf16[128,256]{1,0:T(8,128)(2,1)S(1)} %bitcast.32), channel_id=1, source_target_pairs={{2,0},{19,1},{32,2},{49,3},{42,4},{59,5},{8,6},{25,7},{6,8},{23,9}... | collective-permute-start | bytes 196616 | tf_op jit(solution)/shard_map/ppermute | solution.py:310
  11.1 0.0 collective-permute-start.1
  11.1 0.7 collective-permute-start.2
  11.8 3.5 %collective-permute-start.3 = (bf16[128,256]{1,0:T(8,128)(2,1)S(1)}, bf16[128,256]{1,0:T(8,128)(2,1)S(1)}, u32[]{:S(2)}, u32[]{:S(2)}) collective-permute-start(bf16[128,256]{1,0:T(8,128)(2,1)S(1)} %bitcast.35), channel_id=1, source_target_pairs={{1,0},{16,1},{35,2},{50,3},{41,4},{56,5},{11,6},{26,7},{5,8},{20,9... | collective-permute-start | bytes 196616 | tf_op jit(solution)/shard_map/ppermute | solution.py:310
  15.2 0.7 broadcast_and_fusion.occ_ref
  15.9 0.0 collective-permute-done
  15.9 0.7 collective-permute-done.1
  16.6 0.6 collective-permute-start.7
  17.2 1.5 %collective-permute-start.11 = (bf16[2,128,256]{2,1,0:T(8,128)(2,1)S(1)}, bf16[2,128,256]{2,1,0:T(8,128)(2,1)S(1)}, u32[]{:S(2)}, u32[]{:S(2)}) collective-permute-start(bf16[2,128,256]{2,1,0:T(8,128)(2,1)S(1)} %pad_maximum_fusion.refs_1_), channel_id=1, source_target_pairs={{0,64},{1,65},{2,66},{3,67},{4,68},{5,69},{6,70},{7,71},{8,72},{9,... | collective-permute-start | bytes 393224 | tf_op jit(solution)/shard_map/ppermute | solution.py:310
  18.7 0.0 collective-permute-done.2
  18.7 0.0 collective-permute-done.3
  18.7 0.6 collective-permute-start.6
  19.3 2.0 %collective-permute-start.10 = (bf16[2,128,256]{2,1,0:T(8,128)(2,1)S(1)}, bf16[2,128,256]{2,1,0:T(8,128)(2,1)S(1)}, u32[]{:S(2)}, u32[]{:S(2)}) collective-permute-start(bf16[2,128,256]{2,1,0:T(8,128)(2,1)S(1)} %pad_maximum_fusion.1.refs_0_), channel_id=1, source_target_pairs={{0,64},{1,65},{2,66},{3,67},{4,68},{5,69},{6,70},{7,71},{8,72},{9,... | collective-permute-start | bytes 393224 | tf_op jit(solution)/shard_map/ppermute | solution.py:310
  21.3 0.6 collective-permute-done.7.refs_5_
  21.9 0.0 collective-permute-start.9
  21.9 0.8 collective-permute-done.11.refs_9_
  22.7 0.0 collective-permute-start.13
  22.7 1.9 %collective-permute-done.6.refs_4_ = bf16[2,128,256]{2,1,0:T(8,128)(2,1)S(1)} collective-permute-done((bf16[2,128,256]{2,1,0:T(8,128)(2,1)S(1)}, bf16[2,128,256]{2,1,0:T(8,128)(2,1)S(1)}, u32[]{:S(2)}, u32[]{:S(2)}) %collective-permute-start.6) | collective-permute-done | bytes 131104 | tf_op jit(solution)/shard_map/ppermute | solution.py:310
  24.5 0.0 collective-permute-start.8
  24.5 0.5 collective-permute-done.10.refs_8_
  25.0 0.0 collective-permute-start.12
  25.0 0.5 collective-permute-start.5
  25.5 0.0 collective-permute-done.9.refs_7_
  25.5 0.0 collective-permute-start.4
  25.5 0.0 collective-permute-done.13.refs_11_
  25.5 0.3 collective-permute-done.8.refs_6_
  25.9 0.5 collective-permute-done.12.refs_10_
  26.3 0.1 maximum_select_fusion
  26.5 2.1 %collective-permute-start.14 = (bf16[4,2,128,256]{3,2,1,0:T(8,128)(2,1)S(1)}, bf16[4,2,128,256]{3,2,1,0:T(8,128)(2,1)S(1)}, u32[]{:S(2)}, u32[]{:S(2)}) collective-permute-start(bf16[4,2,128,256]{3,2,1,0:T(8,128)(2,1)S(1)} %maximum_select_fusion), channel_id=1, source_target_pairs={{0,192},{1,193},{2,194},{3,195},{4,196},{5,197},{6,198},{7,199},{8... | collective-permute-start | bytes 1572872 | tf_op jit(solution)/shard_map/ppermute | solution.py:310
  28.5 0.0 collective-permute-done.5.refs_3_
  28.5 0.0 collective-permute-done.4.refs_2_
  28.5 13.7 %shard_map.37 = (f32[8,4,128]{2,1,0:T(4,128)S(1)}, f32[2,8,4,128]{3,2,1,0:T(4,128)S(1)}) custom-call(s32[32]{0:T(128)S(1)} %broadcast_and_fusion.occ_ref, bf16[32,8,128,128]{3,2,1,0:T(8,128)(2,1)} %bitcast.40, bf16[2,128,256]{2,1,0:T(8,128)(2,1)S(1)} %pad_maximum_fusion.1.refs_0_, bf16[2,128,256]{2,1,0:T(8,128)(2,1)S(1)} %pad_maximum_fusion.refs_1_, ...), custom_call_target="tpu_custom_call" | custom-call | flops 8000000000 | bytes 12000000 | tf_op jit(solution)/shard_map/pallas_call | solution.py:278
  42.2 0.0 collective-permute-done.14.refs_12_
  42.2 14.9 %shard_map.38 = (f32[8,4,128]{2,1,0:T(4,128)S(1)}, f32[2,8,4,128]{3,2,1,0:T(4,128)S(1)}) custom-call(s32[32]{0:T(128)S(1)} %broadcast_and_fusion.occ_ref, bf16[32,8,128,128]{3,2,1,0:T(8,128)(2,1)} %bitcast.41, f32[8,4,128]{2,1,0:T(4,128)S(1)} %get-tuple-element.13.own_in, f32[2,8,4,128]{3,2,1,0:T(4,128)S(1)} %get-tuple-element.14.mirror_in, ...), custom_call_target="tpu_custom_call" | custom-call | flops 8000000000 | bytes 12000000 | tf_op jit(solution)/shard_map/pallas_call | solution.py:278
  57.1 0.9 %collective-permute-start.15 = (f32[8,4,128]{2,1,0:T(4,128)S(1)}, f32[8,4,128]{2,1,0:T(4,128)S(1)}, u32[]{:S(2)}, u32[]{:S(2)}) collective-permute-start(f32[8,4,128]{2,1,0:T(4,128)S(1)} %slice_bitcast_fusion), channel_id=1, source_target_pairs={{0,8},{1,9},{2,10},{3,11},{4,12},{5,13},{6,14},{7,15},{8,0},{9,1},... | collective-permute-start | bytes 49160 | tf_op jit(solution)/shard_map/ppermute | solution.py:310
  58.1 0.8 collective-permute-done.15
  58.9 8.4 %collective-permute-start.16 = (f32[8,4,128]{2,1,0:T(4,128)S(1)}, f32[8,4,128]{2,1,0:T(4,128)S(1)}, u32[]{:S(2)}, u32[]{:S(2)}) collective-permute-start(f32[8,4,128]{2,1,0:T(4,128)S(1)} %bitcast_add_fusion), channel_id=1, source_target_pairs={{0,0},{1,1},{2,2},{3,3},{4,4},{5,5},{6,6},{7,7},{8,8},{9,9},{10,10... | collective-permute-start | bytes 49160 | tf_op jit(solution)/shard_map/ppermute | solution.py:310
  67.4 3.5 %collective-permute-done.16 = f32[8,4,128]{2,1,0:T(4,128)S(1)} collective-permute-done((f32[8,4,128]{2,1,0:T(4,128)S(1)}, f32[8,4,128]{2,1,0:T(4,128)S(1)}, u32[]{:S(2)}, u32[]{:S(2)}) %collective-permute-start.16) | collective-permute-done | bytes 16416 | tf_op jit(solution)/shard_map/ppermute | solution.py:310
  70.9 15.8 %all_to_all.5 = f32[8,4,128]{2,1,0:T(4,128)S(1)} all-to-all(f32[8,4,128]{2,1,0:T(4,128)S(1)} %add.12), channel_id=1, replica_groups=mesh['oi'=4,'oj'=8,'vert'=8] {'vert'}, dimensions={0} | all-to-all | bytes 32768 | tf_op jit(solution)/shard_map/all_to_all | solution.py:332
  86.7 0.1 reshape.9
  86.8 0.8 copy.6
  (6 shorter events, 0.1 us)
Async XLA Ops:
  0.0 1.0 %copy-start = (bf16[1,256,4,128]{3,2,1,0:T(4,128)(2,1)S(1)}, bf16[1,256,4,128]{3,2,1,0:T(4,128)(2,1)}, u32[]{:S(2)}) copy-start(bf16[1,256,4,128]{3,2,1,0:T(4,128)(2,1)} %param.4) | copy-start | bytes 786436
  1.2 14.7 %collective-permute-start = (bf16[128,256]{1,0:T(8,128)(2,1)S(1)}, bf16[128,256]{1,0:T(8,128)(2,1)S(1)}, u32[]{:S(2)}, u32[]{:S(2)}) collective-permute-start(bf16[128,256]{1,0:T(8,128)(2,1)S(1)} %bitcast.32), channel_id=1, source_target_pairs={{2,0},{19,1},{32,2},{49,3},{42,4},{59,5},{8,6},{25,7},{6,8},{23,9}... | collective-permute-start | bytes 196616 | tf_op jit(solution)/shard_map/ppermute | solution.py:310
  11.1 5.5 %collective-permute-start.1 = (bf16[128,256]{1,0:T(8,128)(2,1)S(1)}, bf16[128,256]{1,0:T(8,128)(2,1)S(1)}, u32[]{:S(2)}, u32[]{:S(2)}) collective-permute-start(bf16[128,256]{1,0:T(8,128)(2,1)S(1)} %bitcast.33), channel_id=1, source_target_pairs={{3,0},{18,1},{33,2},{48,3},{43,4},{58,5},{9,6},{24,7},{7,8},{22,9}... | collective-permute-start | bytes 196616 | tf_op jit(solution)/shard_map/ppermute | solution.py:310
  11.1 7.6 %collective-permute-start.2 = (bf16[128,256]{1,0:T(8,128)(2,1)S(1)}, bf16[128,256]{1,0:T(8,128)(2,1)S(1)}, u32[]{:S(2)}, u32[]{:S(2)}) collective-permute-start(bf16[128,256]{1,0:T(8,128)(2,1)S(1)} %bitcast.34), channel_id=1, source_target_pairs={{0,0},{17,1},{34,2},{51,3},{40,4},{57,5},{10,6},{27,7},{4,8},{21,9... | collective-permute-start | bytes 196616 | tf_op jit(solution)/shard_map/ppermute | solution.py:310
  11.8 6.9 %collective-permute-start.3 = (bf16[128,256]{1,0:T(8,128)(2,1)S(1)}, bf16[128,256]{1,0:T(8,128)(2,1)S(1)}, u32[]{:S(2)}, u32[]{:S(2)}) collective-permute-start(bf16[128,256]{1,0:T(8,128)(2,1)S(1)} %bitcast.35), channel_id=1, source_target_pairs={{1,0},{16,1},{35,2},{50,3},{41,4},{56,5},{11,6},{26,7},{5,8},{20,9... | collective-permute-start | bytes 196616 | tf_op jit(solution)/shard_map/ppermute | solution.py:310
  16.6 5.3 %collective-permute-start.7 = (bf16[2,128,256]{2,1,0:T(8,128)(2,1)S(1)}, bf16[2,128,256]{2,1,0:T(8,128)(2,1)S(1)}, u32[]{:S(2)}, u32[]{:S(2)}) collective-permute-start(bf16[2,128,256]{2,1,0:T(8,128)(2,1)S(1)} %pad_maximum_fusion.refs_1_), channel_id=1, source_target_pairs={{0,192},{1,193},{2,194},{3,195},{4,196},{5,197},{6,198},{7,199},{8... | collective-permute-start | bytes 393224 | tf_op jit(solution)/shard_map/ppermute | solution.py:310
  17.2 5.4 %collective-permute-start.11 = (bf16[2,128,256]{2,1,0:T(8,128)(2,1)S(1)}, bf16[2,128,256]{2,1,0:T(8,128)(2,1)S(1)}, u32[]{:S(2)}, u32[]{:S(2)}) collective-permute-start(bf16[2,128,256]{2,1,0:T(8,128)(2,1)S(1)} %pad_maximum_fusion.refs_1_), channel_id=1, source_target_pairs={{0,64},{1,65},{2,66},{3,67},{4,68},{5,69},{6,70},{7,71},{8,72},{9,... | collective-permute-start | bytes 393224 | tf_op jit(solution)/shard_map/ppermute | solution.py:310
  18.7 5.8 %collective-permute-start.6 = (bf16[2,128,256]{2,1,0:T(8,128)(2,1)S(1)}, bf16[2,128,256]{2,1,0:T(8,128)(2,1)S(1)}, u32[]{:S(2)}, u32[]{:S(2)}) collective-permute-start(bf16[2,128,256]{2,1,0:T(8,128)(2,1)S(1)} %pad_maximum_fusion.1.refs_0_), channel_id=1, source_target_pairs={{0,192},{1,193},{2,194},{3,195},{4,196},{5,197},{6,198},{7,199},{8... | collective-permute-start | bytes 393224 | tf_op jit(solution)/shard_map/ppermute | solution.py:310
  19.3 5.6 %collective-permute-start.10 = (bf16[2,128,256]{2,1,0:T(8,128)(2,1)S(1)}, bf16[2,128,256]{2,1,0:T(8,128)(2,1)S(1)}, u32[]{:S(2)}, u32[]{:S(2)}) collective-permute-start(bf16[2,128,256]{2,1,0:T(8,128)(2,1)S(1)} %pad_maximum_fusion.1.refs_0_), channel_id=1, source_target_pairs={{0,64},{1,65},{2,66},{3,67},{4,68},{5,69},{6,70},{7,71},{8,72},{9,... | collective-permute-start | bytes 393224 | tf_op jit(solution)/shard_map/ppermute | solution.py:310
  21.9 3.6 %collective-permute-start.9 = (bf16[2,128,256]{2,1,0:T(8,128)(2,1)S(1)}, bf16[2,128,256]{2,1,0:T(8,128)(2,1)S(1)}, u32[]{:S(2)}, u32[]{:S(2)}) collective-permute-start(bf16[2,128,256]{2,1,0:T(8,128)(2,1)S(1)} %collective-permute-done.7.refs_5_), channel_id=1, source_target_pairs={{0,8},{1,9},{2,10},{3,11},{4,12},{5,13},{6,14},{7,15},{8,0},{9,1},... | collective-permute-start | bytes 393224 | tf_op jit(solution)/shard_map/ppermute | solution.py:310
  22.7 2.9 %collective-permute-start.13 = (bf16[2,128,256]{2,1,0:T(8,128)(2,1)S(1)}, bf16[2,128,256]{2,1,0:T(8,128)(2,1)S(1)}, u32[]{:S(2)}, u32[]{:S(2)}) collective-permute-start(bf16[2,128,256]{2,1,0:T(8,128)(2,1)S(1)} %collective-permute-done.11.refs_9_), channel_id=1, source_target_pairs={{0,8},{1,9},{2,10},{3,11},{4,12},{5,13},{6,14},{7,15},{8,0},{9,1},... | collective-permute-start | bytes 393224 | tf_op jit(solution)/shard_map/ppermute | solution.py:310
  24.5 1.3 %collective-permute-start.8 = (bf16[2,128,256]{2,1,0:T(8,128)(2,1)S(1)}, bf16[2,128,256]{2,1,0:T(8,128)(2,1)S(1)}, u32[]{:S(2)}, u32[]{:S(2)}) collective-permute-start(bf16[2,128,256]{2,1,0:T(8,128)(2,1)S(1)} %collective-permute-done.6.refs_4_), channel_id=1, source_target_pairs={{0,8},{1,9},{2,10},{3,11},{4,12},{5,13},{6,14},{7,15},{8,0},{9,1},... | collective-permute-start | bytes 393224 | tf_op jit(solution)/shard_map/ppermute | solution.py:310
  25.0 1.3 %collective-permute-start.12 = (bf16[2,128,256]{2,1,0:T(8,128)(2,1)S(1)}, bf16[2,128,256]{2,1,0:T(8,128)(2,1)S(1)}, u32[]{:S(2)}, u32[]{:S(2)}) collective-permute-start(bf16[2,128,256]{2,1,0:T(8,128)(2,1)S(1)} %collective-permute-done.10.refs_8_), channel_id=1, source_target_pairs={{0,8},{1,9},{2,10},{3,11},{4,12},{5,13},{6,14},{7,15},{8,0},{9,1},... | collective-permute-start | bytes 393224 | tf_op jit(solution)/shard_map/ppermute | solution.py:310
  25.0 3.5 %collective-permute-start.5 = (bf16[2,128,256]{2,1,0:T(8,128)(2,1)S(1)}, bf16[2,128,256]{2,1,0:T(8,128)(2,1)S(1)}, u32[]{:S(2)}, u32[]{:S(2)}) collective-permute-start(bf16[2,128,256]{2,1,0:T(8,128)(2,1)S(1)} %pad_maximum_fusion.refs_1_), channel_id=1, source_target_pairs={{0,8},{1,9},{2,10},{3,11},{4,12},{5,13},{6,14},{7,15},{8,0},{9,1},... | collective-permute-start | bytes 393224 | tf_op jit(solution)/shard_map/ppermute | solution.py:310
  25.5 3.0 %collective-permute-start.4 = (bf16[2,128,256]{2,1,0:T(8,128)(2,1)S(1)}, bf16[2,128,256]{2,1,0:T(8,128)(2,1)S(1)}, u32[]{:S(2)}, u32[]{:S(2)}) collective-permute-start(bf16[2,128,256]{2,1,0:T(8,128)(2,1)S(1)} %pad_maximum_fusion.1.refs_0_), channel_id=1, source_target_pairs={{0,8},{1,9},{2,10},{3,11},{4,12},{5,13},{6,14},{7,15},{8,0},{9,1},... | collective-permute-start | bytes 393224 | tf_op jit(solution)/shard_map/ppermute | solution.py:310
  26.5 15.8 %collective-permute-start.14 = (bf16[4,2,128,256]{3,2,1,0:T(8,128)(2,1)S(1)}, bf16[4,2,128,256]{3,2,1,0:T(8,128)(2,1)S(1)}, u32[]{:S(2)}, u32[]{:S(2)}) collective-permute-start(bf16[4,2,128,256]{3,2,1,0:T(8,128)(2,1)S(1)} %maximum_select_fusion), channel_id=1, source_target_pairs={{0,192},{1,193},{2,194},{3,195},{4,196},{5,197},{6,198},{7,199},{8... | collective-permute-start | bytes 1572872 | tf_op jit(solution)/shard_map/ppermute | solution.py:310
  57.1 1.8 %collective-permute-start.15 = (f32[8,4,128]{2,1,0:T(4,128)S(1)}, f32[8,4,128]{2,1,0:T(4,128)S(1)}, u32[]{:S(2)}, u32[]{:S(2)}) collective-permute-start(f32[8,4,128]{2,1,0:T(4,128)S(1)} %slice_bitcast_fusion), channel_id=1, source_target_pairs={{0,8},{1,9},{2,10},{3,11},{4,12},{5,13},{6,14},{7,15},{8,0},{9,1},... | collective-permute-start | bytes 49160 | tf_op jit(solution)/shard_map/ppermute | solution.py:310
  58.9 11.9 %collective-permute-start.16 = (f32[8,4,128]{2,1,0:T(4,128)S(1)}, f32[8,4,128]{2,1,0:T(4,128)S(1)}, u32[]{:S(2)}, u32[]{:S(2)}) collective-permute-start(f32[8,4,128]{2,1,0:T(4,128)S(1)} %bitcast_add_fusion), channel_id=1, source_target_pairs={{0,0},{1,1},{2,2},{3,3},{4,4},{5,5},{6,6},{7,7},{8,8},{9,9},{10,10... | collective-permute-start | bytes 49160 | tf_op jit(solution)/shard_map/ppermute | solution.py:310

commit v5 on v4

--- a/solution.py
+++ b/solution.py
@@ -42,6 +42,10 @@
     return [(flat_index(*d), flat_index(*move(*d))) for d in CHIPS]
 
 
+def next_row(x, zh, core, zl, y):
+    return (x, zh, core, zl, y ^ 1)
+
+
 def lower(x, zh, core, zl, y):
     return ((x + 3) % 4, zh, core, zl, y)
 
@@ -170,7 +174,7 @@
     )
 
 
-def begin(occ_ref, amp_ref, pieces, chol, amp, occ, sems, flip, first):
+def begin(occ_ref, amp_ref, pieces, chol, amp, occ, sems, flip, first, x, oj, slots, turned):
     chol_sem, amp_sem, occ_sem = sems
     occ_copy = pltpu.make_async_copy(occ_ref, occ, occ_sem)
     occ_copy.start()
@@ -179,26 +183,29 @@
     for copy in copies:
         copy.start()
     occ_copy.wait()
+    sym = pair_labels(occ, x, oj)
+    for a, b in slots:
+        turned[:, WB * a + b] = jnp.zeros((IRREPS, LO, COLS), jnp.float32)
     for copy in copies:
         copy.wait()
     for ga in range(1, IRREPS):
         amp_copy(amp_ref, amp, amp_sem, flip, ga).start()
+    return sym
 
 
 def early_kernel(occ_ref, amp_ref, *refs):
     pieces, (own_ref, mirror_ref) = refs[:12], refs[12:14]
     chol, amp, window, spread, straight, turned, occ, *sems = refs[14:]
     x, oj, vert, core, flip, first = place_of()
-    begin(occ_ref, amp_ref, pieces, chol, amp, occ, sems, flip, first)
-    sym = pair_labels(occ, x, oj)
     where = []
     for tile in range(12):
         for a in range(3):
             for at in (2 * tile, 2 * tile + 1):
                 where.append((at // 3, a, at % 3))
     slots = [(a, b) for a in range(3) for b in range(3)]
-    for a, b in slots:
-        turned[:, WB * a + b] = jnp.zeros((IRREPS, LO, COLS), jnp.float32)
+    sym = begin(
+        occ_ref, amp_ref, pieces, chol, amp, occ, sems, flip, first, x, oj, slots, turned
+    )
     own_ref[...] = jnp.zeros_like(own_ref)
     mirror_ref[...] = jnp.zeros_like(mirror_ref)
 
@@ -229,8 +236,6 @@
     pieces, (own_ref, mirror_ref) = refs[:13], refs[13:15]
     chol, amp, window, spread, straight, turned, occ, *sems = refs[15:]
     x, oj, vert, core, flip, first = place_of()
-    begin(occ_ref, amp_ref, pieces, chol, amp, occ, sems, flip, first)
-    sym = pair_labels(occ, x, oj)
     where = []
     for tile in range(4):
         for a in range(4):
@@ -238,36 +243,44 @@
     for at in range(24):
         where.append((at // 3, 3, at % 3))
     slots = [(a, 3) for a in range(4)] + [(3, b) for b in range(3)]
-    for a, b in slots:
-        turned[:, WB * a + b] = jnp.zeros((IRREPS, LO, COLS), jnp.float32)
+    sym = begin(
+        occ_ref, amp_ref, pieces, chol, amp, occ, sems, flip, first, x, oj, slots, turned
+    )
     own_ref[...] = own_in[...]
     mirror_ref[...] = mirror_in[...]
 
-    def one_irrep(ga, carry):
-        amp_copy(amp_ref, amp, sems[1], flip, ga).wait()
-        spread_out(amp[ga], spread)
-        left = chol[ga].reshape(WB * VB, PB)
-        for tile in range(4):
-            two = [chol[2 * tile, 3], chol[2 * tile + 1, 3]]
-            block = lax.dot_general(
-                left, jnp.concatenate(two, 0), NT, preferred_element_type=jnp.float32
-            )
-            for a in range(WB):
-                store_block(window, (tile * WB + a) * 2 * LO, block, a * VB)
+    def two_irreps(step, carry):
+        last = chol[pl.ds(2 * step, 2), 3].reshape(2 * VB, PB)
         for tile in range(12):
             two = [chol[at // 3, at % 3] for at in (2 * tile, 2 * tile + 1)]
             block = lax.dot_general(
-                chol[ga, 3], jnp.concatenate(two, 0), NT, preferred_element_type=jnp.float32
+                last, jnp.concatenate(two, 0), NT, preferred_element_type=jnp.float32
             )
-            store_block(window, (16 + tile) * 2 * LO, block, 0)
-        for start, stop in ((0, 32), (32, 56)):
-            rows = window[start * LO : stop * LO]
-            part = lax.dot_general(rows, spread[...], NT, preferred_element_type=jnp.float32)
-            part = part.reshape(stop - start, LO, COLS)
-            collect(part, sym, ga, where[start:stop], straight, turned)
-        return carry
-
-    lax.fori_loop(0, IRREPS, one_irrep, 0)
+            for u in range(2):
+                store_block(window, (32 + 24 * u + 2 * tile) * LO, block, u * VB)
+
+        def one_irrep(u, carry):
+            ga = 2 * step + u
+            amp_copy(amp_ref, amp, sems[1], flip, ga).wait()
+            spread_out(amp[ga], spread)
+            left = chol[ga].reshape(WB * VB, PB)
+            for tile in range(4):
+                two = [chol[2 * tile, 3], chol[2 * tile + 1, 3]]
+                block = lax.dot_general(
+                    left, jnp.concatenate(two, 0), NT, preferred_element_type=jnp.float32
+                )
+                for a in range(WB):
+                    store_block(window, (tile * WB + a) * 2 * LO, block, a * VB)
+            lower = window[pl.ds(pl.multiple_of((32 + 24 * u) * LO, 2 * LO), 24 * LO)]
+            for rows, start, stop in ((window[: 32 * LO], 0, 32), (lower, 32, 56)):
+                part = lax.dot_general(rows, spread[...], NT, preferred_element_type=jnp.float32)
+                part = part.reshape(stop - start, LO, COLS)
+                collect(part, sym, ga, where[start:stop], straight, turned)
+            return carry
+
+        return lax.fori_loop(0, 2, one_irrep, carry)
+
+    lax.fori_loop(0, IRREPS // 2, two_irreps, 0)
     finish(slots, straight, turned, own_ref, mirror_ref, x, core, vert)
 
 
@@ -310,14 +323,15 @@
         return lax.ppermute(value, AXES, pairs)
 
     mine = lax.dynamic_index_in_dim(chol[0], x, 1, False).T
-    rows = [permute(mine, fetch_pairs(row)) for row in range(4)]
-    near = [jnp.stack(rows[:2]), jnp.stack(rows[2:])]
+    pair = jnp.stack([mine, permute(mine, moved_pairs(next_row))])
+    near = [permute(pair, fetch_pairs(row)) for row in (0, 2)]
     near[1], labels = lax.optimization_barrier((near[1], jnp.bitwise_and(occ_irrep, IRREPS - 1)))
     above = [permute(half, moved_pairs(lower)) for half in near]
     below = [permute(half, moved_pairs(upper)) for half in near]
-    pieces = []
-    for piece in (near, above, below):
-        pieces += piece + [permute(half, moved_pairs(other_core)) for half in piece]
+    swap = moved_pairs(other_core)
+    beside = [permute(jnp.stack([above[far], below[far]]), swap) for far in range(2)]
+    pieces = near + [permute(half, swap) for half in near]
+    pieces += above + [beside[0][0], beside[1][0]] + below + [beside[0][1], beside[1][1]]
     beyond = jnp.where(core == 0, jnp.stack(pieces[4:8]), jnp.stack(pieces[8:12]))
     beyond = permute(beyond, moved_pairs(apart))
     occ_rows, occ_cols = amplitudes.shape[0], amplitudes.shape[1]
@@ -326,7 +340,7 @@
     mine, other = ladder(early_kernel, 3, (72 * LO,), before, pieces)
     before += (mine, other)
     pieces += [beyond]
-    mine, other = ladder(late_kernel, 4, (56 * LO,), before, pieces)
+    mine, other = ladder(late_kernel, 4, (80 * LO,), before, pieces)
     other = other[0] + permute(other[1], moved_pairs(other_core))
     total = mine + permute(other, moved_pairs(mirrored))
     total = jnp.sum(lax.all_to_all(total, "vert", 0, 0), axis=0)

time: 87.8 us -> 85.5 us (0.974); the launches traced: 87.6 us -> 84.4 us
  waiting for transfers between devices: 9.51 us -> 19.4 us
  starting transfers between devices: 30.7 us -> 23.9 us
  blocking collectives: 15.8 us -> 10.1 us
    ppermute x17 -> x14, waiting for transfers between devices: 9.51 us -> 19.4 us  [permute(): return lax.ppermute(value, AXES, pairs)]
    ppermute x17 -> x14, starting transfers between devices: 30.7 us -> 23.9 us  [permute(): return lax.ppermute(value, AXES, pairs)]
    all_to_all x1, blocking collectives: 15.8 us -> 10.1 us  [local(): total = jnp.sum(lax.all_to_all(total, 'vert', 0, 0), axis=0)]
  transfers between devices with their start and end apart: 17 -> 14, of which waited for: 9 -> 8; matrix products, arithmetic and copies ran while one was open for 1% -> 1% of each run, Pallas kernels for 16% -> 16%
where the time goes in v5:
time: 85.5 us; the launch traced here: 84.4 us
  Pallas kernels  27.9 us (33%)
  starting transfers between devices  23.9 us (28%)
  waiting for transfers between devices  19.4 us (23%)
  blocking collectives  10.1 us (12%)
  local copies, waits for them, and re-layouts  2.17 us (3%)
  other arithmetic  0.88 us (1%)
    pallas_call x2, Pallas kernels, ladder(): pl.pallas_call(kernel, out_shape=[jax.ShapeDtypeStruct((IRREPS, WB, VB),...  27.9 us
    ppermute x14, starting transfers between devices, permute(): return lax.ppermute(value, AXES, pairs)  23.9 us
    ppermute x14, waiting for transfers between devices, permute(): return lax.ppermute(value, AXES, pairs)  19.4 us
    all_to_all x1, blocking collectives, local(): total = jnp.sum(lax.all_to_all(total, 'vert', 0, 0), axis=0)  10.1 us
  transfers between devices with their start and end apart: 14, of which 8 were waited for; matrix products, arithmetic and copies ran while one was open for 1% of the time, Pallas kernels for 16%

profile of v5, /device:TPU:4, one launch (start us, length us, event | category | flops | bytes accessed | tf_op | source)
XLA Modules:
  0.0 84.4 jit_solution(3094779342711931805)
XLA Ops:
  0.0 0.0 copy-start
  0.0 0.9 %copy-done = bf16[1,256,4,128]{3,2,1,0:T(4,128)(2,1)S(1)} copy-done((bf16[1,256,4,128]{3,2,1,0:T(4,128)(2,1)S(1)}, bf16[1,256,4,128]{3,2,1,0:T(4,128)(2,1)}, u32[]{:S(2)}) %copy-start) | copy-done | bytes 262168
  1.0 0.1 constant_dynamic-slice_fusion
  1.1 0.1 copy.5
  1.2 1.7 %collective-permute-start = (bf16[128,256]{1,0:T(8,128)(2,1)S(1)}, bf16[128,256]{1,0:T(8,128)(2,1)S(1)}, u32[]{:S(2)}, u32[]{:S(2)}) collective-permute-start(bf16[128,256]{1,0:T(8,128)(2,1)S(1)} %bitcast.34), channel_id=1, source_target_pairs={{0,1},{1,0},{2,3},{3,2},{4,5},{5,4},{6,7},{7,6},{8,9},{9,8},{10,11... | collective-permute-start | bytes 196616 | tf_op jit(solution)/shard_map/ppermute | solution.py:323
  2.9 2.7 %collective-permute-done = bf16[128,256]{1,0:T(8,128)(2,1)S(1)} collective-permute-done((bf16[128,256]{1,0:T(8,128)(2,1)S(1)}, bf16[128,256]{1,0:T(8,128)(2,1)S(1)}, u32[]{:S(2)}, u32[]{:S(2)}) %collective-permute-start) | collective-permute-done | bytes 65568 | tf_op jit(solution)/shard_map/ppermute | solution.py:323
  5.6 9.9 %collective-permute-start.1 = (bf16[2,128,256]{2,1,0:T(8,128)(2,1)S(1)}, bf16[2,128,256]{2,1,0:T(8,128)(2,1)S(1)}, u32[]{:S(2)}, u32[]{:S(2)}) collective-permute-start(bf16[2,128,256]{2,1,0:T(8,128)(2,1)S(1)} %pad_maximum_fusion.2), channel_id=1, source_target_pairs={{2,0},{19,1},{32,2},{49,3},{42,4},{59,5},{8,6},{25,7},{6,8},{23,9}... | collective-permute-start | bytes 393224 | tf_op jit(solution)/shard_map/ppermute | solution.py:323
  15.5 0.7 broadcast_and_fusion.occ_ref
  16.1 0.7 collective-permute-start.2
  16.8 3.1 %collective-permute-done.1.refs_1_ = bf16[2,128,256]{2,1,0:T(8,128)(2,1)S(1)} collective-permute-done((bf16[2,128,256]{2,1,0:T(8,128)(2,1)S(1)}, bf16[2,128,256]{2,1,0:T(8,128)(2,1)S(1)}, u32[]{:S(2)}, u32[]{:S(2)}) %collective-permute-start.1) | collective-permute-done | bytes 131104 | tf_op jit(solution)/shard_map/ppermute | solution.py:323
  20.0 1.2 %collective-permute-start.9 = (bf16[2,128,256]{2,1,0:T(8,128)(2,1)S(1)}, bf16[2,128,256]{2,1,0:T(8,128)(2,1)S(1)}, u32[]{:S(2)}, u32[]{:S(2)}) collective-permute-start(bf16[2,128,256]{2,1,0:T(8,128)(2,1)S(1)} %collective-permute-done.1.refs_1_), channel_id=1, source_target_pairs={{0,64},{1,65},{2,66},{3,67},{4,68},{5,69},{6,70},{7,71},{8,72},{9,... | collective-permute-start | bytes 393224 | tf_op jit(solution)/shard_map/ppermute | solution.py:323
  21.1 0.8 collective-permute-start.6
  22.0 0.0 collective-permute-done.2.refs_0_
  22.0 0.5 collective-permute-start.5
  22.5 1.5 %collective-permute-start.7 = (bf16[2,128,256]{2,1,0:T(8,128)(2,1)S(1)}, bf16[2,128,256]{2,1,0:T(8,128)(2,1)S(1)}, u32[]{:S(2)}, u32[]{:S(2)}) collective-permute-start(bf16[2,128,256]{2,1,0:T(8,128)(2,1)S(1)} %collective-permute-done.2.refs_0_), channel_id=1, source_target_pairs={{0,64},{1,65},{2,66},{3,67},{4,68},{5,69},{6,70},{7,71},{8,72},{9,... | collective-permute-start | bytes 393224 | tf_op jit(solution)/shard_map/ppermute | solution.py:323
  24.0 0.9 %collective-permute-done.9.refs_9_ = bf16[2,128,256]{2,1,0:T(8,128)(2,1)S(1)} collective-permute-done((bf16[2,128,256]{2,1,0:T(8,128)(2,1)S(1)}, bf16[2,128,256]{2,1,0:T(8,128)(2,1)S(1)}, u32[]{:S(2)}, u32[]{:S(2)}) %collective-permute-start.9) | collective-permute-done | bytes 131104 | tf_op jit(solution)/shard_map/ppermute | solution.py:323
  24.9 1.2 %collective-permute-done.6.refs_5_ = bf16[2,128,256]{2,1,0:T(8,128)(2,1)S(1)} collective-permute-done((bf16[2,128,256]{2,1,0:T(8,128)(2,1)S(1)}, bf16[2,128,256]{2,1,0:T(8,128)(2,1)S(1)}, u32[]{:S(2)}, u32[]{:S(2)}) %collective-permute-start.6) | collective-permute-done | bytes 131104 | tf_op jit(solution)/shard_map/ppermute | solution.py:323
  26.1 0.1 collective-permute-start.10
  26.2 2.1 %collective-permute-done.5.refs_4_ = bf16[2,128,256]{2,1,0:T(8,128)(2,1)S(1)} collective-permute-done((bf16[2,128,256]{2,1,0:T(8,128)(2,1)S(1)}, bf16[2,128,256]{2,1,0:T(8,128)(2,1)S(1)}, u32[]{:S(2)}, u32[]{:S(2)}) %collective-permute-start.5) | collective-permute-done | bytes 131104 | tf_op jit(solution)/shard_map/ppermute | solution.py:323
  28.4 0.0 collective-permute-done.7.refs_8_
  28.4 0.5 collective-permute-start.8
  28.9 0.1 collective-permute-start.4
  29.0 0.4 collective-permute-start.3
  29.4 0.0 collective-permute-done.10
  29.4 0.6 collective-permute-done.8
  30.1 0.1 maximum_select_fusion
  30.2 2.0 %collective-permute-start.11 = (bf16[4,2,128,256]{3,2,1,0:T(8,128)(2,1)S(1)}, bf16[4,2,128,256]{3,2,1,0:T(8,128)(2,1)S(1)}, u32[]{:S(2)}, u32[]{:S(2)}) collective-permute-start(bf16[4,2,128,256]{3,2,1,0:T(8,128)(2,1)S(1)} %maximum_select_fusion), channel_id=1, source_target_pairs={{0,192},{1,193},{2,194},{3,195},{4,196},{5,197},{6,198},{7,199},{8... | collective-permute-start | bytes 1572872 | tf_op jit(solution)/shard_map/ppermute | solution.py:323
  32.2 0.0 collective-permute-done.4.refs_3_
  32.2 0.0 collective-permute-done.3.refs_2_
  32.2 13.7 %shard_map.37 = (f32[8,4,128]{2,1,0:T(4,128)S(1)}, f32[2,8,4,128]{3,2,1,0:T(4,128)S(1)}) custom-call(s32[32]{0:T(128)S(1)} %broadcast_and_fusion.occ_ref, bf16[32,8,128,128]{3,2,1,0:T(8,128)(2,1)} %bitcast.38, bf16[2,128,256]{2,1,0:T(8,128)(2,1)S(1)} %collective-permute-done.2.refs_0_, bf16[2,128,256]{2,1,0:T(8,128)(2,1)S(1)} %collective-permute-done.1.refs_1_, ...), custom_call_target="tpu_custom_call" | custom-call | flops 8000000000 | bytes 12000000 | tf_op jit(solution)/shard_map/pallas_call | solution.py:291
  45.9 0.0 collective-permute-done.11.refs_12_
  45.9 14.2 %shard_map.38 = (f32[8,4,128]{2,1,0:T(4,128)S(1)}, f32[2,8,4,128]{3,2,1,0:T(4,128)S(1)}) custom-call(s32[32]{0:T(128)S(1)} %broadcast_and_fusion.occ_ref, bf16[32,8,128,128]{3,2,1,0:T(8,128)(2,1)} %bitcast.39, f32[8,4,128]{2,1,0:T(4,128)S(1)} %get-tuple-element.13.own_in, f32[2,8,4,128]{3,2,1,0:T(4,128)S(1)} %get-tuple-element.14.mirror_in, ...), custom_call_target="tpu_custom_call" | custom-call | flops 8000000000 | bytes 12000000 | tf_op jit(solution)/shard_map/pallas_call | solution.py:291
  60.1 0.3 collective-permute-start.12
  60.4 1.0 %collective-permute-done.12 = f32[8,4,128]{2,1,0:T(4,128)S(1)} collective-permute-done((f32[8,4,128]{2,1,0:T(4,128)S(1)}, f32[8,4,128]{2,1,0:T(4,128)S(1)}, u32[]{:S(2)}, u32[]{:S(2)}) %collective-permute-start.12) | collective-permute-done | bytes 16416 | tf_op jit(solution)/shard_map/ppermute | solution.py:323
  61.4 4.2 %collective-permute-start.13 = (f32[8,4,128]{2,1,0:T(4,128)S(1)}, f32[8,4,128]{2,1,0:T(4,128)S(1)}, u32[]{:S(2)}, u32[]{:S(2)}) collective-permute-start(f32[8,4,128]{2,1,0:T(4,128)S(1)} %bitcast_add_fusion), channel_id=1, source_target_pairs={{0,0},{1,1},{2,2},{3,3},{4,4},{5,5},{6,6},{7,7},{8,8},{9,9},{10,10... | collective-permute-start | bytes 49160 | tf_op jit(solution)/shard_map/ppermute | solution.py:323
  65.7 7.7 %collective-permute-done.13 = f32[8,4,128]{2,1,0:T(4,128)S(1)} collective-permute-done((f32[8,4,128]{2,1,0:T(4,128)S(1)}, f32[8,4,128]{2,1,0:T(4,128)S(1)}, u32[]{:S(2)}, u32[]{:S(2)}) %collective-permute-start.13) | collective-permute-done | bytes 16416 | tf_op jit(solution)/shard_map/ppermute | solution.py:323
  73.4 10.1 %all_to_all.5 = f32[8,4,128]{2,1,0:T(4,128)S(1)} all-to-all(f32[8,4,128]{2,1,0:T(4,128)S(1)} %add.12), channel_id=1, replica_groups=mesh['oi'=4,'oj'=8,'vert'=8] {'vert'}, dimensions={0} | all-to-all | bytes 32768 | tf_op jit(solution)/shard_map/all_to_all | solution.py:346
  83.5 0.1 reshape.9
  83.6 0.8 copy.6
  (9 shorter events, 0.2 us)
Async XLA Ops:
  0.0 1.0 %copy-start = (bf16[1,256,4,128]{3,2,1,0:T(4,128)(2,1)S(1)}, bf16[1,256,4,128]{3,2,1,0:T(4,128)(2,1)}, u32[]{:S(2)}) copy-start(bf16[1,256,4,128]{3,2,1,0:T(4,128)(2,1)} %param.4) | copy-start | bytes 786436
  1.2 4.4 %collective-permute-start = (bf16[128,256]{1,0:T(8,128)(2,1)S(1)}, bf16[128,256]{1,0:T(8,128)(2,1)S(1)}, u32[]{:S(2)}, u32[]{:S(2)}) collective-permute-start(bf16[128,256]{1,0:T(8,128)(2,1)S(1)} %bitcast.34), channel_id=1, source_target_pairs={{0,1},{1,0},{2,3},{3,2},{4,5},{5,4},{6,7},{7,6},{8,9},{9,8},{10,11... | collective-permute-start | bytes 196616 | tf_op jit(solution)/shard_map/ppermute | solution.py:323
  5.6 14.4 %collective-permute-start.1 = (bf16[2,128,256]{2,1,0:T(8,128)(2,1)S(1)}, bf16[2,128,256]{2,1,0:T(8,128)(2,1)S(1)}, u32[]{:S(2)}, u32[]{:S(2)}) collective-permute-start(bf16[2,128,256]{2,1,0:T(8,128)(2,1)S(1)} %pad_maximum_fusion.2), channel_id=1, source_target_pairs={{2,0},{19,1},{32,2},{49,3},{42,4},{59,5},{8,6},{25,7},{6,8},{23,9}... | collective-permute-start | bytes 393224 | tf_op jit(solution)/shard_map/ppermute | solution.py:323
  16.1 5.8 %collective-permute-start.2 = (bf16[2,128,256]{2,1,0:T(8,128)(2,1)S(1)}, bf16[2,128,256]{2,1,0:T(8,128)(2,1)S(1)}, u32[]{:S(2)}, u32[]{:S(2)}) collective-permute-start(bf16[2,128,256]{2,1,0:T(8,128)(2,1)S(1)} %pad_maximum_fusion.2), channel_id=1, source_target_pairs={{0,0},{17,1},{34,2},{51,3},{40,4},{57,5},{10,6},{27,7},{4,8},{21,9... | collective-permute-start | bytes 393224 | tf_op jit(solution)/shard_map/ppermute | solution.py:323
  20.0 5.0 %collective-permute-start.9 = (bf16[2,128,256]{2,1,0:T(8,128)(2,1)S(1)}, bf16[2,128,256]{2,1,0:T(8,128)(2,1)S(1)}, u32[]{:S(2)}, u32[]{:S(2)}) collective-permute-start(bf16[2,128,256]{2,1,0:T(8,128)(2,1)S(1)} %collective-permute-done.1.refs_1_), channel_id=1, source_target_pairs={{0,64},{1,65},{2,66},{3,67},{4,68},{5,69},{6,70},{7,71},{8,72},{9,... | collective-permute-start | bytes 393224 | tf_op jit(solution)/shard_map/ppermute | solution.py:323
  21.1 5.0 %collective-permute-start.6 = (bf16[2,128,256]{2,1,0:T(8,128)(2,1)S(1)}, bf16[2,128,256]{2,1,0:T(8,128)(2,1)S(1)}, u32[]{:S(2)}, u32[]{:S(2)}) collective-permute-start(bf16[2,128,256]{2,1,0:T(8,128)(2,1)S(1)} %collective-permute-done.1.refs_1_), channel_id=1, source_target_pairs={{0,192},{1,193},{2,194},{3,195},{4,196},{5,197},{6,198},{7,199},{8... | collective-permute-start | bytes 393224 | tf_op jit(solution)/shard_map/ppermute | solution.py:323
  22.0 6.4 %collective-permute-start.5 = (bf16[2,128,256]{2,1,0:T(8,128)(2,1)S(1)}, bf16[2,128,256]{2,1,0:T(8,128)(2,1)S(1)}, u32[]{:S(2)}, u32[]{:S(2)}) collective-permute-start(bf16[2,128,256]{2,1,0:T(8,128)(2,1)S(1)} %collective-permute-done.2.refs_0_), channel_id=1, source_target_pairs={{0,192},{1,193},{2,194},{3,195},{4,196},{5,197},{6,198},{7,199},{8... | collective-permute-start | bytes 393224 | tf_op jit(solution)/shard_map/ppermute | solution.py:323
  22.5 5.8 %collective-permute-start.7 = (bf16[2,128,256]{2,1,0:T(8,128)(2,1)S(1)}, bf16[2,128,256]{2,1,0:T(8,128)(2,1)S(1)}, u32[]{:S(2)}, u32[]{:S(2)}) collective-permute-start(bf16[2,128,256]{2,1,0:T(8,128)(2,1)S(1)} %collective-permute-done.2.refs_0_), channel_id=1, source_target_pairs={{0,64},{1,65},{2,66},{3,67},{4,68},{5,69},{6,70},{7,71},{8,72},{9,... | collective-permute-start | bytes 393224 | tf_op jit(solution)/shard_map/ppermute | solution.py:323
  26.1 3.2 %collective-permute-start.10 = (bf16[2,2,128,256]{3,2,1,0:T(8,128)(2,1)S(1)}, bf16[2,2,128,256]{3,2,1,0:T(8,128)(2,1)S(1)}, u32[]{:S(2)}, u32[]{:S(2)}) collective-permute-start(bf16[2,2,128,256]{3,2,1,0:T(8,128)(2,1)S(1)} %pad_maximum_fusion.1), channel_id=1, source_target_pairs={{0,8},{1,9},{2,10},{3,11},{4,12},{5,13},{6,14},{7,15},{8,0},{9,1},... | collective-permute-start | bytes 786440 | tf_op jit(solution)/shard_map/ppermute | solution.py:323
  28.4 1.6 %collective-permute-start.8 = (bf16[2,2,128,256]{3,2,1,0:T(8,128)(2,1)S(1)}, bf16[2,2,128,256]{3,2,1,0:T(8,128)(2,1)S(1)}, u32[]{:S(2)}, u32[]{:S(2)}) collective-permute-start(bf16[2,2,128,256]{3,2,1,0:T(8,128)(2,1)S(1)} %pad_maximum_fusion), channel_id=1, source_target_pairs={{0,8},{1,9},{2,10},{3,11},{4,12},{5,13},{6,14},{7,15},{8,0},{9,1},... | collective-permute-start | bytes 786440 | tf_op jit(solution)/shard_map/ppermute | solution.py:323
  28.9 3.3 %collective-permute-start.4 = (bf16[2,128,256]{2,1,0:T(8,128)(2,1)S(1)}, bf16[2,128,256]{2,1,0:T(8,128)(2,1)S(1)}, u32[]{:S(2)}, u32[]{:S(2)}) collective-permute-start(bf16[2,128,256]{2,1,0:T(8,128)(2,1)S(1)} %collective-permute-done.1.refs_1_), channel_id=1, source_target_pairs={{0,8},{1,9},{2,10},{3,11},{4,12},{5,13},{6,14},{7,15},{8,0},{9,1},... | collective-permute-start | bytes 393224 | tf_op jit(solution)/shard_map/ppermute | solution.py:323
  29.0 3.2 %collective-permute-start.3 = (bf16[2,128,256]{2,1,0:T(8,128)(2,1)S(1)}, bf16[2,128,256]{2,1,0:T(8,128)(2,1)S(1)}, u32[]{:S(2)}, u32[]{:S(2)}) collective-permute-start(bf16[2,128,256]{2,1,0:T(8,128)(2,1)S(1)} %collective-permute-done.2.refs_0_), channel_id=1, source_target_pairs={{0,8},{1,9},{2,10},{3,11},{4,12},{5,13},{6,14},{7,15},{8,0},{9,1},... | collective-permute-start | bytes 393224 | tf_op jit(solution)/shard_map/ppermute | solution.py:323
  30.2 15.7 %collective-permute-start.11 = (bf16[4,2,128,256]{3,2,1,0:T(8,128)(2,1)S(1)}, bf16[4,2,128,256]{3,2,1,0:T(8,128)(2,1)S(1)}, u32[]{:S(2)}, u32[]{:S(2)}) collective-permute-start(bf16[4,2,128,256]{3,2,1,0:T(8,128)(2,1)S(1)} %maximum_select_fusion), channel_id=1, source_target_pairs={{0,192},{1,193},{2,194},{3,195},{4,196},{5,197},{6,198},{7,199},{8... | collective-permute-start | bytes 1572872 | tf_op jit(solution)/shard_map/ppermute | solution.py:323
  60.1 1.3 %collective-permute-start.12 = (f32[8,4,128]{2,1,0:T(4,128)S(1)}, f32[8,4,128]{2,1,0:T(4,128)S(1)}, u32[]{:S(2)}, u32[]{:S(2)}) collective-permute-start(f32[8,4,128]{2,1,0:T(4,128)S(1)} %slice_bitcast_fusion), channel_id=1, source_target_pairs={{0,8},{1,9},{2,10},{3,11},{4,12},{5,13},{6,14},{7,15},{8,0},{9,1},... | collective-permute-start | bytes 49160 | tf_op jit(solution)/shard_map/ppermute | solution.py:323
  61.4 11.9 %collective-permute-start.13 = (f32[8,4,128]{2,1,0:T(4,128)S(1)}, f32[8,4,128]{2,1,0:T(4,128)S(1)}, u32[]{:S(2)}, u32[]{:S(2)}) collective-permute-start(f32[8,4,128]{2,1,0:T(4,128)S(1)} %bitcast_add_fusion), channel_id=1, source_target_pairs={{0,0},{1,1},{2,2},{3,3},{4,4},{5,5},{6,6},{7,7},{8,8},{9,9},{10,10... | collective-permute-start | bytes 49160 | tf_op jit(solution)/shard_map/ppermute | solution.py:323

commit v6 on v5

--- a/solution.py
+++ b/solution.py
@@ -341,9 +341,10 @@
     before += (mine, other)
     pieces += [beyond]
     mine, other = ladder(late_kernel, 4, (80 * LO,), before, pieces)
-    other = other[0] + permute(other[1], moved_pairs(other_core))
-    total = mine + permute(other, moved_pairs(mirrored))
-    total = jnp.sum(lax.all_to_all(total, "vert", 0, 0), axis=0)
+    every = jnp.concatenate([mine, other[0], other[1]], axis=1)
+    every = jnp.sum(lax.all_to_all(every, "vert", 0, 0), axis=0)
+    other = every[WB : 2 * WB] + permute(every[2 * WB :], moved_pairs(other_core))
+    total = every[:WB] + permute(other, moved_pairs(mirrored))
     total = total.reshape(WB, WB, occ_rows, occ_cols)
     return jnp.transpose(total, (2, 3, 0, 1))[:, :, None]
 

time: 85.5 us -> 84.8 us (level)
  waiting for transfers between devices: 19.4 us -> 14.2 us
  starting transfers between devices: 23.9 us -> 28.8 us
    ppermute x14, waiting for transfers between devices: 19.4 us -> 14.2 us  [permute(): return lax.ppermute(value, AXES, pairs)]
    ppermute x14, starting transfers between devices: 23.9 us -> 28.8 us  [permute(): return lax.ppermute(value, AXES, pairs)]
where the time goes in v6:
time: 84.8 us; the launch traced here: 84.3 us
  starting transfers between devices  28.8 us (34%)
  Pallas kernels  27.9 us (33%)
  waiting for transfers between devices  14.2 us (17%)
  blocking collectives  10.1 us (12%)
  local copies, waits for them, and re-layouts  2.17 us (3%)
  other arithmetic  0.89 us (1%)
    ppermute x14, starting transfers between devices, permute(): return lax.ppermute(value, AXES, pairs)  28.8 us
    pallas_call x2, Pallas kernels, ladder(): pl.pallas_call(kernel, out_shape=[jax.ShapeDtypeStruct((IRREPS, WB, VB),...  27.9 us
    ppermute x14, waiting for transfers between devices, permute(): return lax.ppermute(value, AXES, pairs)  14.2 us
    all_to_all x1, blocking collectives, local(): every = jnp.sum(lax.all_to_all(every, 'vert', 0, 0), axis=0)  10.1 us
  transfers between devices with their start and end apart: 14, of which 8 were waited for; matrix products, arithmetic and copies ran while one was open for 1% of the time, Pallas kernels for 16%

profile of v6, /device:TPU:4, one launch (start us, length us, event | category | flops | bytes accessed | tf_op | source)
XLA Modules:
  0.0 84.3 jit_solution(6356858732255774060)
XLA Ops:
  0.0 0.0 copy-start
  0.0 0.9 %copy-done = bf16[1,256,4,128]{3,2,1,0:T(4,128)(2,1)S(1)} copy-done((bf16[1,256,4,128]{3,2,1,0:T(4,128)(2,1)S(1)}, bf16[1,256,4,128]{3,2,1,0:T(4,128)(2,1)}, u32[]{:S(2)}) %copy-start) | copy-done | bytes 262168
  1.0 0.1 constant_dynamic-slice_fusion
  1.1 0.1 copy.5
  1.2 1.7 %collective-permute-start = (bf16[128,256]{1,0:T(8,128)(2,1)S(1)}, bf16[128,256]{1,0:T(8,128)(2,1)S(1)}, u32[]{:S(2)}, u32[]{:S(2)}) collective-permute-start(bf16[128,256]{1,0:T(8,128)(2,1)S(1)} %bitcast.34), channel_id=1, source_target_pairs={{0,1},{1,0},{2,3},{3,2},{4,5},{5,4},{6,7},{7,6},{8,9},{9,8},{10,11... | collective-permute-start | bytes 196616 | tf_op jit(solution)/shard_map/ppermute | solution.py:323
  2.9 2.7 %collective-permute-done = bf16[128,256]{1,0:T(8,128)(2,1)S(1)} collective-permute-done((bf16[128,256]{1,0:T(8,128)(2,1)S(1)}, bf16[128,256]{1,0:T(8,128)(2,1)S(1)}, u32[]{:S(2)}, u32[]{:S(2)}) %collective-permute-start) | collective-permute-done | bytes 65568 | tf_op jit(solution)/shard_map/ppermute | solution.py:323
  5.6 9.9 %collective-permute-start.1 = (bf16[2,128,256]{2,1,0:T(8,128)(2,1)S(1)}, bf16[2,128,256]{2,1,0:T(8,128)(2,1)S(1)}, u32[]{:S(2)}, u32[]{:S(2)}) collective-permute-start(bf16[2,128,256]{2,1,0:T(8,128)(2,1)S(1)} %pad_maximum_fusion.2), channel_id=1, source_target_pairs={{2,0},{19,1},{32,2},{49,3},{42,4},{59,5},{8,6},{25,7},{6,8},{23,9}... | collective-permute-start | bytes 393224 | tf_op jit(solution)/shard_map/ppermute | solution.py:323
  15.5 0.7 broadcast_and_fusion.occ_ref
  16.1 0.7 collective-permute-start.2
  16.8 3.1 %collective-permute-done.1.refs_1_ = bf16[2,128,256]{2,1,0:T(8,128)(2,1)S(1)} collective-permute-done((bf16[2,128,256]{2,1,0:T(8,128)(2,1)S(1)}, bf16[2,128,256]{2,1,0:T(8,128)(2,1)S(1)}, u32[]{:S(2)}, u32[]{:S(2)}) %collective-permute-start.1) | collective-permute-done | bytes 131104 | tf_op jit(solution)/shard_map/ppermute | solution.py:323
  20.0 1.2 %collective-permute-start.9 = (bf16[2,128,256]{2,1,0:T(8,128)(2,1)S(1)}, bf16[2,128,256]{2,1,0:T(8,128)(2,1)S(1)}, u32[]{:S(2)}, u32[]{:S(2)}) collective-permute-start(bf16[2,128,256]{2,1,0:T(8,128)(2,1)S(1)} %collective-permute-done.1.refs_1_), channel_id=1, source_target_pairs={{0,64},{1,65},{2,66},{3,67},{4,68},{5,69},{6,70},{7,71},{8,72},{9,... | collective-permute-start | bytes 393224 | tf_op jit(solution)/shard_map/ppermute | solution.py:323
  21.1 0.8 collective-permute-start.6
  22.0 0.0 collective-permute-done.2.refs_0_
  22.0 0.5 collective-permute-start.5
  22.5 1.5 %collective-permute-start.7 = (bf16[2,128,256]{2,1,0:T(8,128)(2,1)S(1)}, bf16[2,128,256]{2,1,0:T(8,128)(2,1)S(1)}, u32[]{:S(2)}, u32[]{:S(2)}) collective-permute-start(bf16[2,128,256]{2,1,0:T(8,128)(2,1)S(1)} %collective-permute-done.2.refs_0_), channel_id=1, source_target_pairs={{0,64},{1,65},{2,66},{3,67},{4,68},{5,69},{6,70},{7,71},{8,72},{9,... | collective-permute-start | bytes 393224 | tf_op jit(solution)/shard_map/ppermute | solution.py:323
  24.0 0.9 %collective-permute-done.9.refs_9_ = bf16[2,128,256]{2,1,0:T(8,128)(2,1)S(1)} collective-permute-done((bf16[2,128,256]{2,1,0:T(8,128)(2,1)S(1)}, bf16[2,128,256]{2,1,0:T(8,128)(2,1)S(1)}, u32[]{:S(2)}, u32[]{:S(2)}) %collective-permute-start.9) | collective-permute-done | bytes 131104 | tf_op jit(solution)/shard_map/ppermute | solution.py:323
  24.9 1.2 %collective-permute-done.6.refs_5_ = bf16[2,128,256]{2,1,0:T(8,128)(2,1)S(1)} collective-permute-done((bf16[2,128,256]{2,1,0:T(8,128)(2,1)S(1)}, bf16[2,128,256]{2,1,0:T(8,128)(2,1)S(1)}, u32[]{:S(2)}, u32[]{:S(2)}) %collective-permute-start.6) | collective-permute-done | bytes 131104 | tf_op jit(solution)/shard_map/ppermute | solution.py:323
  26.1 0.1 collective-permute-start.10
  26.2 2.1 %collective-permute-done.5.refs_4_ = bf16[2,128,256]{2,1,0:T(8,128)(2,1)S(1)} collective-permute-done((bf16[2,128,256]{2,1,0:T(8,128)(2,1)S(1)}, bf16[2,128,256]{2,1,0:T(8,128)(2,1)S(1)}, u32[]{:S(2)}, u32[]{:S(2)}) %collective-permute-start.5) | collective-permute-done | bytes 131104 | tf_op jit(solution)/shard_map/ppermute | solution.py:323
  28.4 0.0 collective-permute-done.7.refs_8_
  28.4 0.5 collective-permute-start.8
  28.9 0.1 collective-permute-start.4
  29.0 0.4 collective-permute-start.3
  29.4 0.0 collective-permute-done.10
  29.4 0.6 collective-permute-done.8
  30.1 0.1 maximum_select_fusion
  30.2 2.0 %collective-permute-start.11 = (bf16[4,2,128,256]{3,2,1,0:T(8,128)(2,1)S(1)}, bf16[4,2,128,256]{3,2,1,0:T(8,128)(2,1)S(1)}, u32[]{:S(2)}, u32[]{:S(2)}) collective-permute-start(bf16[4,2,128,256]{3,2,1,0:T(8,128)(2,1)S(1)} %maximum_select_fusion), channel_id=1, source_target_pairs={{0,192},{1,193},{2,194},{3,195},{4,196},{5,197},{6,198},{7,199},{8... | collective-permute-start | bytes 1572872 | tf_op jit(solution)/shard_map/ppermute | solution.py:323
  32.2 0.0 collective-permute-done.4.refs_3_
  32.2 0.0 collective-permute-done.3.refs_2_
  32.2 13.7 %shard_map.37 = (f32[8,4,128]{2,1,0:T(4,128)S(1)}, f32[2,8,4,128]{3,2,1,0:T(4,128)S(1)}) custom-call(s32[32]{0:T(128)S(1)} %broadcast_and_fusion.occ_ref, bf16[32,8,128,128]{3,2,1,0:T(8,128)(2,1)} %bitcast.38, bf16[2,128,256]{2,1,0:T(8,128)(2,1)S(1)} %collective-permute-done.2.refs_0_, bf16[2,128,256]{2,1,0:T(8,128)(2,1)S(1)} %collective-permute-done.1.refs_1_, ...), custom_call_target="tpu_custom_call" | custom-call | flops 8000000000 | bytes 12000000 | tf_op jit(solution)/shard_map/pallas_call | solution.py:291
  45.9 0.0 collective-permute-done.11.refs_12_
  45.9 14.2 %shard_map.38 = (f32[8,4,128]{2,1,0:T(4,128)S(1)}, f32[2,8,4,128]{3,2,1,0:T(4,128)S(1)}) custom-call(s32[32]{0:T(128)S(1)} %broadcast_and_fusion.occ_ref, bf16[32,8,128,128]{3,2,1,0:T(8,128)(2,1)} %bitcast.39, f32[8,4,128]{2,1,0:T(4,128)S(1)} %get-tuple-element.13.own_in, f32[2,8,4,128]{3,2,1,0:T(4,128)S(1)} %get-tuple-element.14.mirror_in, ...), custom_call_target="tpu_custom_call" | custom-call | flops 8000000000 | bytes 12000000 | tf_op jit(solution)/shard_map/pallas_call | solution.py:291
  60.2 10.1 %all_to_all.5 = f32[8,12,128]{2,1,0:T(8,128)S(1)} all-to-all(f32[8,12,128]{2,1,0:T(8,128)S(1)} %pad_maximum_fusion.3), channel_id=1, replica_groups=mesh['oi'=4,'oj'=8,'vert'=8] {'vert'}, dimensions={0} | all-to-all | bytes 98304 | tf_op jit(solution)/shard_map/all_to_all | solution.py:345
  70.3 0.1 collective-permute-start.12
  70.4 1.1 %collective-permute-done.12 = f32[4,128]{1,0:T(4,128)S(1)} collective-permute-done((f32[4,128]{1,0:T(4,128)S(1)}, f32[4,128]{1,0:T(4,128)S(1)}, u32[]{:S(2)}, u32[]{:S(2)}) %collective-permute-start.12) | collective-permute-done | bytes 2080 | tf_op jit(solution)/shard_map/ppermute | solution.py:323
  71.6 9.4 %collective-permute-start.13 = (f32[4,128]{1,0:T(4,128)S(1)}, f32[4,128]{1,0:T(4,128)S(1)}, u32[]{:S(2)}, u32[]{:S(2)}) collective-permute-start(f32[4,128]{1,0:T(4,128)S(1)} %slice_add_fusion), channel_id=1, source_target_pairs={{0,0},{1,1},{2,2},{3,3},{4,4},{5,5},{6,6},{7,7},{8,8},{9,9},{10,10... | collective-permute-start | bytes 6152 | tf_op jit(solution)/shard_map/ppermute | solution.py:323
  80.9 2.4 %collective-permute-done.13 = f32[4,128]{1,0:T(4,128)S(1)} collective-permute-done((f32[4,128]{1,0:T(4,128)S(1)}, f32[4,128]{1,0:T(4,128)S(1)}, u32[]{:S(2)}, u32[]{:S(2)}) %collective-permute-start.13) | collective-permute-done | bytes 2080 | tf_op jit(solution)/shard_map/ppermute | solution.py:323
  83.4 0.1 reshape.9
  83.5 0.8 copy.6
  (11 shorter events, 0.2 us)
Async XLA Ops:
  0.0 1.0 %copy-start = (bf16[1,256,4,128]{3,2,1,0:T(4,128)(2,1)S(1)}, bf16[1,256,4,128]{3,2,1,0:T(4,128)(2,1)}, u32[]{:S(2)}) copy-start(bf16[1,256,4,128]{3,2,1,0:T(4,128)(2,1)} %param.4) | copy-start | bytes 786436
  1.2 4.4 %collective-permute-start = (bf16[128,256]{1,0:T(8,128)(2,1)S(1)}, bf16[128,256]{1,0:T(8,128)(2,1)S(1)}, u32[]{:S(2)}, u32[]{:S(2)}) collective-permute-start(bf16[128,256]{1,0:T(8,128)(2,1)S(1)} %bitcast.34), channel_id=1, source_target_pairs={{0,1},{1,0},{2,3},{3,2},{4,5},{5,4},{6,7},{7,6},{8,9},{9,8},{10,11... | collective-permute-start | bytes 196616 | tf_op jit(solution)/shard_map/ppermute | solution.py:323
  5.6 14.4 %collective-permute-start.1 = (bf16[2,128,256]{2,1,0:T(8,128)(2,1)S(1)}, bf16[2,128,256]{2,1,0:T(8,128)(2,1)S(1)}, u32[]{:S(2)}, u32[]{:S(2)}) collective-permute-start(bf16[2,128,256]{2,1,0:T(8,128)(2,1)S(1)} %pad_maximum_fusion.2), channel_id=1, source_target_pairs={{2,0},{19,1},{32,2},{49,3},{42,4},{59,5},{8,6},{25,7},{6,8},{23,9}... | collective-permute-start | bytes 393224 | tf_op jit(solution)/shard_map/ppermute | solution.py:323
  16.1 5.8 %collective-permute-start.2 = (bf16[2,128,256]{2,1,0:T(8,128)(2,1)S(1)}, bf16[2,128,256]{2,1,0:T(8,128)(2,1)S(1)}, u32[]{:S(2)}, u32[]{:S(2)}) collective-permute-start(bf16[2,128,256]{2,1,0:T(8,128)(2,1)S(1)} %pad_maximum_fusion.2), channel_id=1, source_target_pairs={{0,0},{17,1},{34,2},{51,3},{40,4},{57,5},{10,6},{27,7},{4,8},{21,9... | collective-permute-start | bytes 393224 | tf_op jit(solution)/shard_map/ppermute | solution.py:323
  20.0 5.0 %collective-permute-start.9 = (bf16[2,128,256]{2,1,0:T(8,128)(2,1)S(1)}, bf16[2,128,256]{2,1,0:T(8,128)(2,1)S(1)}, u32[]{:S(2)}, u32[]{:S(2)}) collective-permute-start(bf16[2,128,256]{2,1,0:T(8,128)(2,1)S(1)} %collective-permute-done.1.refs_1_), channel_id=1, source_target_pairs={{0,64},{1,65},{2,66},{3,67},{4,68},{5,69},{6,70},{7,71},{8,72},{9,... | collective-permute-start | bytes 393224 | tf_op jit(solution)/shard_map/ppermute | solution.py:323
  21.1 5.0 %collective-permute-start.6 = (bf16[2,128,256]{2,1,0:T(8,128)(2,1)S(1)}, bf16[2,128,256]{2,1,0:T(8,128)(2,1)S(1)}, u32[]{:S(2)}, u32[]{:S(2)}) collective-permute-start(bf16[2,128,256]{2,1,0:T(8,128)(2,1)S(1)} %collective-permute-done.1.refs_1_), channel_id=1, source_target_pairs={{0,192},{1,193},{2,194},{3,195},{4,196},{5,197},{6,198},{7,199},{8... | collective-permute-start | bytes 393224 | tf_op jit(solution)/shard_map/ppermute | solution.py:323
  22.0 6.4 %collective-permute-start.5 = (bf16[2,128,256]{2,1,0:T(8,128)(2,1)S(1)}, bf16[2,128,256]{2,1,0:T(8,128)(2,1)S(1)}, u32[]{:S(2)}, u32[]{:S(2)}) collective-permute-start(bf16[2,128,256]{2,1,0:T(8,128)(2,1)S(1)} %collective-permute-done.2.refs_0_), channel_id=1, source_target_pairs={{0,192},{1,193},{2,194},{3,195},{4,196},{5,197},{6,198},{7,199},{8... | collective-permute-start | bytes 393224 | tf_op jit(solution)/shard_map/ppermute | solution.py:323
  22.5 5.8 %collective-permute-start.7 = (bf16[2,128,256]{2,1,0:T(8,128)(2,1)S(1)}, bf16[2,128,256]{2,1,0:T(8,128)(2,1)S(1)}, u32[]{:S(2)}, u32[]{:S(2)}) collective-permute-start(bf16[2,128,256]{2,1,0:T(8,128)(2,1)S(1)} %collective-permute-done.2.refs_0_), channel_id=1, source_target_pairs={{0,64},{1,65},{2,66},{3,67},{4,68},{5,69},{6,70},{7,71},{8,72},{9,... | collective-permute-start | bytes 393224 | tf_op jit(solution)/shard_map/ppermute | solution.py:323
  26.1 3.2 %collective-permute-start.10 = (bf16[2,2,128,256]{3,2,1,0:T(8,128)(2,1)S(1)}, bf16[2,2,128,256]{3,2,1,0:T(8,128)(2,1)S(1)}, u32[]{:S(2)}, u32[]{:S(2)}) collective-permute-start(bf16[2,2,128,256]{3,2,1,0:T(8,128)(2,1)S(1)} %pad_maximum_fusion.1), channel_id=1, source_target_pairs={{0,8},{1,9},{2,10},{3,11},{4,12},{5,13},{6,14},{7,15},{8,0},{9,1},... | collective-permute-start | bytes 786440 | tf_op jit(solution)/shard_map/ppermute | solution.py:323
  28.4 1.6 %collective-permute-start.8 = (bf16[2,2,128,256]{3,2,1,0:T(8,128)(2,1)S(1)}, bf16[2,2,128,256]{3,2,1,0:T(8,128)(2,1)S(1)}, u32[]{:S(2)}, u32[]{:S(2)}) collective-permute-start(bf16[2,2,128,256]{3,2,1,0:T(8,128)(2,1)S(1)} %pad_maximum_fusion), channel_id=1, source_target_pairs={{0,8},{1,9},{2,10},{3,11},{4,12},{5,13},{6,14},{7,15},{8,0},{9,1},... | collective-permute-start | bytes 786440 | tf_op jit(solution)/shard_map/ppermute | solution.py:323
  28.9 3.3 %collective-permute-start.4 = (bf16[2,128,256]{2,1,0:T(8,128)(2,1)S(1)}, bf16[2,128,256]{2,1,0:T(8,128)(2,1)S(1)}, u32[]{:S(2)}, u32[]{:S(2)}) collective-permute-start(bf16[2,128,256]{2,1,0:T(8,128)(2,1)S(1)} %collective-permute-done.1.refs_1_), channel_id=1, source_target_pairs={{0,8},{1,9},{2,10},{3,11},{4,12},{5,13},{6,14},{7,15},{8,0},{9,1},... | collective-permute-start | bytes 393224 | tf_op jit(solution)/shard_map/ppermute | solution.py:323
  29.0 3.2 %collective-permute-start.3 = (bf16[2,128,256]{2,1,0:T(8,128)(2,1)S(1)}, bf16[2,128,256]{2,1,0:T(8,128)(2,1)S(1)}, u32[]{:S(2)}, u32[]{:S(2)}) collective-permute-start(bf16[2,128,256]{2,1,0:T(8,128)(2,1)S(1)} %collective-permute-done.2.refs_0_), channel_id=1, source_target_pairs={{0,8},{1,9},{2,10},{3,11},{4,12},{5,13},{6,14},{7,15},{8,0},{9,1},... | collective-permute-start | bytes 393224 | tf_op jit(solution)/shard_map/ppermute | solution.py:323
  30.2 15.7 %collective-permute-start.11 = (bf16[4,2,128,256]{3,2,1,0:T(8,128)(2,1)S(1)}, bf16[4,2,128,256]{3,2,1,0:T(8,128)(2,1)S(1)}, u32[]{:S(2)}, u32[]{:S(2)}) collective-permute-start(bf16[4,2,128,256]{3,2,1,0:T(8,128)(2,1)S(1)} %maximum_select_fusion), channel_id=1, source_target_pairs={{0,192},{1,193},{2,194},{3,195},{4,196},{5,197},{6,198},{7,199},{8... | collective-permute-start | bytes 1572872 | tf_op jit(solution)/shard_map/ppermute | solution.py:323
  70.3 1.2 %collective-permute-start.12 = (f32[4,128]{1,0:T(4,128)S(1)}, f32[4,128]{1,0:T(4,128)S(1)}, u32[]{:S(2)}, u32[]{:S(2)}) collective-permute-start(f32[4,128]{1,0:T(4,128)S(1)} %slice.42), channel_id=1, source_target_pairs={{0,8},{1,9},{2,10},{3,11},{4,12},{5,13},{6,14},{7,15},{8,0},{9,1},... | collective-permute-start | bytes 6152 | tf_op jit(solution)/shard_map/ppermute | solution.py:323
  71.6 11.8 %collective-permute-start.13 = (f32[4,128]{1,0:T(4,128)S(1)}, f32[4,128]{1,0:T(4,128)S(1)}, u32[]{:S(2)}, u32[]{:S(2)}) collective-permute-start(f32[4,128]{1,0:T(4,128)S(1)} %slice_add_fusion), channel_id=1, source_target_pairs={{0,0},{1,1},{2,2},{3,3},{4,4},{5,5},{6,6},{7,7},{8,8},{9,9},{10,10... | collective-permute-start | bytes 6152 | tf_op jit(solution)/shard_map/ppermute | solution.py:323

commit v7 on v6

--- a/solution.py
+++ b/solution.py
@@ -158,14 +158,12 @@
             there = (jnp.bitwise_xor(vert, ga), pl.ds(actual[line], 1))
             own_ref[there] = own_ref[there] + value[ga : ga + 1]
     every = summed(turned)
-    target = core * 16 + (source % 4) * 4 + (source // 4) % 4
-    for k in range(2):
-        here = (source // 16) == jnp.bitwise_xor(core, k)
-        other = split(every, ((lane == target) & here).astype(jnp.bfloat16), False)
-        for line, value in other.items():
-            for ga in range(IRREPS):
-                there = (k, jnp.bitwise_xor(vert, ga), pl.ds(actual[line], 1))
-                mirror_ref[there] = mirror_ref[there] + value[ga : ga + 1]
+    target = (source // 16) * 16 + (source % 4) * 4 + (source // 4) % 4
+    other = split(every, (lane == target).astype(jnp.bfloat16), False)
+    for line, value in other.items():
+        for ga in range(IRREPS):
+            there = (jnp.bitwise_xor(vert, ga), pl.ds(actual[line], 1))
+            mirror_ref[there] = mirror_ref[there] + value[ga : ga + 1]
 
 
 def amp_copy(amp_ref, amp, sems, flip, ga):
@@ -292,7 +290,7 @@
         kernel,
         out_shape=[
             jax.ShapeDtypeStruct((IRREPS, WB, VB), jnp.float32),
-            jax.ShapeDtypeStruct((2, IRREPS, WB, VB), jnp.float32),
+            jax.ShapeDtypeStruct((IRREPS, WB, VB), jnp.float32),
         ],
         in_specs=[anywhere] * 2 + [whole] * len(earlier) + [anywhere] * len(pieces),
         out_specs=[whole] * 2,
@@ -341,9 +339,13 @@
     before += (mine, other)
     pieces += [beyond]
     mine, other = ladder(late_kernel, 4, (80 * LO,), before, pieces)
-    every = jnp.concatenate([mine, other[0], other[1]], axis=1)
+    every = jnp.concatenate([mine, other], axis=1)
     every = jnp.sum(lax.all_to_all(every, "vert", 0, 0), axis=0)
-    other = every[WB : 2 * WB] + permute(every[2 * WB :], moved_pairs(other_core))
+    other = every[WB:]
+    given = permute(other, moved_pairs(other_core))
+    side = jnp.arange(VB, dtype=jnp.int32)[None, :] // 16 % 2
+    given = jnp.where(side == 0, jnp.roll(given, -16, 1), jnp.roll(given, 16, 1))
+    other = jnp.where(side == core, other, given)
     total = every[:WB] + permute(other, moved_pairs(mirrored))
     total = total.reshape(WB, WB, occ_rows, occ_cols)
     return jnp.transpose(total, (2, 3, 0, 1))[:, :, None]

time: 84.8 us -> 85.6 us (level)
  blocking collectives: 10.1 us -> 0 us
  waiting for transfers between devices: 14.2 us -> 20.5 us
  starting transfers between devices: 28.8 us -> 32.8 us
    all_to_all x1 -> x0, blocking collectives: 10.1 us -> none  [local(): every = jnp.sum(lax.all_to_all(every, 'vert', 0, 0), axis=0)]
    all_to_all x0 -> x1, waiting for transfers between devices: none -> 6.25 us  [local(): every = jnp.sum(lax.all_to_all(every, 'vert', 0, 0), axis=0)]
    all_to_all x0 -> x1, starting transfers between devices: none -> 4 us  [local(): every = jnp.sum(lax.all_to_all(every, 'vert', 0, 0), axis=0)]
  transfers between devices with their start and end apart: 14 -> 15, of which waited for: 8 -> 9; matrix products, arithmetic and copies ran while one was open for 1% -> 1% of each run, Pallas kernels for 16% -> 16%
where the time goes in v7:
time: 85.6 us; the launch traced here: 85 us
  starting transfers between devices  32.8 us (38%)
  Pallas kernels  27.8 us (32%)
  waiting for transfers between devices  20.5 us (24%)
  local copies, waits for them, and re-layouts  2.31 us (3%)
  other arithmetic  1.58 us (2%)
    ppermute x14, starting transfers between devices, permute(): return lax.ppermute(value, AXES, pairs)  28.8 us
    pallas_call x2, Pallas kernels, ladder(): pl.pallas_call(kernel, out_shape=[jax.ShapeDtypeStruct((IRREPS, WB, VB),...  27.8 us
    ppermute x14, waiting for transfers between devices, permute(): return lax.ppermute(value, AXES, pairs)  14.2 us
    all_to_all x1, waiting for transfers between devices, local(): every = jnp.sum(lax.all_to_all(every, 'vert', 0, 0), axis=0)  6.25 us
    all_to_all x1, starting transfers between devices, local(): every = jnp.sum(lax.all_to_all(every, 'vert', 0, 0), axis=0)  4 us
  transfers between devices with their start and end apart: 15, of which 9 were waited for; matrix products, arithmetic and copies ran while one was open for 1% of the time, Pallas kernels for 16%

profile of v7, /device:TPU:4, one launch (start us, length us, event | category | flops | bytes accessed | tf_op | source)
XLA Modules:
  0.0 85.0 jit_solution(13436529821282570502)
XLA Ops:
  0.0 0.0 copy-start
  0.0 0.9 %copy-done = bf16[1,256,4,128]{3,2,1,0:T(4,128)(2,1)S(1)} copy-done((bf16[1,256,4,128]{3,2,1,0:T(4,128)(2,1)S(1)}, bf16[1,256,4,128]{3,2,1,0:T(4,128)(2,1)}, u32[]{:S(2)}) %copy-start) | copy-done | bytes 262168
  1.0 0.1 constant_dynamic-slice_fusion
  1.1 0.1 copy.5
  1.2 1.7 %collective-permute-start = (bf16[128,256]{1,0:T(8,128)(2,1)S(1)}, bf16[128,256]{1,0:T(8,128)(2,1)S(1)}, u32[]{:S(2)}, u32[]{:S(2)}) collective-permute-start(bf16[128,256]{1,0:T(8,128)(2,1)S(1)} %bitcast.30), channel_id=1, source_target_pairs={{0,1},{1,0},{2,3},{3,2},{4,5},{5,4},{6,7},{7,6},{8,9},{9,8},{10,11... | collective-permute-start | bytes 196616 | tf_op jit(solution)/shard_map/ppermute | solution.py:321
  2.9 2.7 %collective-permute-done = bf16[128,256]{1,0:T(8,128)(2,1)S(1)} collective-permute-done((bf16[128,256]{1,0:T(8,128)(2,1)S(1)}, bf16[128,256]{1,0:T(8,128)(2,1)S(1)}, u32[]{:S(2)}, u32[]{:S(2)}) %collective-permute-start) | collective-permute-done | bytes 65568 | tf_op jit(solution)/shard_map/ppermute | solution.py:321
  5.6 9.9 %collective-permute-start.1 = (bf16[2,128,256]{2,1,0:T(8,128)(2,1)S(1)}, bf16[2,128,256]{2,1,0:T(8,128)(2,1)S(1)}, u32[]{:S(2)}, u32[]{:S(2)}) collective-permute-start(bf16[2,128,256]{2,1,0:T(8,128)(2,1)S(1)} %pad_maximum_fusion.2), channel_id=1, source_target_pairs={{2,0},{19,1},{32,2},{49,3},{42,4},{59,5},{8,6},{25,7},{6,8},{23,9}... | collective-permute-start | bytes 393224 | tf_op jit(solution)/shard_map/ppermute | solution.py:321
  15.5 0.7 broadcast_and_fusion.occ_ref
  16.1 0.7 collective-permute-start.2
  16.8 3.1 %collective-permute-done.1.refs_1_ = bf16[2,128,256]{2,1,0:T(8,128)(2,1)S(1)} collective-permute-done((bf16[2,128,256]{2,1,0:T(8,128)(2,1)S(1)}, bf16[2,128,256]{2,1,0:T(8,128)(2,1)S(1)}, u32[]{:S(2)}, u32[]{:S(2)}) %collective-permute-start.1) | collective-permute-done | bytes 131104 | tf_op jit(solution)/shard_map/ppermute | solution.py:321
  20.0 1.2 %collective-permute-start.9 = (bf16[2,128,256]{2,1,0:T(8,128)(2,1)S(1)}, bf16[2,128,256]{2,1,0:T(8,128)(2,1)S(1)}, u32[]{:S(2)}, u32[]{:S(2)}) collective-permute-start(bf16[2,128,256]{2,1,0:T(8,128)(2,1)S(1)} %collective-permute-done.1.refs_1_), channel_id=1, source_target_pairs={{0,64},{1,65},{2,66},{3,67},{4,68},{5,69},{6,70},{7,71},{8,72},{9,... | collective-permute-start | bytes 393224 | tf_op jit(solution)/shard_map/ppermute | solution.py:321
  21.1 0.8 collective-permute-start.6
  22.0 0.0 collective-permute-done.2.refs_0_
  22.0 0.5 collective-permute-start.5
  22.5 1.5 %collective-permute-start.7 = (bf16[2,128,256]{2,1,0:T(8,128)(2,1)S(1)}, bf16[2,128,256]{2,1,0:T(8,128)(2,1)S(1)}, u32[]{:S(2)}, u32[]{:S(2)}) collective-permute-start(bf16[2,128,256]{2,1,0:T(8,128)(2,1)S(1)} %collective-permute-done.2.refs_0_), channel_id=1, source_target_pairs={{0,64},{1,65},{2,66},{3,67},{4,68},{5,69},{6,70},{7,71},{8,72},{9,... | collective-permute-start | bytes 393224 | tf_op jit(solution)/shard_map/ppermute | solution.py:321
  24.0 0.9 %collective-permute-done.9.refs_9_ = bf16[2,128,256]{2,1,0:T(8,128)(2,1)S(1)} collective-permute-done((bf16[2,128,256]{2,1,0:T(8,128)(2,1)S(1)}, bf16[2,128,256]{2,1,0:T(8,128)(2,1)S(1)}, u32[]{:S(2)}, u32[]{:S(2)}) %collective-permute-start.9) | collective-permute-done | bytes 131104 | tf_op jit(solution)/shard_map/ppermute | solution.py:321
  24.9 1.2 %collective-permute-done.6.refs_5_ = bf16[2,128,256]{2,1,0:T(8,128)(2,1)S(1)} collective-permute-done((bf16[2,128,256]{2,1,0:T(8,128)(2,1)S(1)}, bf16[2,128,256]{2,1,0:T(8,128)(2,1)S(1)}, u32[]{:S(2)}, u32[]{:S(2)}) %collective-permute-start.6) | collective-permute-done | bytes 131104 | tf_op jit(solution)/shard_map/ppermute | solution.py:321
  26.1 0.1 collective-permute-start.10
  26.2 2.1 %collective-permute-done.5.refs_4_ = bf16[2,128,256]{2,1,0:T(8,128)(2,1)S(1)} collective-permute-done((bf16[2,128,256]{2,1,0:T(8,128)(2,1)S(1)}, bf16[2,128,256]{2,1,0:T(8,128)(2,1)S(1)}, u32[]{:S(2)}, u32[]{:S(2)}) %collective-permute-start.5) | collective-permute-done | bytes 131104 | tf_op jit(solution)/shard_map/ppermute | solution.py:321
  28.4 0.0 collective-permute-done.7.refs_8_
  28.4 0.5 collective-permute-start.8
  28.9 0.1 collective-permute-start.4
  29.0 0.4 collective-permute-start.3
  29.4 0.0 collective-permute-done.10
  29.4 0.6 collective-permute-done.8
  30.1 0.1 maximum_select_fusion
  30.2 2.0 %collective-permute-start.11 = (bf16[4,2,128,256]{3,2,1,0:T(8,128)(2,1)S(1)}, bf16[4,2,128,256]{3,2,1,0:T(8,128)(2,1)S(1)}, u32[]{:S(2)}, u32[]{:S(2)}) collective-permute-start(bf16[4,2,128,256]{3,2,1,0:T(8,128)(2,1)S(1)} %maximum_select_fusion), channel_id=1, source_target_pairs={{0,192},{1,193},{2,194},{3,195},{4,196},{5,197},{6,198},{7,199},{8... | collective-permute-start | bytes 1572872 | tf_op jit(solution)/shard_map/ppermute | solution.py:321
  32.2 0.0 collective-permute-done.4.refs_3_
  32.2 0.0 collective-permute-done.3.refs_2_
  32.2 13.6 %shard_map.37 = (f32[8,4,128]{2,1,0:T(4,128)S(1)}, f32[8,4,128]{2,1,0:T(4,128)S(1)}) custom-call(s32[32]{0:T(128)S(1)} %broadcast_and_fusion.occ_ref, bf16[32,8,128,128]{3,2,1,0:T(8,128)(2,1)} %bitcast.34, bf16[2,128,256]{2,1,0:T(8,128)(2,1)S(1)} %collective-permute-done.2.refs_0_, bf16[2,128,256]{2,1,0:T(8,128)(2,1)S(1)} %collective-permute-done.1.refs_1_, ...), custom_call_target="tpu_custom_call" | custom-call | flops 8000000000 | bytes 12000000 | tf_op jit(solution)/shard_map/pallas_call | solution.py:289
  45.8 0.0 collective-permute-done.11.refs_12_
  45.8 14.1 %shard_map.38 = (f32[8,4,128]{2,1,0:T(4,128)S(1)}, f32[8,4,128]{2,1,0:T(4,128)S(1)}) custom-call(s32[32]{0:T(128)S(1)} %broadcast_and_fusion.occ_ref, bf16[32,8,128,128]{3,2,1,0:T(8,128)(2,1)} %bitcast.35, f32[8,4,128]{2,1,0:T(4,128)S(1)} %get-tuple-element.13.own_in, f32[8,4,128]{2,1,0:T(4,128)S(1)} %get-tuple-element.14.mirror_in, ...), custom_call_target="tpu_custom_call" | custom-call | flops 8000000000 | bytes 12000000 | tf_op jit(solution)/shard_map/pallas_call | solution.py:289
  60.0 0.6 pad_maximum_fusion.3
  60.6 4.0 %all-to-all-start = ((f32[8,8,128]{2,1,0:T(8,128)}), f32[8,8,128]{2,1,0:T(8,128)S(1)}, u32[]{:S(2)}, u32[]{:S(2)}) async-start(f32[8,8,128]{2,1,0:T(8,128)} %pad_maximum_fusion.3), calls=%async_computation | async-start | bytes 65536 | tf_op jit(solution)/shard_map/all_to_all | solution.py:343
  64.6 6.3 %all-to-all-done = f32[8,8,128]{2,1,0:T(8,128)S(1)} async-done(((f32[8,8,128]{2,1,0:T(8,128)}), f32[8,8,128]{2,1,0:T(8,128)S(1)}, u32[]{:S(2)}, u32[]{:S(2)}) %all-to-all-start) | async-done | bytes 32800 | tf_op jit(solution)/shard_map/all_to_all | solution.py:343
  70.9 0.1 collective-permute-start.12
  71.0 1.1 %collective-permute-done.12 = f32[4,128]{1,0:T(4,128)S(1)} collective-permute-done((f32[4,128]{1,0:T(4,128)S(1)}, f32[4,128]{1,0:T(4,128)S(1)}, u32[]{:S(2)}, u32[]{:S(2)}) %collective-permute-start.12) | collective-permute-done | bytes 2080 | tf_op jit(solution)/shard_map/ppermute | solution.py:321
  72.1 0.1 fusion.4
  72.2 0.1 fusion.5
  72.3 0.1 fusion
  72.3 9.4 %collective-permute-start.13 = (f32[4,128]{1,0:T(4,128)S(1)}, f32[4,128]{1,0:T(4,128)S(1)}, u32[]{:S(2)}, u32[]{:S(2)}) collective-permute-start(f32[4,128]{1,0:T(4,128)S(1)} %fusion), channel_id=1, source_target_pairs={{0,0},{1,1},{2,2},{3,3},{4,4},{5,5},{6,6},{7,7},{8,8},{9,9},{10,10... | collective-permute-start | bytes 6152 | tf_op jit(solution)/shard_map/ppermute | solution.py:321
  81.7 2.4 %collective-permute-done.13 = f32[4,128]{1,0:T(4,128)S(1)} collective-permute-done((f32[4,128]{1,0:T(4,128)S(1)}, f32[4,128]{1,0:T(4,128)S(1)}, u32[]{:S(2)}, u32[]{:S(2)}) %collective-permute-start.13) | collective-permute-done | bytes 2080 | tf_op jit(solution)/shard_map/ppermute | solution.py:321
  84.1 0.1 reshape.68
  84.2 0.8 copy.6
  (10 shorter events, 0.2 us)
Async XLA Ops:
  0.0 1.0 %copy-start = (bf16[1,256,4,128]{3,2,1,0:T(4,128)(2,1)S(1)}, bf16[1,256,4,128]{3,2,1,0:T(4,128)(2,1)}, u32[]{:S(2)}) copy-start(bf16[1,256,4,128]{3,2,1,0:T(4,128)(2,1)} %param.4) | copy-start | bytes 786436
  1.2 4.4 %collective-permute-start = (bf16[128,256]{1,0:T(8,128)(2,1)S(1)}, bf16[128,256]{1,0:T(8,128)(2,1)S(1)}, u32[]{:S(2)}, u32[]{:S(2)}) collective-permute-start(bf16[128,256]{1,0:T(8,128)(2,1)S(1)} %bitcast.30), channel_id=1, source_target_pairs={{0,1},{1,0},{2,3},{3,2},{4,5},{5,4},{6,7},{7,6},{8,9},{9,8},{10,11... | collective-permute-start | bytes 196616 | tf_op jit(solution)/shard_map/ppermute | solution.py:321
  5.6 14.4 %collective-permute-start.1 = (bf16[2,128,256]{2,1,0:T(8,128)(2,1)S(1)}, bf16[2,128,256]{2,1,0:T(8,128)(2,1)S(1)}, u32[]{:S(2)}, u32[]{:S(2)}) collective-permute-start(bf16[2,128,256]{2,1,0:T(8,128)(2,1)S(1)} %pad_maximum_fusion.2), channel_id=1, source_target_pairs={{2,0},{19,1},{32,2},{49,3},{42,4},{59,5},{8,6},{25,7},{6,8},{23,9}... | collective-permute-start | bytes 393224 | tf_op jit(solution)/shard_map/ppermute | solution.py:321
  16.1 5.8 %collective-permute-start.2 = (bf16[2,128,256]{2,1,0:T(8,128)(2,1)S(1)}, bf16[2,128,256]{2,1,0:T(8,128)(2,1)S(1)}, u32[]{:S(2)}, u32[]{:S(2)}) collective-permute-start(bf16[2,128,256]{2,1,0:T(8,128)(2,1)S(1)} %pad_maximum_fusion.2), channel_id=1, source_target_pairs={{0,0},{17,1},{34,2},{51,3},{40,4},{57,5},{10,6},{27,7},{4,8},{21,9... | collective-permute-start | bytes 393224 | tf_op jit(solution)/shard_map/ppermute | solution.py:321
  20.0 5.0 %collective-permute-start.9 = (bf16[2,128,256]{2,1,0:T(8,128)(2,1)S(1)}, bf16[2,128,256]{2,1,0:T(8,128)(2,1)S(1)}, u32[]{:S(2)}, u32[]{:S(2)}) collective-permute-start(bf16[2,128,256]{2,1,0:T(8,128)(2,1)S(1)} %collective-permute-done.1.refs_1_), channel_id=1, source_target_pairs={{0,64},{1,65},{2,66},{3,67},{4,68},{5,69},{6,70},{7,71},{8,72},{9,... | collective-permute-start | bytes 393224 | tf_op jit(solution)/shard_map/ppermute | solution.py:321
  21.1 5.0 %collective-permute-start.6 = (bf16[2,128,256]{2,1,0:T(8,128)(2,1)S(1)}, bf16[2,128,256]{2,1,0:T(8,128)(2,1)S(1)}, u32[]{:S(2)}, u32[]{:S(2)}) collective-permute-start(bf16[2,128,256]{2,1,0:T(8,128)(2,1)S(1)} %collective-permute-done.1.refs_1_), channel_id=1, source_target_pairs={{0,192},{1,193},{2,194},{3,195},{4,196},{5,197},{6,198},{7,199},{8... | collective-permute-start | bytes 393224 | tf_op jit(solution)/shard_map/ppermute | solution.py:321
  22.0 6.4 %collective-permute-start.5 = (bf16[2,128,256]{2,1,0:T(8,128)(2,1)S(1)}, bf16[2,128,256]{2,1,0:T(8,128)(2,1)S(1)}, u32[]{:S(2)}, u32[]{:S(2)}) collective-permute-start(bf16[2,128,256]{2,1,0:T(8,128)(2,1)S(1)} %collective-permute-done.2.refs_0_), channel_id=1, source_target_pairs={{0,192},{1,193},{2,194},{3,195},{4,196},{5,197},{6,198},{7,199},{8... | collective-permute-start | bytes 393224 | tf_op jit(solution)/shard_map/ppermute | solution.py:321
  22.5 5.8 %collective-permute-start.7 = (bf16[2,128,256]{2,1,0:T(8,128)(2,1)S(1)}, bf16[2,128,256]{2,1,0:T(8,128)(2,1)S(1)}, u32[]{:S(2)}, u32[]{:S(2)}) collective-permute-start(bf16[2,128,256]{2,1,0:T(8,128)(2,1)S(1)} %collective-permute-done.2.refs_0_), channel_id=1, source_target_pairs={{0,64},{1,65},{2,66},{3,67},{4,68},{5,69},{6,70},{7,71},{8,72},{9,... | collective-permute-start | bytes 393224 | tf_op jit(solution)/shard_map/ppermute | solution.py:321
  26.1 3.2 %collective-permute-start.10 = (bf16[2,2,128,256]{3,2,1,0:T(8,128)(2,1)S(1)}, bf16[2,2,128,256]{3,2,1,0:T(8,128)(2,1)S(1)}, u32[]{:S(2)}, u32[]{:S(2)}) collective-permute-start(bf16[2,2,128,256]{3,2,1,0:T(8,128)(2,1)S(1)} %pad_maximum_fusion.1), channel_id=1, source_target_pairs={{0,8},{1,9},{2,10},{3,11},{4,12},{5,13},{6,14},{7,15},{8,0},{9,1},... | collective-permute-start | bytes 786440 | tf_op jit(solution)/shard_map/ppermute | solution.py:321
  28.4 1.6 %collective-permute-start.8 = (bf16[2,2,128,256]{3,2,1,0:T(8,128)(2,1)S(1)}, bf16[2,2,128,256]{3,2,1,0:T(8,128)(2,1)S(1)}, u32[]{:S(2)}, u32[]{:S(2)}) collective-permute-start(bf16[2,2,128,256]{3,2,1,0:T(8,128)(2,1)S(1)} %pad_maximum_fusion), channel_id=1, source_target_pairs={{0,8},{1,9},{2,10},{3,11},{4,12},{5,13},{6,14},{7,15},{8,0},{9,1},... | collective-permute-start | bytes 786440 | tf_op jit(solution)/shard_map/ppermute | solution.py:321
  28.9 3.3 %collective-permute-start.4 = (bf16[2,128,256]{2,1,0:T(8,128)(2,1)S(1)}, bf16[2,128,256]{2,1,0:T(8,128)(2,1)S(1)}, u32[]{:S(2)}, u32[]{:S(2)}) collective-permute-start(bf16[2,128,256]{2,1,0:T(8,128)(2,1)S(1)} %collective-permute-done.1.refs_1_), channel_id=1, source_target_pairs={{0,8},{1,9},{2,10},{3,11},{4,12},{5,13},{6,14},{7,15},{8,0},{9,1},... | collective-permute-start | bytes 393224 | tf_op jit(solution)/shard_map/ppermute | solution.py:321
  29.0 3.2 %collective-permute-start.3 = (bf16[2,128,256]{2,1,0:T(8,128)(2,1)S(1)}, bf16[2,128,256]{2,1,0:T(8,128)(2,1)S(1)}, u32[]{:S(2)}, u32[]{:S(2)}) collective-permute-start(bf16[2,128,256]{2,1,0:T(8,128)(2,1)S(1)} %collective-permute-done.2.refs_0_), channel_id=1, source_target_pairs={{0,8},{1,9},{2,10},{3,11},{4,12},{5,13},{6,14},{7,15},{8,0},{9,1},... | collective-permute-start | bytes 393224 | tf_op jit(solution)/shard_map/ppermute | solution.py:321
  30.2 15.6 %collective-permute-start.11 = (bf16[4,2,128,256]{3,2,1,0:T(8,128)(2,1)S(1)}, bf16[4,2,128,256]{3,2,1,0:T(8,128)(2,1)S(1)}, u32[]{:S(2)}, u32[]{:S(2)}) collective-permute-start(bf16[4,2,128,256]{3,2,1,0:T(8,128)(2,1)S(1)} %maximum_select_fusion), channel_id=1, source_target_pairs={{0,192},{1,193},{2,194},{3,195},{4,196},{5,197},{6,198},{7,199},{8... | collective-permute-start | bytes 1572872 | tf_op jit(solution)/shard_map/ppermute | solution.py:321
  60.6 10.3 %all-to-all-start = ((f32[8,8,128]{2,1,0:T(8,128)}), f32[8,8,128]{2,1,0:T(8,128)S(1)}, u32[]{:S(2)}, u32[]{:S(2)}) async-start(f32[8,8,128]{2,1,0:T(8,128)} %pad_maximum_fusion.3), calls=%async_computation | async-start | bytes 65536 | tf_op jit(solution)/shard_map/all_to_all | solution.py:343
  70.9 1.2 %collective-permute-start.12 = (f32[4,128]{1,0:T(4,128)S(1)}, f32[4,128]{1,0:T(4,128)S(1)}, u32[]{:S(2)}, u32[]{:S(2)}) collective-permute-start(f32[4,128]{1,0:T(4,128)S(1)} %slice.39), channel_id=1, source_target_pairs={{0,8},{1,9},{2,10},{3,11},{4,12},{5,13},{6,14},{7,15},{8,0},{9,1},... | collective-permute-start | bytes 6152 | tf_op jit(solution)/shard_map/ppermute | solution.py:321
  72.3 11.8 %collective-permute-start.13 = (f32[4,128]{1,0:T(4,128)S(1)}, f32[4,128]{1,0:T(4,128)S(1)}, u32[]{:S(2)}, u32[]{:S(2)}) collective-permute-start(f32[4,128]{1,0:T(4,128)S(1)} %fusion), channel_id=1, source_target_pairs={{0,0},{1,1},{2,2},{3,3},{4,4},{5,5},{6,6},{7,7},{8,8},{9,9},{10,10... | collective-permute-start | bytes 6152 | tf_op jit(solution)/shard_map/ppermute | solution.py:321

commit v8 on v6

--- a/solution.py
+++ b/solution.py
@@ -325,9 +325,10 @@
     mine = lax.dynamic_index_in_dim(chol[0], x, 1, False).T
     pair = jnp.stack([mine, permute(mine, moved_pairs(next_row))])
     near = [permute(pair, fetch_pairs(row)) for row in (0, 2)]
-    near[1], labels = lax.optimization_barrier((near[1], jnp.bitwise_and(occ_irrep, IRREPS - 1)))
     above = [permute(half, moved_pairs(lower)) for half in near]
     below = [permute(half, moved_pairs(upper)) for half in near]
+    labels = jnp.bitwise_and(occ_irrep, IRREPS - 1)
+    above[1], labels = lax.optimization_barrier((above[1], labels))
     swap = moved_pairs(other_core)
     beside = [permute(jnp.stack([above[far], below[far]]), swap) for far in range(2)]
     pieces = near + [permute(half, swap) for half in near]

time: 84.8 us -> 86.7 us (1.022); the launches traced: 84.3 us -> 85.3 us
  starting transfers between devices: 28.8 us -> 31.3 us
  blocking collectives: 10.1 us -> 9.17 us
    ppermute x14, starting transfers between devices: 28.8 us -> 31.3 us  [permute(): return lax.ppermute(value, AXES, pairs)]
    all_to_all x1, blocking collectives: 10.1 us -> 9.17 us  [local(): every = jnp.sum(lax.all_to_all(every, 'vert', 0, 0), axis=0)]
where the time goes in v8:
time: 86.7 us; the launch traced here: 85.3 us
  starting transfers between devices  31.3 us (36%)
  Pallas kernels  27.9 us (32%)
  waiting for transfers between devices  13.6 us (16%)
  blocking collectives  9.17 us (11%)
  local copies, waits for them, and re-layouts  2.17 us (3%)
  other arithmetic  0.89 us (1%)
    ppermute x14, starting transfers between devices, permute(): return lax.ppermute(value, AXES, pairs)  31.3 us
    pallas_call x2, Pallas kernels, ladder(): pl.pallas_call(kernel, out_shape=[jax.ShapeDtypeStruct((IRREPS, WB, VB),...  27.9 us
    ppermute x14, waiting for transfers between devices, permute(): return lax.ppermute(value, AXES, pairs)  13.6 us
    all_to_all x1, blocking collectives, local(): every = jnp.sum(lax.all_to_all(every, 'vert', 0, 0), axis=0)  9.17 us
  transfers between devices with their start and end apart: 14, of which 8 were waited for; matrix products, arithmetic and copies ran while one was open for 1% of the time, Pallas kernels for 16%

profile of v8, /device:TPU:4, one launch (start us, length us, event | category | flops | bytes accessed | tf_op | source)
XLA Modules:
  0.0 85.3 jit_solution(5099040245426265513)
XLA Ops:
  0.0 0.0 copy-start
  0.0 0.9 %copy-done = bf16[1,256,4,128]{3,2,1,0:T(4,128)(2,1)S(1)} copy-done((bf16[1,256,4,128]{3,2,1,0:T(4,128)(2,1)S(1)}, bf16[1,256,4,128]{3,2,1,0:T(4,128)(2,1)}, u32[]{:S(2)}) %copy-start) | copy-done | bytes 262168
  1.0 0.1 constant_dynamic-slice_fusion
  1.1 0.1 copy.5
  1.2 1.7 %collective-permute-start = (bf16[128,256]{1,0:T(8,128)(2,1)S(1)}, bf16[128,256]{1,0:T(8,128)(2,1)S(1)}, u32[]{:S(2)}, u32[]{:S(2)}) collective-permute-start(bf16[128,256]{1,0:T(8,128)(2,1)S(1)} %bitcast.34), channel_id=1, source_target_pairs={{0,1},{1,0},{2,3},{3,2},{4,5},{5,4},{6,7},{7,6},{8,9},{9,8},{10,11... | collective-permute-start | bytes 196616 | tf_op jit(solution)/shard_map/ppermute | solution.py:323
  2.9 2.7 %collective-permute-done = bf16[128,256]{1,0:T(8,128)(2,1)S(1)} collective-permute-done((bf16[128,256]{1,0:T(8,128)(2,1)S(1)}, bf16[128,256]{1,0:T(8,128)(2,1)S(1)}, u32[]{:S(2)}, u32[]{:S(2)}) %collective-permute-start) | collective-permute-done | bytes 65568 | tf_op jit(solution)/shard_map/ppermute | solution.py:323
  5.6 9.9 %collective-permute-start.1 = (bf16[2,128,256]{2,1,0:T(8,128)(2,1)S(1)}, bf16[2,128,256]{2,1,0:T(8,128)(2,1)S(1)}, u32[]{:S(2)}, u32[]{:S(2)}) collective-permute-start(bf16[2,128,256]{2,1,0:T(8,128)(2,1)S(1)} %pad_maximum_fusion.2), channel_id=1, source_target_pairs={{2,0},{19,1},{32,2},{49,3},{42,4},{59,5},{8,6},{25,7},{6,8},{23,9}... | collective-permute-start | bytes 393224 | tf_op jit(solution)/shard_map/ppermute | solution.py:323
  15.5 0.7 collective-permute-start.3
  16.1 3.8 %collective-permute-done.1.refs_1_ = bf16[2,128,256]{2,1,0:T(8,128)(2,1)S(1)} collective-permute-done((bf16[2,128,256]{2,1,0:T(8,128)(2,1)S(1)}, bf16[2,128,256]{2,1,0:T(8,128)(2,1)S(1)}, u32[]{:S(2)}, u32[]{:S(2)}) %collective-permute-start.1) | collective-permute-done | bytes 131104 | tf_op jit(solution)/shard_map/ppermute | solution.py:323
  20.0 0.5 collective-permute-start.2
  20.5 1.5 %collective-permute-start.9 = (bf16[2,128,256]{2,1,0:T(8,128)(2,1)S(1)}, bf16[2,128,256]{2,1,0:T(8,128)(2,1)S(1)}, u32[]{:S(2)}, u32[]{:S(2)}) collective-permute-start(bf16[2,128,256]{2,1,0:T(8,128)(2,1)S(1)} %collective-permute-done.1.refs_1_), channel_id=1, source_target_pairs={{0,64},{1,65},{2,66},{3,67},{4,68},{5,69},{6,70},{7,71},{8,72},{9,... | collective-permute-start | bytes 393224 | tf_op jit(solution)/shard_map/ppermute | solution.py:323
  22.0 0.7 broadcast_and_fusion.occ_ref
  22.6 0.0 collective-permute-done.3.refs_0_
  22.6 0.5 collective-permute-start.6
  23.2 1.9 %collective-permute-start.7 = (bf16[2,128,256]{2,1,0:T(8,128)(2,1)S(1)}, bf16[2,128,256]{2,1,0:T(8,128)(2,1)S(1)}, u32[]{:S(2)}, u32[]{:S(2)}) collective-permute-start(bf16[2,128,256]{2,1,0:T(8,128)(2,1)S(1)} %collective-permute-done.3.refs_0_), channel_id=1, source_target_pairs={{0,64},{1,65},{2,66},{3,67},{4,68},{5,69},{6,70},{7,71},{8,72},{9,... | collective-permute-start | bytes 393224 | tf_op jit(solution)/shard_map/ppermute | solution.py:323
  25.1 0.0 collective-permute-done.2.refs_5_
  25.1 0.4 collective-permute-done.9.refs_9_
  25.5 0.1 collective-permute-start.10
  25.6 2.9 %collective-permute-done.6.refs_4_ = bf16[2,128,256]{2,1,0:T(8,128)(2,1)S(1)} collective-permute-done((bf16[2,128,256]{2,1,0:T(8,128)(2,1)S(1)}, bf16[2,128,256]{2,1,0:T(8,128)(2,1)S(1)}, u32[]{:S(2)}, u32[]{:S(2)}) %collective-permute-start.6) | collective-permute-done | bytes 131104 | tf_op jit(solution)/shard_map/ppermute | solution.py:323
  28.5 0.3 collective-permute-done.7.refs_8_
  28.8 0.1 collective-permute-start.8
  28.9 0.5 collective-permute-start.4
  29.4 0.1 collective-permute-start.5
  29.5 0.0 collective-permute-done.10
  29.5 0.9 %collective-permute-done.8 = bf16[2,2,128,256]{3,2,1,0:T(8,128)(2,1)S(1)} collective-permute-done((bf16[2,2,128,256]{3,2,1,0:T(8,128)(2,1)S(1)}, bf16[2,2,128,256]{3,2,1,0:T(8,128)(2,1)S(1)}, u32[]{:S(2)}, u32[]{:S(2)}) %collective-permute-start.8) | collective-permute-done | bytes 262176 | tf_op jit(solution)/shard_map/ppermute | solution.py:323
  30.4 0.1 maximum_select_fusion
  30.6 2.1 %collective-permute-start.11 = (bf16[4,2,128,256]{3,2,1,0:T(8,128)(2,1)S(1)}, bf16[4,2,128,256]{3,2,1,0:T(8,128)(2,1)S(1)}, u32[]{:S(2)}, u32[]{:S(2)}) collective-permute-start(bf16[4,2,128,256]{3,2,1,0:T(8,128)(2,1)S(1)} %maximum_select_fusion), channel_id=1, source_target_pairs={{0,192},{1,193},{2,194},{3,195},{4,196},{5,197},{6,198},{7,199},{8... | collective-permute-start | bytes 1572872 | tf_op jit(solution)/shard_map/ppermute | solution.py:323
  32.7 0.0 collective-permute-done.4.refs_2_
  32.7 0.0 collective-permute-done.5.refs_3_
  32.7 13.7 %shard_map.37 = (f32[8,4,128]{2,1,0:T(4,128)S(1)}, f32[2,8,4,128]{3,2,1,0:T(4,128)S(1)}) custom-call(s32[32]{0:T(128)S(1)} %broadcast_and_fusion.occ_ref, bf16[32,8,128,128]{3,2,1,0:T(8,128)(2,1)} %bitcast.38, bf16[2,128,256]{2,1,0:T(8,128)(2,1)S(1)} %collective-permute-done.3.refs_0_, bf16[2,128,256]{2,1,0:T(8,128)(2,1)S(1)} %collective-permute-done.1.refs_1_, ...), custom_call_target="tpu_custom_call" | custom-call | flops 8000000000 | bytes 12000000 | tf_op jit(solution)/shard_map/pallas_call | solution.py:291
  46.4 0.0 collective-permute-done.11.refs_12_
  46.4 14.2 %shard_map.38 = (f32[8,4,128]{2,1,0:T(4,128)S(1)}, f32[2,8,4,128]{3,2,1,0:T(4,128)S(1)}) custom-call(s32[32]{0:T(128)S(1)} %broadcast_and_fusion.occ_ref, bf16[32,8,128,128]{3,2,1,0:T(8,128)(2,1)} %bitcast.39, f32[8,4,128]{2,1,0:T(4,128)S(1)} %get-tuple-element.13.own_in, f32[2,8,4,128]{3,2,1,0:T(4,128)S(1)} %get-tuple-element.14.mirror_in, ...), custom_call_target="tpu_custom_call" | custom-call | flops 8000000000 | bytes 12000000 | tf_op jit(solution)/shard_map/pallas_call | solution.py:291
  60.7 9.2 %all_to_all.5 = f32[8,12,128]{2,1,0:T(8,128)S(1)} all-to-all(f32[8,12,128]{2,1,0:T(8,128)S(1)} %pad_maximum_fusion.3), channel_id=1, replica_groups=mesh['oi'=4,'oj'=8,'vert'=8] {'vert'}, dimensions={0} | all-to-all | bytes 98304 | tf_op jit(solution)/shard_map/all_to_all | solution.py:346
  69.9 0.1 collective-permute-start.12
  70.0 1.1 %collective-permute-done.12 = f32[4,128]{1,0:T(4,128)S(1)} collective-permute-done((f32[4,128]{1,0:T(4,128)S(1)}, f32[4,128]{1,0:T(4,128)S(1)}, u32[]{:S(2)}, u32[]{:S(2)}) %collective-permute-start.12) | collective-permute-done | bytes 2080 | tf_op jit(solution)/shard_map/ppermute | solution.py:323
  71.1 11.7 %collective-permute-start.13 = (f32[4,128]{1,0:T(4,128)S(1)}, f32[4,128]{1,0:T(4,128)S(1)}, u32[]{:S(2)}, u32[]{:S(2)}) collective-permute-start(f32[4,128]{1,0:T(4,128)S(1)} %slice_add_fusion), channel_id=1, source_target_pairs={{0,0},{1,1},{2,2},{3,3},{4,4},{5,5},{6,6},{7,7},{8,8},{9,9},{10,10... | collective-permute-start | bytes 6152 | tf_op jit(solution)/shard_map/ppermute | solution.py:323
  82.8 1.5 %collective-permute-done.13 = f32[4,128]{1,0:T(4,128)S(1)} collective-permute-done((f32[4,128]{1,0:T(4,128)S(1)}, f32[4,128]{1,0:T(4,128)S(1)}, u32[]{:S(2)}, u32[]{:S(2)}) %collective-permute-start.13) | collective-permute-done | bytes 2080 | tf_op jit(solution)/shard_map/ppermute | solution.py:323
  84.4 0.1 reshape.9
  84.5 0.8 copy.6
  (11 shorter events, 0.2 us)
Async XLA Ops:
  0.0 1.0 %copy-start = (bf16[1,256,4,128]{3,2,1,0:T(4,128)(2,1)S(1)}, bf16[1,256,4,128]{3,2,1,0:T(4,128)(2,1)}, u32[]{:S(2)}) copy-start(bf16[1,256,4,128]{3,2,1,0:T(4,128)(2,1)} %param.4) | copy-start | bytes 786436
  1.2 4.4 %collective-permute-start = (bf16[128,256]{1,0:T(8,128)(2,1)S(1)}, bf16[128,256]{1,0:T(8,128)(2,1)S(1)}, u32[]{:S(2)}, u32[]{:S(2)}) collective-permute-start(bf16[128,256]{1,0:T(8,128)(2,1)S(1)} %bitcast.34), channel_id=1, source_target_pairs={{0,1},{1,0},{2,3},{3,2},{4,5},{5,4},{6,7},{7,6},{8,9},{9,8},{10,11... | collective-permute-start | bytes 196616 | tf_op jit(solution)/shard_map/ppermute | solution.py:323
  5.6 14.4 %collective-permute-start.1 = (bf16[2,128,256]{2,1,0:T(8,128)(2,1)S(1)}, bf16[2,128,256]{2,1,0:T(8,128)(2,1)S(1)}, u32[]{:S(2)}, u32[]{:S(2)}) collective-permute-start(bf16[2,128,256]{2,1,0:T(8,128)(2,1)S(1)} %pad_maximum_fusion.2), channel_id=1, source_target_pairs={{2,0},{19,1},{32,2},{49,3},{42,4},{59,5},{8,6},{25,7},{6,8},{23,9}... | collective-permute-start | bytes 393224 | tf_op jit(solution)/shard_map/ppermute | solution.py:323
  15.5 7.2 %collective-permute-start.3 = (bf16[2,128,256]{2,1,0:T(8,128)(2,1)S(1)}, bf16[2,128,256]{2,1,0:T(8,128)(2,1)S(1)}, u32[]{:S(2)}, u32[]{:S(2)}) collective-permute-start(bf16[2,128,256]{2,1,0:T(8,128)(2,1)S(1)} %pad_maximum_fusion.2), channel_id=1, source_target_pairs={{0,0},{17,1},{34,2},{51,3},{40,4},{57,5},{10,6},{27,7},{4,8},{21,9... | collective-permute-start | bytes 393224 | tf_op jit(solution)/shard_map/ppermute | solution.py:323
  20.0 5.1 %collective-permute-start.2 = (bf16[2,128,256]{2,1,0:T(8,128)(2,1)S(1)}, bf16[2,128,256]{2,1,0:T(8,128)(2,1)S(1)}, u32[]{:S(2)}, u32[]{:S(2)}) collective-permute-start(bf16[2,128,256]{2,1,0:T(8,128)(2,1)S(1)} %collective-permute-done.1.refs_1_), channel_id=1, source_target_pairs={{0,192},{1,193},{2,194},{3,195},{4,196},{5,197},{6,198},{7,199},{8... | collective-permute-start | bytes 393224 | tf_op jit(solution)/shard_map/ppermute | solution.py:323
  20.5 5.0 %collective-permute-start.9 = (bf16[2,128,256]{2,1,0:T(8,128)(2,1)S(1)}, bf16[2,128,256]{2,1,0:T(8,128)(2,1)S(1)}, u32[]{:S(2)}, u32[]{:S(2)}) collective-permute-start(bf16[2,128,256]{2,1,0:T(8,128)(2,1)S(1)} %collective-permute-done.1.refs_1_), channel_id=1, source_target_pairs={{0,64},{1,65},{2,66},{3,67},{4,68},{5,69},{6,70},{7,71},{8,72},{9,... | collective-permute-start | bytes 393224 | tf_op jit(solution)/shard_map/ppermute | solution.py:323
  22.6 5.8 %collective-permute-start.6 = (bf16[2,128,256]{2,1,0:T(8,128)(2,1)S(1)}, bf16[2,128,256]{2,1,0:T(8,128)(2,1)S(1)}, u32[]{:S(2)}, u32[]{:S(2)}) collective-permute-start(bf16[2,128,256]{2,1,0:T(8,128)(2,1)S(1)} %collective-permute-done.3.refs_0_), channel_id=1, source_target_pairs={{0,192},{1,193},{2,194},{3,195},{4,196},{5,197},{6,198},{7,199},{8... | collective-permute-start | bytes 393224 | tf_op jit(solution)/shard_map/ppermute | solution.py:323
  23.2 5.6 %collective-permute-start.7 = (bf16[2,128,256]{2,1,0:T(8,128)(2,1)S(1)}, bf16[2,128,256]{2,1,0:T(8,128)(2,1)S(1)}, u32[]{:S(2)}, u32[]{:S(2)}) collective-permute-start(bf16[2,128,256]{2,1,0:T(8,128)(2,1)S(1)} %collective-permute-done.3.refs_0_), channel_id=1, source_target_pairs={{0,64},{1,65},{2,66},{3,67},{4,68},{5,69},{6,70},{7,71},{8,72},{9,... | collective-permute-start | bytes 393224 | tf_op jit(solution)/shard_map/ppermute | solution.py:323
  25.5 4.0 %collective-permute-start.10 = (bf16[2,2,128,256]{3,2,1,0:T(8,128)(2,1)S(1)}, bf16[2,2,128,256]{3,2,1,0:T(8,128)(2,1)S(1)}, u32[]{:S(2)}, u32[]{:S(2)}) collective-permute-start(bf16[2,2,128,256]{3,2,1,0:T(8,128)(2,1)S(1)} %pad_maximum_fusion.1), channel_id=1, source_target_pairs={{0,8},{1,9},{2,10},{3,11},{4,12},{5,13},{6,14},{7,15},{8,0},{9,1},... | collective-permute-start | bytes 786440 | tf_op jit(solution)/shard_map/ppermute | solution.py:323
  28.8 1.6 %collective-permute-start.8 = (bf16[2,2,128,256]{3,2,1,0:T(8,128)(2,1)S(1)}, bf16[2,2,128,256]{3,2,1,0:T(8,128)(2,1)S(1)}, u32[]{:S(2)}, u32[]{:S(2)}) collective-permute-start(bf16[2,2,128,256]{3,2,1,0:T(8,128)(2,1)S(1)} %pad_maximum_fusion), channel_id=1, source_target_pairs={{0,8},{1,9},{2,10},{3,11},{4,12},{5,13},{6,14},{7,15},{8,0},{9,1},... | collective-permute-start | bytes 786440 | tf_op jit(solution)/shard_map/ppermute | solution.py:323
  28.9 3.8 %collective-permute-start.4 = (bf16[2,128,256]{2,1,0:T(8,128)(2,1)S(1)}, bf16[2,128,256]{2,1,0:T(8,128)(2,1)S(1)}, u32[]{:S(2)}, u32[]{:S(2)}) collective-permute-start(bf16[2,128,256]{2,1,0:T(8,128)(2,1)S(1)} %collective-permute-done.3.refs_0_), channel_id=1, source_target_pairs={{0,8},{1,9},{2,10},{3,11},{4,12},{5,13},{6,14},{7,15},{8,0},{9,1},... | collective-permute-start | bytes 393224 | tf_op jit(solution)/shard_map/ppermute | solution.py:323
  29.4 3.4 %collective-permute-start.5 = (bf16[2,128,256]{2,1,0:T(8,128)(2,1)S(1)}, bf16[2,128,256]{2,1,0:T(8,128)(2,1)S(1)}, u32[]{:S(2)}, u32[]{:S(2)}) collective-permute-start(bf16[2,128,256]{2,1,0:T(8,128)(2,1)S(1)} %collective-permute-done.1.refs_1_), channel_id=1, source_target_pairs={{0,8},{1,9},{2,10},{3,11},{4,12},{5,13},{6,14},{7,15},{8,0},{9,1},... | collective-permute-start | bytes 393224 | tf_op jit(solution)/shard_map/ppermute | solution.py:323
  30.6 15.8 %collective-permute-start.11 = (bf16[4,2,128,256]{3,2,1,0:T(8,128)(2,1)S(1)}, bf16[4,2,128,256]{3,2,1,0:T(8,128)(2,1)S(1)}, u32[]{:S(2)}, u32[]{:S(2)}) collective-permute-start(bf16[4,2,128,256]{3,2,1,0:T(8,128)(2,1)S(1)} %maximum_select_fusion), channel_id=1, source_target_pairs={{0,192},{1,193},{2,194},{3,195},{4,196},{5,197},{6,198},{7,199},{8... | collective-permute-start | bytes 1572872 | tf_op jit(solution)/shard_map/ppermute | solution.py:323
  69.9 1.2 %collective-permute-start.12 = (f32[4,128]{1,0:T(4,128)S(1)}, f32[4,128]{1,0:T(4,128)S(1)}, u32[]{:S(2)}, u32[]{:S(2)}) collective-permute-start(f32[4,128]{1,0:T(4,128)S(1)} %slice.42), channel_id=1, source_target_pairs={{0,8},{1,9},{2,10},{3,11},{4,12},{5,13},{6,14},{7,15},{8,0},{9,1},... | collective-permute-start | bytes 6152 | tf_op jit(solution)/shard_map/ppermute | solution.py:323
  71.1 13.2 %collective-permute-start.13 = (f32[4,128]{1,0:T(4,128)S(1)}, f32[4,128]{1,0:T(4,128)S(1)}, u32[]{:S(2)}, u32[]{:S(2)}) collective-permute-start(f32[4,128]{1,0:T(4,128)S(1)} %slice_add_fusion), channel_id=1, source_target_pairs={{0,0},{1,1},{2,2},{3,3},{4,4},{5,5},{6,6},{7,7},{8,8},{9,9},{10,10... | collective-permute-start | bytes 6152 | tf_op jit(solution)/shard_map/ppermute | solution.py:323
